TPU v7x, 512 devices: a whole 4x4x16 slice. The times are simulated.
512 devices in a mesh: dp: 2 (over core), tensor: 16 (over z), expert: 16 (over y, x).
Axes of the slice: x: 4, y: 4, z: 16, core: 2. Of those that a mesh axis runs over, the one named last changes fastest.
Arguments:
- queries: bfloat16 [4096, 8192], P(('dp', 'expert'), 'tensor'), parts along dimension 0, may hold values from -120 to 120
- all_key_rows: bfloat16 [4096, 512], P(('dp', 'expert')), parts along dimension 0, may hold values from -6 to 6
- all_value_rows: bfloat16 [4096, 512], P(('dp', 'expert')), parts along dimension 0, may hold values from -6 to 6
- out_weight: bfloat16 [8192, 4096], P('tensor', 'expert'), may hold values from -0.5 to 0.5
- residual: bfloat16 [4096, 4096], P(('dp', 'expert')), parts along dimension 0, may hold values from -6 to 6
- post_gain: float32 [4096], replicated, may hold values from 0.4 to 2.5
- routes: int32 [4096, 2], P(('dp', 'expert')), parts along dimension 0, may hold values from 0 to 15, all different within a row; in each aligned block of 128 rows (0 to 127, 128 to 255, ...) at most 32 rows name the same one
- route_weight: float32 [4096, 2], P(('dp', 'expert')), parts along dimension 0, may hold values from 0.1 to 1
- gate_weight: bfloat16 [16, 4096, 1536], P('expert', None, 'tensor'), may hold values from -0.09375 to 0.09375
- up_weight: bfloat16 [16, 4096, 1536], P('expert', None, 'tensor'), may hold values from -0.09375 to 0.09375
- down_weight: bfloat16 [16, 1536, 4096], P('expert', None, 'tensor'), may hold values from -0.15625 to 0.15625
Outputs:
- layer_out: bfloat16 [4096, 4096], P(('dp', 'expert'), 'tensor'), parts along dimension 0
There are 2 independent parts, one for each index of `dp`. A program takes and returns all parts, laid end to end along the dimension named above; an argument that names none is the same for every part. Nothing has to cross between parts.
Inputs may be any that keep to these rules, and one draw needn't show every extreme that they name: `routes`: each row names 2 different experts. The rows of one device name any expert at most 32 times, and in every draw some expert is named exactly 32 times by the rows of some device.
All inputs are finite; a program needn't handle non-finite values.
Results may differ from a plain program's by a relative error of at most 0.023.
Values may be sent and summed in bfloat16 or wider, within the bound.
No kernel may reach another device: no remote copies, remote signals or barrier semaphores. Data moves between devices by JAX's collectives and lax.ppermute only.
A program may use at most 64 MiB of HBM per device.

v0:
```python
import jax
import jax.numpy as jnp
from jax import lax
from jax.sharding import PartitionSpec as P

D = 4096
QUERY_HEADS = 64
KEY_VALUE_HEADS = 4
HEAD_WIDTH = 128
TOP = 2


def route_slots(routes, experts_count, capacity):
    flat_routes = routes.reshape(-1)
    onehot = (flat_routes[:, None] == jnp.arange(experts_count, dtype=jnp.int32)[None, :]).astype(
        jnp.int32
    )
    ranking = jnp.cumsum(onehot, axis=0) - 1
    slot_index = jnp.sum(ranking * onehot, axis=1)
    return flat_routes * capacity + slot_index


def pack_rows(rows, target, experts_count, capacity):
    source_row = jnp.arange(target.shape[0], dtype=jnp.int32) // TOP
    packed = (
        jnp.zeros((experts_count * capacity, rows.shape[1]), rows.dtype)
        .at[target]
        .set(rows[source_row])
    )
    return packed.reshape(experts_count, capacity, rows.shape[1])


def local(
    queries,
    all_key_rows,
    all_value_rows,
    out_weight,
    residual,
    post_gain,
    routes,
    route_weight,
    gate_weight,
    up_weight,
    down_weight,
):
    tokens = queries.shape[0]
    local_heads = queries.shape[1] // HEAD_WIDTH
    group_width = QUERY_HEADS // KEY_VALUE_HEADS
    tensor_count = lax.axis_size("tensor")
    expert_count = lax.axis_size("expert")
    tensor_index = lax.axis_index("tensor")
    expert_index = lax.axis_index("expert")
    shared = tensor_index * local_heads // group_width
    key_head = lax.dynamic_slice_in_dim(all_key_rows, shared * HEAD_WIDTH, HEAD_WIDTH, 1)
    value_head = lax.dynamic_slice_in_dim(all_value_rows, shared * HEAD_WIDTH, HEAD_WIDTH, 1)
    query_heads = queries.reshape(tokens, local_heads, HEAD_WIDTH)
    query_place = expert_index * tokens + jnp.arange(tokens, dtype=jnp.int32)
    row_max = jnp.full((local_heads, tokens), -1e30, jnp.float32)
    key_piece = lax.all_gather(key_head, "expert", axis=0, tiled=True)
    value_piece = lax.all_gather(value_head, "expert", axis=0, tiled=True)
    scores = jnp.einsum(
        "thd,sd->hts", query_heads, key_piece, preferred_element_type=jnp.float32
    ) * HEAD_WIDTH ** (-0.5)
    key_place = jnp.arange(key_piece.shape[0], dtype=jnp.int32)
    visible = (query_place[:, None] >= key_place[None, :])[None, :, :]
    masked = jnp.where(visible, scores, -1e30)
    new_max = jnp.maximum(row_max, jnp.max(masked, axis=2))
    exponent = jnp.where(visible, jnp.exp(masked - new_max[:, :, None]), 0.0)
    row_total = jnp.sum(exponent, axis=2)
    update = jnp.einsum(
        "hts,sd->htd",
        exponent.astype(jnp.bfloat16),
        value_piece,
        preferred_element_type=jnp.float32,
    )
    row_max, row_total, accumulated = (new_max, row_total, update)
    attended = (accumulated / row_total[:, :, None]).astype(jnp.bfloat16)
    attended = jnp.transpose(attended, (1, 0, 2)).reshape(tokens, local_heads * HEAD_WIDTH)
    partial_value = jnp.dot(
        attended,
        lax.all_gather(out_weight, "expert", axis=1, tiled=True),
        preferred_element_type=jnp.float32,
    )
    columns = D // tensor_count
    column_start = tensor_index * columns
    capacity = 2 * tokens * TOP // expert_count
    slot_count = expert_count * capacity
    target = route_slots(routes, expert_count, capacity)
    gate_local = gate_weight[0]
    up_local = up_weight[0]
    down_local = down_weight[0]
    head_total = lax.psum(partial_value.astype(jnp.bfloat16), "tensor").astype(jnp.float32)
    hidden = residual.astype(jnp.float32) + head_total
    mean_square = jnp.mean(hidden * hidden, axis=1, keepdims=True)
    normed = (hidden * lax.rsqrt(mean_square + 1e-06) * post_gain).astype(jnp.bfloat16)
    hidden_share = lax.dynamic_slice_in_dim(hidden, column_start, columns, 1)
    arrived = lax.all_to_all(
        pack_rows(normed, target, expert_count, capacity),
        "expert",
        split_axis=0,
        concat_axis=0,
        tiled=True,
    ).reshape(slot_count, D)
    gate_values = jnp.dot(arrived, gate_local, preferred_element_type=jnp.float32)
    up_values = jnp.dot(arrived, up_local, preferred_element_type=jnp.float32)
    activation = (jax.nn.silu(gate_values) * up_values).astype(jnp.bfloat16)
    expert_out = jnp.dot(
        lax.all_gather(activation, "tensor", axis=1, tiled=True),
        down_local,
        preferred_element_type=jnp.float32,
    ).astype(jnp.bfloat16)
    returned = lax.all_to_all(
        expert_out.reshape(expert_count, capacity, columns),
        "expert",
        split_axis=0,
        concat_axis=0,
        tiled=True,
    ).reshape(slot_count, columns)
    picked = returned[target].astype(jnp.float32).reshape(tokens, TOP, columns)
    mixed = jnp.sum(picked * route_weight[:, :, None], axis=1)
    return (hidden_share + mixed).astype(jnp.bfloat16)


def solution(mesh):
    return jax.shard_map(
        local,
        mesh=mesh,
        in_specs=(
            P(("dp", "expert"), "tensor"),
            P(("dp", "expert"), None),
            P(("dp", "expert"), None),
            P("tensor", "expert"),
            P(("dp", "expert"), None),
            P(),
            P(("dp", "expert"), None),
            P(("dp", "expert"), None),
            P("expert", None, "tensor"),
            P("expert", None, "tensor"),
            P("expert", None, "tensor"),
        ),
        out_specs=P(("dp", "expert"), "tensor"),
        check_vma=False,
    )
```

profile of v0, /device:TPU:2, one launch (start us, length us, event | category | flops | bytes accessed | tf_op | source)
XLA Modules:
  0.0 390.6 jit_solution(862753136660117940)
XLA Ops:
  6.5 0.0 copy-start
  6.5 0.0 all-gather.3.cloned.1.call-start
  6.5 0.7 all-gather.3.cloned.1.call-update
  7.3 0.0 all-reduce.2.cloned.1.call-start
  7.3 0.8 copy.20
  8.1 0.1 eq.29
  8.2 0.1 eq.25
  8.4 0.8 constant_dynamic-slice_fusion
  9.2 0.1 copy.25
  9.3 0.8 constant_dynamic-slice_fusion.1
  10.1 27.5 %all_gather.12 = bf16[2048,128]{1,0:T(8,128)(2,1)S(1)} all-gather(bf16[128,128]{1,0:T(8,128)(2,1)S(1)} %constant_dynamic-slice_fusion.1), channel_id=1, replica_groups=mesh['dp'=2,'tensor'=16,'expert'=16] {'expert'}, dimensions={0}, use_global_device_ids=true | all-gather | bytes 557056 | tf_op jit(solution)/shard_map/all_gather | solution.py:59
  37.6 21.7 %all_gather.13 = bf16[2048,128]{0,1:T(8,128)(2,1)S(1)} all-gather(bf16[128,128]{0,1:T(8,128)(2,1)S(1)} %copy.25), channel_id=1, replica_groups=mesh['dp'=2,'tensor'=16,'expert'=16] {'expert'}, dimensions={0}, use_global_device_ids=true | all-gather | bytes 557056 | tf_op jit(solution)/shard_map/all_gather | solution.py:60
  59.3 0.2 iota_compare_fusion
  59.5 1.6 fusion
  61.1 1.0 fusion.1
  62.2 1.0 fusion.16
  63.2 0.0 copy-start.5
  63.2 0.0 copy-start.1
  63.2 25.1 %all-gather.3.cloned.1.call-done = bf16[512,4096]{1,0:T(8,128)(2,1)} async-done(((bf16[512,256]{1,0:T(8,128)(2,1)}), bf16[512,4096]{1,0:T(8,128)(2,1)}) %all-gather.3.cloned.1.call-update) | async-done | bytes 4194320 | tf_op jit(solution)/shard_map/all_gather | solution.py:81
  88.4 0.0 copy-start.4
  88.4 3.9 %convolution_convert_fusion = bf16[128,4096]{1,0:T(8,128)(2,1)} fusion(bf16[128,512]{0,1:T(8,128)(2,1)S(1)} %bitcast.82, bf16[512,4096]{1,0:T(8,128)(2,1)} %all-gather.3.cloned.1.call-done), kind=kOutput, calls=%fused_computation.3 | convolution fusion | flops 537395200 | bytes 5373952 | tf_op jit(solution)/shard_map/dot_general | solution.py:79
  92.3 0.0 all-reduce.2.cloned.1.call-update
  92.3 0.2 all-gather.5.cloned.1.call-start
  92.6 0.6 reduce-window.6
  93.1 0.2 slice_reduce_fusion
  93.4 0.0 copy-done.5
  93.4 0.1 copy.19
  93.5 0.1 mul.84
  93.7 0.1 fusion.29
  93.8 137.3 %all-reduce.2.cloned.1.call-done = bf16[128,4096]{1,0:T(8,128)(2,1)} async-done(((bf16[128,4096]{1,0:T(8,128)(2,1)}), bf16[128,4096]{1,0:T(8,128)(2,1)}) %all-reduce.2.cloned.1.call-update) | async-done | bytes 1048592 | tf_op jit(solution)/shard_map/psum | solution.py:92
  231.1 0.0 copy-done.1
  231.1 0.0 copy-start.2
  231.1 3.0 convert_add_fusion
  234.0 0.0 copy-done.4
  234.0 0.0 copy-done.2
  234.1 0.4 multiply_convert_fusion
  234.5 12.1 %scatter_custom_fusion = bf16[512,4096]{1,0:T(8,128)(2,1)} fusion(s32[256]{0:T(256)S(1)} %bitcast.83, bf16[128,4096]{1,0:T(8,128)(2,1)S(1)} %multiply_convert_fusion, s32[1024]{0:T(1024)S(1)} %pad_clamp_fusion.1, bf16[]{:T(256)} %constant.71.clone.1), kind=kCustom, calls=%fused_computation.9 | custom fusion | bytes 4194306 | tf_op jit(solution)/shard_map/scatter | solution.py:28
  246.6 0.0 copy-start.3
  246.6 47.8 %all_to_all.10 = bf16[16,32,4096]{2,1,0:T(8,128)(2,1)S(1)} all-to-all(bf16[16,32,4096]{2,1,0:T(8,128)(2,1)} %bitcast.80), channel_id=1, replica_groups=mesh['dp'=2,'tensor'=16,'expert'=16] {'expert'}, dimensions={0} | all-to-all | bytes 8388608 | tf_op jit(solution)/shard_map/all_to_all | solution.py:97
  294.3 0.0 copy-start.7
  294.3 0.0 copy-done.3
  294.3 1.4 fusion.21
  295.7 0.0 copy-done.7
  295.8 2.1 fusion.12
  297.8 0.0 copy-start.6
  297.8 0.0 all-gather.5.cloned.1.call-update
  297.8 65.7 %all-gather.5.cloned.1.call-done = bf16[512,1536]{0,1:T(8,128)(2,1)} async-done(((bf16[512,96]{0,1:T(8,128)(2,1)}), bf16[512,1536]{0,1:T(8,128)(2,1)}) %all-gather.5.cloned.1.call-update) | async-done | bytes 1572880 | tf_op jit(solution)/shard_map/all_gather | solution.py:108
  363.5 0.0 copy-done
  363.5 2.7 convolution_convert_fusion.1
  366.2 7.3 %all-to-all-start.1 = ((bf16[16,32,256]{2,1,0:T(8,128)(2,1)}), bf16[16,32,256]{2,1,0:T(8,128)(2,1)S(1)}, u32[]{:S(2)}, u32[]{:S(2)}) async-start(bf16[16,32,256]{2,1,0:T(8,128)(2,1)} %bitcast.15), calls=%async_computation.1 | async-start | bytes 524288 | tf_op jit(solution)/shard_map/all_to_all | solution.py:112
  373.5 0.0 copy-done.6
  373.5 0.1 copy.23
  373.6 7.2 %all-to-all-done.1 = bf16[16,32,256]{2,1,0:T(8,128)(2,1)S(1)} async-done(((bf16[16,32,256]{2,1,0:T(8,128)(2,1)}), bf16[16,32,256]{2,1,0:T(8,128)(2,1)S(1)}, u32[]{:S(2)}, u32[]{:S(2)}) %all-to-all-start.1) | async-done | bytes 262176 | tf_op jit(solution)/shard_map/all_to_all | solution.py:112
  380.8 1.2 gather_fusion
  382.0 0.1 reshape.157
  382.1 0.4 multiply_reduce_fusion.1
  382.5 1.6 add_convert_fusion
  (11 shorter events, 0.1 us)
Async XLA Ops:
  6.5 357.0 %copy-start = (bf16[1,1536,256]{2,1,0:T(8,128)(2,1)S(1)}, bf16[1,1536,256]{2,1,0:T(8,128)(2,1)}, u32[]{:S(2)}) copy-start(bf16[1,1536,256]{2,1,0:T(8,128)(2,1)} %param.21) | copy-start | bytes 2359300
  6.5 81.8 %all-gather.3.cloned.1.call-start = ((), (), s32[]{:S(2)}) async-start(), calls=%async_computation.2 | async-start | bytes 4456448 | tf_op jit(solution)/shard_map/all_gather | solution.py:81
  7.3 223.8 %all-reduce.2.cloned.1.call-start = ((), (), s32[]{:S(2)}) async-start(), calls=%async_computation.3 | async-start | bytes 2097152 | tf_op jit(solution)/shard_map/psum | solution.py:92
  63.2 30.2 %copy-start.5 = (s32[128,2]{0,1:T(2,128)S(1)}, s32[128,2]{0,1:T(2,128)}, u32[]{:S(2)}) copy-start(s32[128,2]{0,1:T(2,128)} %param.17) | copy-start | bytes 3076
  63.2 167.9 %copy-start.1 = (bf16[128,4096]{1,0:T(8,128)(2,1)S(1)}, bf16[128,4096]{1,0:T(8,128)(2,1)}, u32[]{:S(2)}) copy-start(bf16[128,4096]{1,0:T(8,128)(2,1)} %param.15) | copy-start | bytes 3145732
  88.4 145.7 %copy-start.4 = (f32[4096]{0:T(1024)S(1)}, f32[4096]{0:T(1024)}, u32[]{:S(2)}) copy-start(f32[4096]{0:T(1024)} %param.16) | copy-start | bytes 49156
  92.3 271.2 %all-gather.5.cloned.1.call-start = ((), (), s32[]{:S(2)}) async-start(), calls=%async_computation.4 | async-start | bytes 1671168 | tf_op jit(solution)/shard_map/all_gather | solution.py:108
  231.1 3.0 copy-start.2
  246.6 47.8 %copy-start.3 = (bf16[1,4096,96]{1,2,0:T(8,128)(2,1)S(1)}, bf16[1,4096,96]{1,2,0:T(8,128)(2,1)}, u32[]{:S(2)}) copy-start(bf16[1,4096,96]{1,2,0:T(8,128)(2,1)} %param.19) | copy-start | bytes 2359300
  294.3 1.4 copy-start.7
  297.8 75.7 %copy-start.6 = (f32[128,2]{0,1:T(2,128)S(1)}, f32[128,2]{0,1:T(2,128)}, u32[]{:S(2)}) copy-start(f32[128,2]{0,1:T(2,128)} %param.18) | copy-start | bytes 3076
  366.2 14.6 %all-to-all-start.1 = ((bf16[16,32,256]{2,1,0:T(8,128)(2,1)}), bf16[16,32,256]{2,1,0:T(8,128)(2,1)S(1)}, u32[]{:S(2)}, u32[]{:S(2)}) async-start(bf16[16,32,256]{2,1,0:T(8,128)(2,1)} %bitcast.15), calls=%async_computation.1 | async-start | bytes 524288 | tf_op jit(solution)/shard_map/all_to_all | solution.py:112
Sparse Core Ops, SparseCore 0:
  10.3 77.9 all-gather.2
  92.4 138.5 all-reduce.1
  298.0 65.4 all-gather.4
where the time goes:
time: 392 us; the launch traced here: 391 us
  waiting for transfers between devices  236 us (60%)
  blocking collectives  97 us (25%)
  local copies, waits for them, and re-layouts  16.7 us (4%)
  between operations  13.3 us (3%)
  matrix products  12.8 us (3%)
  starting transfers between devices  7.54 us (2%)
  other arithmetic  7.31 us (2%)
    psum x1, waiting for transfers between devices, local(): lax.psum(partial_value.astype(jnp.bfloat16), 'tensor').astype(jnp.float32)  137 us
    all_gather x1, waiting for transfers between devices, local(): lax.all_gather(activation, 'tensor', axis=1, tiled=True)  65.7 us
    all_to_all x1, blocking collectives, local(): lax.all_to_all(pack_rows(normed, target, expert_count, capacity), 'expert...  47.8 us
    all_gather x1, blocking collectives, local(): key_piece = lax.all_gather(key_head, 'expert', axis=0, tiled=True)  27.5 us
    all_gather x1, waiting for transfers between devices, local(): lax.all_gather(out_weight, 'expert', axis=1, tiled=True)  25.1 us
    all_gather x1, blocking collectives, local(): value_piece = lax.all_gather(value_head, 'expert', axis=0, tiled=True)  21.7 us
    scatter x1, local copies, waits for them, and re-layouts, pack_rows(): packed = jnp.zeros((experts_count * capacity, rows.shape[1]), rows.dtype)...  12.1 us
  transfers between devices with their start and end apart: 4, of which 4 were waited for; matrix products, arithmetic and copies ran while one was open for 2% of the time, Pallas kernels for 0%

commit v1 on v0

v1 whole, which is shorter than its diff:
```python
import jax
import jax.numpy as jnp
from jax import lax
from jax.sharding import PartitionSpec as P

D = 4096
QUERY_HEADS = 64
KEY_VALUE_HEADS = 4
HEAD_WIDTH = 128
TOP = 2
QUARTER = 4
CLOSE = [[QUARTER * i + j for j in range(QUARTER)] for i in range(QUARTER)]
SPREAD = [[QUARTER * j + i for j in range(QUARTER)] for i in range(QUARTER)]
SWAP = [(0, 1), (1, 0)]


def route_slots(routes, experts_count, capacity):
    flat_routes = routes.reshape(-1)
    onehot = (
        flat_routes[:, None] == jnp.arange(experts_count, dtype=jnp.int32)[None, :]
    ).astype(jnp.bfloat16)
    order = jnp.arange(flat_routes.shape[0], dtype=jnp.int32)
    before = (order[:, None] > order[None, :]).astype(jnp.bfloat16)
    ranking = jnp.dot(before, onehot, preferred_element_type=jnp.float32)
    slot_index = jnp.sum(ranking * onehot.astype(jnp.float32), axis=1).astype(jnp.int32)
    return flat_routes, slot_index


def local(
    queries,
    all_key_rows,
    all_value_rows,
    out_weight,
    residual,
    post_gain,
    routes,
    route_weight,
    gate_weight,
    up_weight,
    down_weight,
):
    tokens = queries.shape[0]
    local_heads = queries.shape[1] // HEAD_WIDTH
    group_width = QUERY_HEADS // KEY_VALUE_HEADS
    tensor_count = lax.axis_size("tensor")
    expert_count = lax.axis_size("expert")
    tensor_index = lax.axis_index("tensor")
    expert_index = lax.axis_index("expert")
    core = lax.axis_index("dp")
    columns = D // tensor_count
    capacity = 2 * tokens * TOP // expert_count
    slot_count = expert_count * capacity
    part = capacity // QUARTER
    rows = expert_count * part

    gate_or_up = jnp.where(core == 0, gate_weight[0], up_weight[0]).T
    first_own = lax.all_gather(gate_or_up, "tensor", axis=0, tiled=True, axis_index_groups=CLOSE)
    first_other = lax.ppermute(first_own, "dp", SWAP)
    hidden_units = down_weight.shape[1]
    half_units = hidden_units // 2
    down_half = lax.dynamic_slice_in_dim(down_weight[0], core * half_units, half_units, 0)
    down_own = lax.all_gather(down_half, "tensor", axis=0, axis_index_groups=CLOSE)
    down_other = lax.ppermute(down_own, "dp", SWAP)

    shared = tensor_index * local_heads // group_width
    key_head = lax.dynamic_slice_in_dim(all_key_rows, shared * HEAD_WIDTH, HEAD_WIDTH, 1)
    value_head = lax.dynamic_slice_in_dim(all_value_rows, shared * HEAD_WIDTH, HEAD_WIDTH, 1)
    half_rows = out_weight.shape[0] // 2
    weight_half = lax.dynamic_slice_in_dim(out_weight, core * half_rows, half_rows, 0)
    message = jnp.concatenate([jnp.concatenate([key_head, value_head], axis=1), weight_half], axis=0)
    gathered = lax.all_to_all(
        jnp.broadcast_to(message[None], (expert_count,) + message.shape),
        "expert",
        split_axis=0,
        concat_axis=0,
        tiled=True,
    )
    weight_own = gathered[:, tokens:, :]
    weight_other = lax.ppermute(weight_own, "dp", SWAP)
    key_piece = gathered[:, :tokens, :HEAD_WIDTH].reshape(expert_count * tokens, HEAD_WIDTH)
    value_piece = gathered[:, :tokens, HEAD_WIDTH:].reshape(expert_count * tokens, HEAD_WIDTH)

    query_heads = queries.reshape(tokens, local_heads, HEAD_WIDTH)
    query_place = expert_index * tokens + jnp.arange(tokens, dtype=jnp.int32)
    scores = jnp.einsum(
        "thd,sd->hts", query_heads, key_piece, preferred_element_type=jnp.float32
    ) * HEAD_WIDTH ** (-0.5)
    key_place = jnp.arange(key_piece.shape[0], dtype=jnp.int32)
    visible = (query_place[:, None] >= key_place[None, :])[None, :, :]
    masked = jnp.where(visible, scores, -1e30)
    row_max = jnp.max(masked, axis=2)
    exponent = jnp.where(visible, jnp.exp(masked - row_max[:, :, None]), 0.0)
    row_total = jnp.sum(exponent, axis=2)
    accumulated = jnp.einsum(
        "hts,sd->htd",
        exponent.astype(jnp.bfloat16),
        value_piece,
        preferred_element_type=jnp.float32,
    )
    attended = (accumulated / row_total[:, :, None]).astype(jnp.bfloat16)
    attended = jnp.transpose(attended, (1, 0, 2)).reshape(tokens, local_heads * HEAD_WIDTH)

    attended_own = lax.dynamic_slice_in_dim(attended, core * half_rows, half_rows, 1)
    attended_other = lax.dynamic_slice_in_dim(attended, (1 - core) * half_rows, half_rows, 1)
    partial_value = jnp.einsum(
        "tk,ekn->etn", attended_own, weight_own, preferred_element_type=jnp.float32
    ) + jnp.einsum(
        "tk,ekn->etn", attended_other, weight_other, preferred_element_type=jnp.float32
    )
    partial_sums = lax.all_to_all(
        partial_value.astype(jnp.bfloat16), "tensor", split_axis=0, concat_axis=0, tiled=True
    )
    head_total = jnp.sum(partial_sums.astype(jnp.float32), axis=0)
    residual_share = lax.dynamic_slice_in_dim(residual, tensor_index * columns, columns, 1)
    hidden_share = residual_share.astype(jnp.float32) + head_total

    flat_routes, slot_index = route_slots(routes, expert_count, capacity)
    target = flat_routes * capacity + slot_index
    slot_place = jnp.arange(slot_count, dtype=jnp.int32)
    packing = jnp.any(
        target.reshape(tokens, TOP)[None, :, :] == slot_place[:, None, None], axis=2
    ).astype(jnp.bfloat16)
    packed = jnp.dot(
        packing, hidden_share.astype(jnp.bfloat16), preferred_element_type=jnp.float32
    ).astype(jnp.bfloat16)
    arrived = lax.all_to_all(
        packed.reshape(expert_count, capacity, columns),
        "expert",
        split_axis=0,
        concat_axis=0,
        tiled=True,
    )
    quarters = jnp.transpose(
        arrived.reshape(expert_count, QUARTER, part, columns), (1, 0, 2, 3)
    ).reshape(1, QUARTER, rows, columns)
    quarters = jnp.broadcast_to(quarters, (tensor_count // QUARTER, QUARTER, rows, columns))
    full_rows = lax.all_to_all(
        quarters.reshape(tensor_count, rows, columns),
        "tensor",
        split_axis=0,
        concat_axis=0,
        tiled=True,
    )
    full_rows = jnp.transpose(full_rows, (1, 0, 2)).reshape(rows, D).astype(jnp.float32)
    mean_square = jnp.mean(full_rows * full_rows, axis=1, keepdims=True)
    normed = (full_rows * lax.rsqrt(mean_square + 1e-06) * post_gain).astype(jnp.bfloat16)

    contract_last = (((1,), (1,)), ((), ()))
    product_own = lax.dot_general(
        normed, first_own, contract_last, preferred_element_type=jnp.float32
    )
    product_other = lax.dot_general(
        normed, first_other, contract_last, preferred_element_type=jnp.float32
    )
    gate_values = jnp.where(core == 0, product_own, product_other)
    up_values = jnp.where(core == 0, product_other, product_own)
    activation = (jax.nn.silu(gate_values) * up_values).astype(jnp.bfloat16)
    activation = lax.all_to_all(
        jnp.broadcast_to(activation[None], (QUARTER,) + activation.shape),
        "tensor",
        split_axis=0,
        concat_axis=0,
        tiled=True,
        axis_index_groups=SPREAD,
    )
    activation = jnp.transpose(activation, (1, 0, 2)).reshape(rows, hidden_units)
    activation_own = lax.dynamic_slice_in_dim(activation, core * half_units, half_units, 1)
    activation_other = lax.dynamic_slice_in_dim(activation, (1 - core) * half_units, half_units, 1)
    expert_out = jnp.einsum(
        "rk,ckn->crn", activation_own, down_own, preferred_element_type=jnp.float32
    ) + jnp.einsum(
        "rk,ckn->crn", activation_other, down_other, preferred_element_type=jnp.float32
    )
    together = [
        [
            (QUARTER * far + near) * expert_count + place
            for near in range(QUARTER)
            for place in range(expert_count)
        ]
        for far in range(tensor_count // QUARTER)
    ]
    returned = lax.all_to_all(
        expert_out.astype(jnp.bfloat16).reshape(QUARTER * expert_count, part, columns),
        ("tensor", "expert"),
        split_axis=0,
        concat_axis=0,
        tiled=True,
        axis_index_groups=together,
    ).reshape(slot_count, columns)
    place = (slot_index // part * expert_count + flat_routes) * part + slot_index % part
    picking = (place[:, None] == slot_place[None, :]).astype(jnp.bfloat16)
    picked = jnp.dot(picking, returned, preferred_element_type=jnp.float32)
    picked = picked.reshape(tokens, TOP, columns)
    mixed = jnp.sum(picked * route_weight[:, :, None], axis=1)
    return (hidden_share + mixed).astype(jnp.bfloat16)


def solution(mesh):
    return jax.shard_map(
        local,
        mesh=mesh,
        in_specs=(
            P(("dp", "expert"), "tensor"),
            P(("dp", "expert"), None),
            P(("dp", "expert"), None),
            P("tensor", "expert"),
            P(("dp", "expert"), None),
            P(),
            P(("dp", "expert"), None),
            P(("dp", "expert"), None),
            P("expert", None, "tensor"),
            P("expert", None, "tensor"),
            P("expert", None, "tensor"),
        ),
        out_specs=P(("dp", "expert"), "tensor"),
        check_vma=False,
    )
```

time: 392 us -> 355 us (0.906)
  the two profiles are of different devices: /device:TPU:2 before, /device:TPU:1 now
where the time goes in v1:
time: 355 us; the launch traced here: 352 us
  waiting for transfers between devices  176 us (50%)
  blocking collectives  74.7 us (21%)
  starting transfers between devices  49.1 us (14%)
  local copies, waits for them, and re-layouts  17.9 us (5%)
  matrix products  17.1 us (5%)
  between operations  13.8 us (4%)
  other arithmetic  3.92 us (1%)
    all_to_all x1, waiting for transfers between devices, local(): lax.all_to_all(partial_value.astype(jnp.bfloat16), 'tensor', split_axis=0...  56.7 us
    all_gather x1, waiting for transfers between devices, local(): lax.all_gather(gate_or_up, 'tensor', axis=0, tiled=True, axis_index_group...  48.8 us
    all_gather x1, waiting for transfers between devices, local(): lax.all_gather(down_half, 'tensor', axis=0, axis_index_groups=CLOSE)  46.6 us
    all_to_all x1, blocking collectives, local(): lax.all_to_all(jnp.broadcast_to(message[None], (expert_count,) + message....  46.5 us
    all_to_all x1, waiting for transfers between devices, local(): lax.all_to_all(jnp.broadcast_to(activation[None], (QUARTER,) + activation...  23.5 us
    all_to_all x1, blocking collectives, local(): lax.all_to_all(expert_out.astype(jnp.bfloat16).reshape(QUARTER * expert_c...  18 us
    all_to_all x1, starting transfers between devices, local(): lax.all_to_all(quarters.reshape(tensor_count, rows, columns), 'tensor', s...  14.5 us
    all_to_all x1, starting transfers between devices, local(): lax.all_to_all(partial_value.astype(jnp.bfloat16), 'tensor', split_axis=0...  14 us
  transfers between devices with their start and end apart: 8, of which 4 were waited for; matrix products, arithmetic and copies ran while one was open for 8% of the time, Pallas kernels for 0%

profile of v1, /device:TPU:1, one launch (start us, length us, event | category | flops | bytes accessed | tf_op | source)
XLA Modules:
  0.0 352.1 jit_solution(14177174952103597210)
XLA Ops:
  6.5 1.0 constant_dynamic-slice_fusion.1
  7.5 0.8 constant_dynamic-slice_fusion.2
  8.4 0.2 copy.112
  8.5 0.4 broadcast_in_dim.26
  8.9 46.5 %all_to_all.30 = bf16[16,384,256]{1,2,0:T(8,128)(2,1)S(1)} all-to-all(bf16[16,384,256]{1,2,0:T(8,128)(2,1)S(1)} %broadcast_in_dim.26), channel_id=1, replica_groups=mesh['dp'=2,'tensor'=16,'expert'=16] {'expert'}, dimensions={0} | all-to-all | bytes 6291456 | tf_op jit(solution)/shard_map/all_to_all | solution.py:71
  55.4 1.6 copy-done.1
  57.1 1.5 slice.12
  58.6 4.6 %collective-permute-start = (bf16[16,256,256]{1,2,0:T(8,128)(2,1)}, bf16[16,256,256]{1,2,0:T(8,128)(2,1)S(1)}, u32[]{:S(2)}, u32[]{:S(2)}) collective-permute-start(bf16[16,256,256]{1,2,0:T(8,128)(2,1)} %slice.12), channel_id=1, source_target_pairs={{0,256},{256,0},{1,257},{257,1},{2,258},{258,2},{3,259},{259,3},{4... | collective-permute-start | bytes 6291464 | tf_op jit(solution)/shard_map/ppermute | solution.py:79
  63.2 0.2 iota_compare_fusion
  63.4 2.1 fusion.72
  65.5 1.1 copy.115
  66.6 2.0 reshape.159
  68.7 2.0 copy.113
  70.7 2.9 fusion.73
  73.6 3.1 fusion.18
  76.7 2.3 fusion.52
  79.0 0.0 collective-permute-done
  79.0 1.8 fusion.9
  80.8 14.0 %all-to-all-start.1 = ((bf16[16,128,256]{1,2,0:T(8,128)(2,1)}), bf16[16,128,256]{1,2,0:T(8,128)(2,1)S(1)}, u32[]{:S(2)}, u32[]{:S(2)}) async-start(bf16[16,128,256]{1,2,0:T(8,128)(2,1)} %fusion.9), calls=%async_computation.1 | async-start | bytes 2097152 | tf_op jit(solution)/shard_map/all_to_all | solution.py:110
  94.8 0.0 all-gather.5.cloned.1.call-start
  94.8 2.2 select_bitcast_fusion
  97.0 0.0 all-gather.5.cloned.1.call-update
  97.1 0.1 copy.131
  97.2 0.1 copy.119
  97.3 0.1 eq.64
  97.5 0.2 fusion.21
  97.7 0.1 convert_element_type.83
  97.8 0.1 copy.120
  97.9 0.1 fusion.26
  98.0 0.0 copy-start.4
  98.0 56.7 %all-to-all-done.1 = bf16[16,128,256]{1,2,0:T(8,128)(2,1)S(1)} async-done(((bf16[16,128,256]{1,2,0:T(8,128)(2,1)}), bf16[16,128,256]{1,2,0:T(8,128)(2,1)S(1)}, u32[]{:S(2)}, u32[]{:S(2)}) %all-to-all-start.1) | async-done | bytes 1048608 | tf_op jit(solution)/shard_map/all_to_all | solution.py:110
  154.7 0.1 convert_reduce_fusion
  154.8 0.2 convolution_convert_fusion
  155.1 10.1 %all_to_all.31 = bf16[16,32,256]{2,1,0:T(8,128)(2,1)S(1)} all-to-all(bf16[16,32,256]{2,1,0:T(8,128)(2,1)S(1)} %bitcast.113), channel_id=1, replica_groups=mesh['dp'=2,'tensor'=16,'expert'=16] {'expert'}, dimensions={0} | all-to-all | bytes 524288 | tf_op jit(solution)/shard_map/all_to_all | solution.py:126
  165.2 0.0 copy-start.5
  165.2 0.2 copy.126
  165.4 1.2 broadcast_in_dim.31
  166.6 14.5 %all-to-all-start.3 = ((bf16[16,128,256]{1,2,0:T(8,128)(2,1)}), bf16[16,128,256]{1,2,0:T(8,128)(2,1)S(1)}, u32[]{:S(2)}, u32[]{:S(2)}) async-start(bf16[16,128,256]{1,2,0:T(8,128)(2,1)} %bitcast.14), calls=%async_computation.3 | async-start | bytes 2097152 | tf_op jit(solution)/shard_map/all_to_all | solution.py:137
  181.1 0.0 all-gather.3.cloned.1.call-start
  181.2 0.8 constant_dynamic-slice_fusion
  182.0 0.0 all-gather.3.cloned.1.call-update
  182.0 48.8 %all-gather.5.cloned.1.call-done = bf16[384,4096]{1,0:T(8,128)(2,1)} async-done(((bf16[96,4096]{1,0:T(8,128)(2,1)}), bf16[384,4096]{1,0:T(8,128)(2,1)}) %all-gather.5.cloned.1.call-update) | async-done | bytes 3145744 | tf_op jit(solution)/shard_map/all_gather | solution.py:57
  230.7 3.2 collective-permute-start.1
  234.0 46.6 %all-gather.3.cloned.1.call-done = bf16[4,768,256]{2,1,0:T(8,128)(2,1)} async-done(((bf16[1,768,256]{2,1,0:T(8,128)(2,1)}), bf16[4,768,256]{2,1,0:T(8,128)(2,1)}) %all-gather.3.cloned.1.call-update) | async-done | bytes 1572880 | tf_op jit(solution)/shard_map/all_gather | solution.py:62
  280.6 2.8 collective-permute-start.2
  283.4 0.0 all-to-all-done.3
  283.4 0.6 multiply_reduce_fusion
  284.0 0.0 copy-done.5
  284.0 0.7 fusion.3
  284.7 0.6 copy-done.2
  285.3 1.1 fusion.76
  286.3 0.0 copy-start.3
  286.3 0.0 collective-permute-done.1
  286.4 3.2 multiply_convert_fusion
  289.5 0.8 broadcast_in_dim.32
  290.3 10.0 %all-to-all-start.4 = ((bf16[4,128,384]{2,1,0:T(8,128)(2,1)}), bf16[4,128,384]{2,1,0:T(8,128)(2,1)S(1)}, u32[]{:S(2)}, u32[]{:S(2)}) async-start(bf16[4,128,384]{2,1,0:T(8,128)(2,1)} %broadcast_in_dim.32), calls=%async_computation.4 | async-start | bytes 786432 | tf_op jit(solution)/shard_map/all_to_all | solution.py:158
  300.3 23.5 %all-to-all-done.4 = bf16[4,128,384]{2,1,0:T(8,128)(2,1)S(1)} async-done(((bf16[4,128,384]{2,1,0:T(8,128)(2,1)}), bf16[4,128,384]{2,1,0:T(8,128)(2,1)S(1)}, u32[]{:S(2)}, u32[]{:S(2)}) %all-to-all-start.4) | async-done | bytes 393248 | tf_op jit(solution)/shard_map/all_to_all | solution.py:158
  323.8 0.4 fusion.30
  324.2 0.0 collective-permute-done.2
  324.2 1.8 fusion.10
  326.0 18.0 %all_to_all.32 = bf16[64,8,256]{2,1,0:T(8,128)(2,1)S(1)} all-to-all(bf16[64,8,256]{2,1,0:T(8,128)(2,1)S(1)} %bitcast.114), channel_id=1, replica_groups={{0,1,2,3,4,5,6,7,8,9,10,11,12,13,14,15,16,17,18,19,20,21,22,23,24,25,26..., dimensions={0} | all-to-all | bytes 524288 | tf_op jit(solution)/shard_map/all_to_all | solution.py:182
  344.1 0.3 fusion.17
  344.3 0.1 copy.128
  344.5 0.7 copy.129
  (21 shorter events, 0.2 us)
Async XLA Ops:
  6.5 90.5 %copy-start = (bf16[128,4096]{1,0:T(8,128)(2,1)S(1)}, bf16[128,4096]{1,0:T(8,128)(2,1)}, u32[]{:S(2)}) copy-start(bf16[128,4096]{1,0:T(8,128)(2,1)} %param.15) | copy-start | bytes 3145732
  55.4 1.6 copy-start.1
  58.6 12.1 %copy-start.7 = (bf16[128,512]{1,0:T(8,128)(2,1)S(1)}, bf16[128,512]{1,0:T(8,128)(2,1)}, u32[]{:S(2)}) copy-start(bf16[128,512]{1,0:T(8,128)(2,1)} %param.11) | copy-start | bytes 393220
  58.6 20.5 %collective-permute-start = (bf16[16,256,256]{1,2,0:T(8,128)(2,1)}, bf16[16,256,256]{1,2,0:T(8,128)(2,1)S(1)}, u32[]{:S(2)}, u32[]{:S(2)}) collective-permute-start(bf16[16,256,256]{1,2,0:T(8,128)(2,1)} %slice.12), channel_id=1, source_target_pairs={{0,256},{256,0},{1,257},{257,1},{2,258},{258,2},{3,259},{259,3},{4... | collective-permute-start | bytes 6291464 | tf_op jit(solution)/shard_map/ppermute | solution.py:79
  80.8 16.4 %copy-start.6 = (s32[128,2]{0,1:T(2,128)S(1)}, s32[128,2]{0,1:T(2,128)}, u32[]{:S(2)}) copy-start(s32[128,2]{0,1:T(2,128)} %param.17) | copy-start | bytes 3076
  80.8 73.9 %all-to-all-start.1 = ((bf16[16,128,256]{1,2,0:T(8,128)(2,1)}), bf16[16,128,256]{1,2,0:T(8,128)(2,1)S(1)}, u32[]{:S(2)}, u32[]{:S(2)}) async-start(bf16[16,128,256]{1,2,0:T(8,128)(2,1)} %fusion.9), calls=%async_computation.1 | async-start | bytes 2097152 | tf_op jit(solution)/shard_map/all_to_all | solution.py:110
  94.8 136.0 %all-gather.5.cloned.1.call-start = ((), (), s32[]{:S(2)}) async-start(), calls=%async_computation.7 | async-start | bytes 3932160 | tf_op jit(solution)/shard_map/all_gather | solution.py:57
  98.0 83.2 %copy-start.4 = (bf16[1,1536,256]{2,1,0:T(8,128)(2,1)S(1)}, bf16[1,1536,256]{2,1,0:T(8,128)(2,1)}, u32[]{:S(2)}) copy-start(bf16[1,1536,256]{2,1,0:T(8,128)(2,1)} %param.21) | copy-start | bytes 2359300
  165.2 118.7 %copy-start.5 = (f32[4096]{0:T(1024)S(1)}, f32[4096]{0:T(1024)}, u32[]{:S(2)}) copy-start(f32[4096]{0:T(1024)} %param.16) | copy-start | bytes 49156
  166.6 116.8 %all-to-all-start.3 = ((bf16[16,128,256]{1,2,0:T(8,128)(2,1)}), bf16[16,128,256]{1,2,0:T(8,128)(2,1)S(1)}, u32[]{:S(2)}, u32[]{:S(2)}) async-start(bf16[16,128,256]{1,2,0:T(8,128)(2,1)} %bitcast.14), calls=%async_computation.3 | async-start | bytes 2097152 | tf_op jit(solution)/shard_map/all_to_all | solution.py:137
  181.1 99.5 %all-gather.3.cloned.1.call-start = ((), (), s32[]{:S(2)}) async-start(), calls=%async_computation.6 | async-start | bytes 1966080 | tf_op jit(solution)/shard_map/all_gather | solution.py:62
  230.7 55.6 %collective-permute-start.1 = (bf16[384,4096]{1,0:T(8,128)(2,1)}, bf16[384,4096]{1,0:T(8,128)(2,1)}, u32[]{:S(2)}, u32[]{:S(2)}) collective-permute-start(bf16[384,4096]{1,0:T(8,128)(2,1)} %all-gather.5.cloned.1.call-done), channel_id=1, source_target_pairs={{0,256},{256,0},{1,257},{257,1},{2,258},{258,2},{3,259},{259,3},{4... | collective-permute-start | bytes 9437192 | tf_op jit(solution)/shard_map/ppermute | solution.py:58
  280.6 43.7 %collective-permute-start.2 = (bf16[4,768,256]{2,1,0:T(8,128)(2,1)}, bf16[4,768,256]{2,1,0:T(8,128)(2,1)}, u32[]{:S(2)}, u32[]{:S(2)}) collective-permute-start(bf16[4,768,256]{2,1,0:T(8,128)(2,1)} %all-gather.3.cloned.1.call-done), channel_id=1, source_target_pairs={{0,256},{256,0},{1,257},{257,1},{2,258},{258,2},{3,259},{259,3},{4... | collective-permute-start | bytes 4718600 | tf_op jit(solution)/shard_map/ppermute | solution.py:63
  283.4 1.9 copy-start.2
  286.3 37.5 %copy-start.3 = (bf16[4,768,256]{2,1,0:T(8,128)(2,1)S(1)}, bf16[4,768,256]{2,1,0:T(8,128)(2,1)}, u32[]{:S(2)}) copy-start(bf16[4,768,256]{2,1,0:T(8,128)(2,1)} %all-gather.3.cloned.1.call-done) | copy-start | bytes 4718596
  290.3 33.5 %all-to-all-start.4 = ((bf16[4,128,384]{2,1,0:T(8,128)(2,1)}), bf16[4,128,384]{2,1,0:T(8,128)(2,1)S(1)}, u32[]{:S(2)}, u32[]{:S(2)}) async-start(bf16[4,128,384]{2,1,0:T(8,128)(2,1)} %broadcast_in_dim.32), calls=%async_computation.4 | async-start | bytes 786432 | tf_op jit(solution)/shard_map/all_to_all | solution.py:158
  300.3 43.7 %copy-start.8 = (f32[128,2]{0,1:T(2,128)S(1)}, f32[128,2]{0,1:T(2,128)}, u32[]{:S(2)}) copy-start(f32[128,2]{0,1:T(2,128)} %param.18) | copy-start | bytes 3076
Sparse Core Ops, SparseCore 0:
  97.7 132.9 all-gather.4
  232.8 47.6 all-gather.2

commit v2 on v1

v2 whole, which is shorter than its diff:
```python
import jax
import jax.numpy as jnp
from jax import lax
from jax.experimental import pallas as pl
from jax.experimental.pallas import tpu as pltpu
from jax.sharding import PartitionSpec as P

D = 4096
QUERY_HEADS = 64
KEY_VALUE_HEADS = 4
HEAD_WIDTH = 128
TOP = 2
QUARTER = 4
CLOSE = [[QUARTER * i + j for j in range(QUARTER)] for i in range(QUARTER)]
SPREAD = [[QUARTER * j + i for j in range(QUARTER)] for i in range(QUARTER)]
SWAP = [(0, 1), (1, 0)]
CHUNK = 512
UNIT = 96


def route_slots(routes, experts_count, capacity):
    flat_routes = routes.reshape(-1)
    onehot = (
        flat_routes[:, None] == jnp.arange(experts_count, dtype=jnp.int32)[None, :]
    ).astype(jnp.bfloat16)
    order = jnp.arange(flat_routes.shape[0], dtype=jnp.int32)
    before = (order[:, None] > order[None, :]).astype(jnp.bfloat16)
    ranking = jnp.dot(before, onehot, preferred_element_type=jnp.float32)
    slot_index = jnp.sum(ranking * onehot.astype(jnp.float32), axis=1).astype(jnp.int32)
    return flat_routes, slot_index


CONTRACT_LAST = (((1,), (1,)), ((), ()))


def attend(place_ref, query_ref, piece_ref, out_ref, score_ref):
    tokens = query_ref.shape[0]
    heads = query_ref.shape[1] // HEAD_WIDTH
    rows = heads * tokens
    blocks = CHUNK // tokens
    place = place_ref[0]
    stacked = jnp.concatenate(
        [query_ref[:, HEAD_WIDTH * h : HEAD_WIDTH * (h + 1)] for h in range(heads)], axis=0
    )
    token = place * tokens + lax.broadcasted_iota(jnp.int32, (rows, CHUNK), 0) % tokens
    offset = token - lax.broadcasted_iota(jnp.int32, (rows, CHUNK), 1)

    def score(step, row_max):
        keys = piece_ref[pl.ds(step * blocks, blocks), :, :HEAD_WIDTH].reshape(CHUNK, HEAD_WIDTH)
        scores = lax.dot_general(
            stacked, keys, CONTRACT_LAST, preferred_element_type=jnp.float32
        ) * HEAD_WIDTH ** (-0.5)
        masked = jnp.where(offset >= step * CHUNK, scores, -1e30)
        score_ref[step] = masked
        return jnp.maximum(row_max, jnp.max(masked, axis=1, keepdims=True))

    def weigh(step, carry):
        total, summed = carry
        exponent = jnp.exp(score_ref[step] - row_max)
        values = piece_ref[pl.ds(step * blocks, blocks), :, HEAD_WIDTH:].reshape(CHUNK, HEAD_WIDTH)
        return (
            total + jnp.sum(exponent, axis=1, keepdims=True),
            summed
            + jnp.dot(exponent.astype(jnp.bfloat16), values, preferred_element_type=jnp.float32),
        )

    steps = place // blocks + 1
    row_max = lax.fori_loop(0, steps, score, jnp.full((rows, 1), -1e30, jnp.float32))
    total, summed = lax.fori_loop(
        0,
        steps,
        weigh,
        (jnp.zeros((rows, 1), jnp.float32), jnp.zeros((rows, HEAD_WIDTH), jnp.float32)),
    )
    attended = (summed / total).astype(out_ref.dtype)
    halves = heads // 2
    for h in range(heads):
        out_ref[h // halves, :, HEAD_WIDTH * (h % halves) : HEAD_WIDTH * (h % halves + 1)] = (
            attended[tokens * h : tokens * (h + 1)]
        )


def project(core_ref, attended_ref, own_ref, other_ref, out_ref):
    core = core_ref[0]
    for block in range(own_ref.shape[0]):
        out_ref[block] = (
            jnp.dot(attended_ref[core], own_ref[block], preferred_element_type=jnp.float32)
            + jnp.dot(attended_ref[1 - core], other_ref[block], preferred_element_type=jnp.float32)
        ).astype(out_ref.dtype)


def gate_up(core_ref, rows_ref, gain_ref, own_ref, other_ref, out_ref, square, first, second):
    step = pl.program_id(0)
    units = own_ref.shape[0] * own_ref.shape[2]
    width = own_ref.shape[3]

    @pl.when(step == 0)
    def _():
        square[...] = jnp.zeros_like(square)
        first[...] = jnp.zeros_like(first)
        second[...] = jnp.zeros_like(second)

    rows = rows_ref[0].astype(jnp.float32)
    square[...] += jnp.sum(rows * rows, axis=1, keepdims=True)
    scaled = (rows * gain_ref[0]).astype(jnp.bfloat16)
    first[...] += lax.dot_general(
        scaled,
        own_ref[...].reshape(units, width),
        CONTRACT_LAST,
        preferred_element_type=jnp.float32,
    )
    second[...] += lax.dot_general(
        scaled,
        other_ref[...].reshape(units, width),
        CONTRACT_LAST,
        preferred_element_type=jnp.float32,
    )

    @pl.when(step == pl.num_programs(0) - 1)
    def _():
        scale = lax.rsqrt(square[...] / D + 1e-06)
        own, other = first[...] * scale, second[...] * scale
        gates_here = core_ref[0] == 0
        gate_values = jnp.where(gates_here, own, other)
        up_values = jnp.where(gates_here, other, own)
        silu = gate_values / (1.0 + jnp.exp(-gate_values))
        out_ref[...] = (silu * up_values).astype(out_ref.dtype)


def down(core_ref, activation_ref, own_ref, other_ref, out_ref):
    core = core_ref[0]
    width = own_ref.shape[3]
    units = activation_ref.shape[2]
    own = own_ref[0].reshape(2, units, width)
    other = other_ref[0].reshape(2, units, width)
    total = jnp.zeros(out_ref.shape[1:], jnp.float32)
    for part in range(2):
        total += jnp.dot(
            activation_ref[2 * core + part], own[part], preferred_element_type=jnp.float32
        )
        total += jnp.dot(
            activation_ref[2 * (1 - core) + part], other[part], preferred_element_type=jnp.float32
        )
    out_ref[0] = total.astype(out_ref.dtype)


SCALAR = pl.BlockSpec(memory_space=pltpu.SMEM)
LIMIT = pltpu.CompilerParams(vmem_limit_bytes=32 * 1024 * 1024)


def exchange(message, axis, groups=None):
    return lax.all_to_all(
        message, axis, split_axis=0, concat_axis=0, tiled=True, axis_index_groups=groups
    )


def local(
    queries,
    all_key_rows,
    all_value_rows,
    out_weight,
    residual,
    post_gain,
    routes,
    route_weight,
    gate_weight,
    up_weight,
    down_weight,
):
    tokens = queries.shape[0]
    local_heads = queries.shape[1] // HEAD_WIDTH
    group_width = QUERY_HEADS // KEY_VALUE_HEADS
    tensor_count = lax.axis_size("tensor")
    expert_count = lax.axis_size("expert")
    tensor_index = lax.axis_index("tensor")
    expert_index = lax.axis_index("expert")
    core = lax.axis_index("dp")
    columns = D // tensor_count
    capacity = 2 * tokens * TOP // expert_count
    slot_count = expert_count * capacity
    part = capacity // QUARTER
    rows = expert_count * part

    core_scalar = core.astype(jnp.int32).reshape(1)
    hidden_units = down_weight.shape[1]
    half_units = hidden_units // 2
    local_units = gate_weight.shape[2]
    first_blocks = D // columns
    blocks = first_blocks + half_units // local_units

    gate_or_up = jnp.where(core == 0, gate_weight[0], up_weight[0]).T
    gate_or_up = jnp.transpose(gate_or_up.reshape(local_units, first_blocks, columns), (1, 0, 2))
    down_half = lax.dynamic_slice_in_dim(down_weight[0], core * half_units, half_units, 0)
    weights_here = jnp.concatenate(
        [gate_or_up.reshape(D // columns * local_units, columns), down_half], axis=0
    )

    shared = tensor_index * local_heads // group_width
    key_head = lax.dynamic_slice_in_dim(all_key_rows, shared * HEAD_WIDTH, HEAD_WIDTH, 1)
    value_head = lax.dynamic_slice_in_dim(all_value_rows, shared * HEAD_WIDTH, HEAD_WIDTH, 1)
    half_rows = out_weight.shape[0] // 2
    weight_half = lax.dynamic_slice_in_dim(out_weight, core * half_rows, half_rows, 0)
    message = jnp.concatenate([weight_half, jnp.concatenate([key_head, value_head], axis=1)], axis=0)
    message, weights_here = lax.optimization_barrier((message, weights_here))
    weights_own = lax.all_gather(weights_here, "tensor", axis=0, axis_index_groups=CLOSE)
    gathered = exchange(jnp.broadcast_to(message[None], (expert_count,) + message.shape), "expert")
    weight_own = gathered[:, :half_rows, :]
    weight_other = lax.ppermute(weight_own, "dp", SWAP)

    attended = pl.pallas_call(
        attend,
        out_shape=jax.ShapeDtypeStruct((2, tokens, half_rows), jnp.bfloat16),
        grid=(1,),
        in_specs=[
            SCALAR,
            pl.BlockSpec((tokens, local_heads * HEAD_WIDTH), lambda i: (0, 0)),
            pl.BlockSpec(
                (expert_count, tokens, 2 * HEAD_WIDTH), lambda i: (0, half_rows // tokens, 0)
            ),
        ],
        out_specs=pl.BlockSpec((2, tokens, half_rows), lambda i: (0, 0, 0)),
        scratch_shapes=[
            pltpu.VMEM((expert_count * tokens // CHUNK, local_heads * tokens, CHUNK), jnp.float32)
        ],
        compiler_params=LIMIT,
        name="attend",
    )(expert_index.astype(jnp.int32).reshape(1), queries, gathered)

    wide = 4
    partial_value = pl.pallas_call(
        project,
        out_shape=jax.ShapeDtypeStruct((tensor_count, tokens, columns), jnp.bfloat16),
        grid=(tensor_count // wide,),
        in_specs=[
            SCALAR,
            pl.BlockSpec((2, tokens, half_rows), lambda i: (0, 0, 0)),
            pl.BlockSpec((wide, half_rows, columns), lambda i: (i, 0, 0)),
            pl.BlockSpec((wide, half_rows, columns), lambda i: (i, 0, 0)),
        ],
        out_specs=pl.BlockSpec((wide, tokens, columns), lambda i: (i, 0, 0)),
        compiler_params=LIMIT,
        name="project",
    )(core_scalar, attended, gathered, weight_other)
    partial_value, weights_own = lax.optimization_barrier((partial_value, weights_own))
    partial_sums = exchange(partial_value, "tensor")
    weights_other = lax.ppermute(weights_own, "dp", SWAP)
    shape = (QUARTER, blocks, local_units, columns)
    weights_own, weights_other = weights_own.reshape(shape), weights_other.reshape(shape)
    head_total = jnp.sum(partial_sums.astype(jnp.float32), axis=0)
    residual_share = lax.dynamic_slice_in_dim(residual, tensor_index * columns, columns, 1)
    hidden_share = residual_share.astype(jnp.float32) + head_total

    flat_routes, slot_index = route_slots(routes, expert_count, capacity)
    target = flat_routes * capacity + slot_index
    slot_place = jnp.arange(slot_count, dtype=jnp.int32)
    packing = jnp.any(
        target.reshape(tokens, TOP)[None, :, :] == slot_place[:, None, None], axis=2
    ).astype(jnp.bfloat16)
    packed = jnp.dot(
        packing, hidden_share.astype(jnp.bfloat16), preferred_element_type=jnp.float32
    ).astype(jnp.bfloat16)
    arrived = exchange(packed.reshape(expert_count, capacity, columns), "expert")
    quarters = jnp.transpose(
        arrived.reshape(expert_count, QUARTER, part, columns), (1, 0, 2, 3)
    ).reshape(1, QUARTER, rows, columns)
    quarters = jnp.broadcast_to(quarters, (tensor_count // QUARTER, QUARTER, rows, columns))
    full_rows = exchange(quarters.reshape(tensor_count, rows, columns), "tensor")

    weight_spec = pl.BlockSpec((QUARTER, 1, local_units, columns), lambda i: (0, i, 0, 0))
    activation = pl.pallas_call(
        gate_up,
        out_shape=jax.ShapeDtypeStruct((rows, QUARTER * local_units), jnp.bfloat16),
        grid=(first_blocks,),
        in_specs=[
            SCALAR,
            pl.BlockSpec((1, rows, columns), lambda i: (i, 0, 0)),
            pl.BlockSpec((1, 1, columns), lambda i: (i, 0, 0)),
            weight_spec,
            weight_spec,
        ],
        out_specs=pl.BlockSpec((rows, QUARTER * local_units), lambda i: (0, 0)),
        scratch_shapes=[
            pltpu.VMEM((rows, 1), jnp.float32),
            pltpu.VMEM((rows, QUARTER * local_units), jnp.float32),
            pltpu.VMEM((rows, QUARTER * local_units), jnp.float32),
        ],
        compiler_params=LIMIT,
        name="gate_up",
    )(core_scalar, full_rows, post_gain.reshape(first_blocks, 1, columns), weights_own, weights_other)
    activation = exchange(
        jnp.broadcast_to(activation[None], (QUARTER,) + activation.shape), "tensor", SPREAD
    )
    down_blocks = half_units // local_units
    weight_spec = pl.BlockSpec(
        (1, down_blocks, local_units, columns), lambda i: (i, first_blocks // down_blocks, 0, 0)
    )
    expert_out = pl.pallas_call(
        down,
        out_shape=jax.ShapeDtypeStruct((QUARTER, rows, columns), jnp.bfloat16),
        grid=(QUARTER,),
        in_specs=[
            SCALAR,
            pl.BlockSpec((QUARTER, rows, QUARTER * local_units), lambda i: (0, 0, 0)),
            weight_spec,
            weight_spec,
        ],
        out_specs=pl.BlockSpec((1, rows, columns), lambda i: (i, 0, 0)),
        compiler_params=LIMIT,
        name="down",
    )(core_scalar, activation, weights_own, weights_other)
    together = [
        [
            (QUARTER * far + near) * expert_count + place
            for near in range(QUARTER)
            for place in range(expert_count)
        ]
        for far in range(tensor_count // QUARTER)
    ]
    returned = exchange(
        expert_out.reshape(QUARTER * expert_count, part, columns), ("tensor", "expert"), together
    ).reshape(slot_count, columns)
    place = (slot_index // part * expert_count + flat_routes) * part + slot_index % part
    picking = (place[:, None] == slot_place[None, :]).astype(jnp.bfloat16)
    picked = jnp.dot(picking, returned, preferred_element_type=jnp.float32)
    picked = picked.reshape(tokens, TOP, columns)
    mixed = jnp.sum(picked * route_weight[:, :, None], axis=1)
    return (hidden_share + mixed).astype(jnp.bfloat16)


def solution(mesh):
    return jax.shard_map(
        local,
        mesh=mesh,
        in_specs=(
            P(("dp", "expert"), "tensor"),
            P(("dp", "expert"), None),
            P(("dp", "expert"), None),
            P("tensor", "expert"),
            P(("dp", "expert"), None),
            P(),
            P(("dp", "expert"), None),
            P(("dp", "expert"), None),
            P("expert", None, "tensor"),
            P("expert", None, "tensor"),
            P("expert", None, "tensor"),
        ),
        out_specs=P(("dp", "expert"), "tensor"),
        check_vma=False,
    )
```

time: 355 us -> 323 us (0.910)
  waiting for transfers between devices: 176 us -> 129 us
  blocking collectives: 74.7 us -> 114 us
  starting transfers between devices: 49.1 us -> 31.8 us
  Pallas kernels: 0 us -> 16.8 us
  matrix products: 17.1 us -> 1.55 us
  local copies, waits for them, and re-layouts: 17.9 us -> 10.5 us
    all_gather x2 -> x1, waiting for transfers between devices: 95.4 us -> 42.2 us  [local(): lax.all_gather(weights_here, 'tensor', axis=0, axis_index_groups=CLOSE)]
    all_to_all x3 -> x4, blocking collectives: 74.7 us -> 114 us  [exchange(): lax.all_to_all(message, axis, split_axis=0, concat_axis=0, tiled=True, ax...]
    pallas_call x0 -> x4, Pallas kernels: none -> 16.8 us  [the longest x1 10.3 us: local(): pl.pallas_call(gate_up, out_shape=jax.ShapeDtypeStruct((rows, QUARTER * l...]
    all_to_all x3 -> x2, starting transfers between devices: 38.5 us -> 24.5 us  [exchange(): lax.all_to_all(message, axis, split_axis=0, concat_axis=0, tiled=True, ax...]
    dot_general x7 -> x0, matrix products: 13.6 us -> none  [the longest x1 3.15 us: local(): lax.dot_general(normed, first_other, contract_last, preferred_element_typ...]
    all_to_all x3 -> x2, waiting for transfers between devices: 80.2 us -> 85.7 us  [exchange(): lax.all_to_all(message, axis, split_axis=0, concat_axis=0, tiled=True, ax...]
    slice x4 -> x1, local copies, waits for them, and re-layouts: 6.82 us -> 1.46 us  [local(): weight_own = gathered[:, :half_rows, :]]
    unnamed x20 -> x22, local copies, waits for them, and re-layouts: 2.5 us -> 6.24 us
  transfers between devices with their start and end apart: 8 -> 5, of which waited for: 4 -> 4; matrix products, arithmetic and copies ran while one was open for 8% -> 1% of each run, Pallas kernels for 0% -> 1%
where the time goes in v2:
time: 323 us; the launch traced here: 322 us
  waiting for transfers between devices  129 us (40%)
  blocking collectives  114 us (35%)
  starting transfers between devices  31.8 us (10%)
  Pallas kernels  16.8 us (5%)
  between operations  13.6 us (4%)
  local copies, waits for them, and re-layouts  10.5 us (3%)
  other arithmetic  4.21 us (1%)
    all_to_all x4, blocking collectives, exchange(): lax.all_to_all(message, axis, split_axis=0, concat_axis=0, tiled=True, ax...  114 us
    all_to_all x2, waiting for transfers between devices, exchange(): lax.all_to_all(message, axis, split_axis=0, concat_axis=0, tiled=True, ax...  85.7 us
    all_gather x1, waiting for transfers between devices, local(): lax.all_gather(weights_here, 'tensor', axis=0, axis_index_groups=CLOSE)  42.2 us
    all_to_all x2, starting transfers between devices, exchange(): lax.all_to_all(message, axis, split_axis=0, concat_axis=0, tiled=True, ax...  24.5 us
    pallas_call x1, Pallas kernels, local(): pl.pallas_call(gate_up, out_shape=jax.ShapeDtypeStruct((rows, QUARTER * l...  10.3 us
  transfers between devices with their start and end apart: 5, of which 4 were waited for; matrix products, arithmetic and copies ran while one was open for 1% of the time, Pallas kernels for 1%

profile of v2, /device:TPU:1, one launch (start us, length us, event | category | flops | bytes accessed | tf_op | source)
XLA Modules:
  0.0 321.8 jit_solution(3831357749127993300)
XLA Ops:
  6.5 0.0 copy-start
  6.5 0.0 all-gather.3.cloned.1.call-start
  6.5 0.0 copy-start.7
  6.5 1.3 broadcast_select_fusion
  7.9 0.2 copy.49
  8.0 0.2 copy.41
  8.3 0.0 copy-done.7
  8.3 0.0 copy-done
  8.4 1.1 pad_maximum_fusion
  9.5 0.8 constant_dynamic-slice_fusion
  10.3 0.0 all-gather.3.cloned.1.call-update
  10.4 0.3 broadcast_in_dim.8
  10.7 46.5 %all_to_all.30.piece_ref.own_ref = bf16[16,384,256]{2,1,0:T(8,128)(2,1)S(1)} all-to-all(bf16[16,384,256]{2,1,0:T(8,128)(2,1)S(1)} %broadcast_in_dim.8), channel_id=1, replica_groups=mesh['dp'=2,'tensor'=16,'expert'=16] {'expert'}, dimensions={0} | all-to-all | bytes 6291456 | tf_op jit(solution)/shard_map/all_to_all | solution.py:152
  57.2 0.0 copy-start.5
  57.2 1.5 slice.4
  58.6 0.0 copy-start.1
  58.6 1.7 copy-done.1
  60.3 4.4 %collective-permute-start = (bf16[16,256,256]{2,1,0:T(8,128)(2,1)}, bf16[16,256,256]{2,1,0:T(8,128)(2,1)S(1)}, u32[]{:S(2)}, u32[]{:S(2)}) collective-permute-start(bf16[16,256,256]{2,1,0:T(8,128)(2,1)} %slice.4), channel_id=1, source_target_pairs={{0,256},{256,0},{1,257},{257,1},{2,258},{258,2},{3,259},{259,3},{4... | collective-permute-start | bytes 6291464 | tf_op jit(solution)/shard_map/ppermute | solution.py:208
  64.8 0.0 copy-done.5
  64.8 0.0 copy-start.2
  64.8 1.9 copy-done.2
  66.7 0.0 copy-start.3
  66.7 1.1 attend.1.attended_ref
  67.8 1.0 collective-permute-done.other_ref
  68.7 0.0 copy-done.3
  68.8 0.0 copy-start.8
  68.8 2.5 project.1
  71.3 42.2 %all-gather.3.cloned.1.call-done = bf16[9216,256]{1,0:T(8,128)(2,1)} async-done(((bf16[2304,256]{1,0:T(8,128)(2,1)}), bf16[9216,256]{1,0:T(8,128)(2,1)}) %all-gather.3.cloned.1.call-update) | async-done | bytes 4718608 | tf_op jit(solution)/shard_map/all_gather | solution.py:205
  113.5 10.9 %all-to-all-start.1 = ((bf16[16,128,256]{2,1,0:T(8,128)(2,1)}), bf16[16,128,256]{2,1,0:T(8,128)(2,1)S(1)}, u32[]{:S(2)}, u32[]{:S(2)}) async-start(bf16[16,128,256]{2,1,0:T(8,128)(2,1)} %project.1), calls=%async_computation.1 | async-start | bytes 2097152 | tf_op jit(solution)/shard_map/all_to_all | solution.py:152
  124.4 0.0 copy-done.8
  124.4 0.1 copy.42
  124.5 0.1 eq.63
  124.6 0.2 fusion.1
  124.9 0.1 convert_element_type.41
  125.0 0.1 copy.43
  125.1 0.1 fusion.4
  125.2 2.9 collective-permute-start.1
  128.0 41.2 %all-to-all-done.1 = bf16[16,128,256]{2,1,0:T(8,128)(2,1)S(1)} async-done(((bf16[16,128,256]{2,1,0:T(8,128)(2,1)}), bf16[16,128,256]{2,1,0:T(8,128)(2,1)S(1)}, u32[]{:S(2)}, u32[]{:S(2)}) %all-to-all-start.1) | async-done | bytes 1048608 | tf_op jit(solution)/shard_map/all_to_all | solution.py:152
  169.2 0.1 convert_reduce_fusion
  169.4 1.1 convolution_convert_fusion
  170.4 0.0 copy-start.6
  170.5 13.9 %all_to_all.31 = bf16[16,32,256]{2,1,0:T(8,128)(2,1)S(1)} all-to-all(bf16[16,32,256]{2,1,0:T(8,128)(2,1)S(1)} %bitcast.43), channel_id=1, replica_groups=mesh['dp'=2,'tensor'=16,'expert'=16] {'expert'}, dimensions={0} | all-to-all | bytes 524288 | tf_op jit(solution)/shard_map/all_to_all | solution.py:152
  184.4 1.1 broadcast_in_dim.10
  185.4 13.6 %all-to-all-start.3 = ((bf16[16,128,256]{2,1,0:T(8,128)(2,1)}), bf16[16,128,256]{2,1,0:T(8,128)(2,1)S(1)}, u32[]{:S(2)}, u32[]{:S(2)}) async-start(bf16[16,128,256]{2,1,0:T(8,128)(2,1)} %bitcast.13), calls=%async_computation.3 | async-start | bytes 2097152 | tf_op jit(solution)/shard_map/all_to_all | solution.py:152
  199.0 0.0 collective-permute-done.1
  199.0 44.5 %all-to-all-done.3.rows_ref = bf16[16,128,256]{2,1,0:T(8,128)(2,1)S(1)} async-done(((bf16[16,128,256]{2,1,0:T(8,128)(2,1)}), bf16[16,128,256]{2,1,0:T(8,128)(2,1)S(1)}, u32[]{:S(2)}, u32[]{:S(2)}) %all-to-all-start.3) | async-done | bytes 1048608 | tf_op jit(solution)/shard_map/all_to_all | solution.py:152
  243.5 0.0 copy-done.6
  243.5 0.0 copy-start.4
  243.5 2.3 copy-done.4
  245.8 10.3 %gate_up.1 = bf16[128,384]{1,0:T(8,128)(2,1)S(1)} custom-call(s32[1]{0:T(128)} %bitcast.core_ref, bf16[16,128,256]{2,1,0:T(8,128)(2,1)S(1)} %all-to-all-done.3.rows_ref, f32[16,1,256]{2,1,0:T(1,128)S(1)} %bitcast.39, bf16[4,24,96,256]{3,2,1,0:T(8,128)(2,1)S(1)} %bitcast.36, bf16[4,24,96,256]{3,2,1,0:T(8,128)(2,1)} %bitcast.16.other_ref), custom_call_target="tpu_custom_call" | custom-call | tf_op jit(solution)/shard_map/gate_up/pallas_call | solution.py:270
  256.2 33.7 %all_to_all.32.activation_ref = bf16[4,128,384]{2,1,0:T(8,128)(2,1)S(1)} all-to-all(bf16[4,128,384]{2,1,0:T(8,128)(2,1)S(1)} %broadcast_in_dim.11), channel_id=1, replica_groups={{0,64,128,192},{16,80,144,208},{32,96,160,224},{48,112,176,240},{1,65,1..., dimensions={0} | all-to-all | bytes 786432 | tf_op jit(solution)/shard_map/all_to_all | solution.py:152
  289.9 0.0 copy-start.9
  289.9 2.9 down.1
  292.8 20.4 %all_to_all.33 = bf16[64,8,256]{2,1,0:T(8,128)(2,1)S(1)} all-to-all(bf16[64,8,256]{2,1,0:T(8,128)(2,1)S(1)} %bitcast.38), channel_id=1, replica_groups={{0,1,2,3,4,5,6,7,8,9,10,11,12,13,14,15,16,17,18,19,20,21,22,23,24,25,26..., dimensions={0} | all-to-all | bytes 524288 | tf_op jit(solution)/shard_map/all_to_all | solution.py:152
  313.2 0.0 copy-done.9
  313.2 0.3 fusion
  313.5 1.5 add_convert_fusion
  (7 shorter events, 0.2 us)
Async XLA Ops:
  6.5 1.8 copy-start
  6.5 107.0 %all-gather.3.cloned.1.call-start = ((), (), s32[]{:S(2)}) async-start(), calls=%async_computation.6 | async-start | bytes 5898240 | tf_op jit(solution)/shard_map/all_gather | solution.py:205
  6.5 1.8 copy-start.7
  57.2 7.6 %copy-start.5 = (bf16[128,512]{1,0:T(8,128)(2,1)S(1)}, bf16[128,512]{1,0:T(8,128)(2,1)}, u32[]{:S(2)}) copy-start(bf16[128,512]{1,0:T(8,128)(2,1)} %query_ref.1) | copy-start | bytes 393220
  58.6 1.7 copy-start.1
  60.3 8.4 %collective-permute-start = (bf16[16,256,256]{2,1,0:T(8,128)(2,1)}, bf16[16,256,256]{2,1,0:T(8,128)(2,1)S(1)}, u32[]{:S(2)}, u32[]{:S(2)}) collective-permute-start(bf16[16,256,256]{2,1,0:T(8,128)(2,1)} %slice.4), channel_id=1, source_target_pairs={{0,256},{256,0},{1,257},{257,1},{2,258},{258,2},{3,259},{259,3},{4... | collective-permute-start | bytes 6291464 | tf_op jit(solution)/shard_map/ppermute | solution.py:208
  64.8 1.9 copy-start.2
  66.7 2.1 copy-start.3
  68.8 55.6 %copy-start.8 = (s32[128,2]{0,1:T(2,128)S(1)}, s32[128,2]{0,1:T(2,128)}, u32[]{:S(2)}) copy-start(s32[128,2]{0,1:T(2,128)} %param.17) | copy-start | bytes 3076
  113.5 55.7 %all-to-all-start.1 = ((bf16[16,128,256]{2,1,0:T(8,128)(2,1)}), bf16[16,128,256]{2,1,0:T(8,128)(2,1)S(1)}, u32[]{:S(2)}, u32[]{:S(2)}) async-start(bf16[16,128,256]{2,1,0:T(8,128)(2,1)} %project.1), calls=%async_computation.1 | async-start | bytes 2097152 | tf_op jit(solution)/shard_map/all_to_all | solution.py:152
  125.2 73.9 %collective-permute-start.1 = (bf16[4,2304,256]{2,1,0:T(8,128)(2,1)}, bf16[4,2304,256]{2,1,0:T(8,128)(2,1)}, u32[]{:S(2)}, u32[]{:S(2)}) collective-permute-start(bf16[4,2304,256]{2,1,0:T(8,128)(2,1)} %bitcast.35), channel_id=1, source_target_pairs={{0,256},{256,0},{1,257},{257,1},{2,258},{258,2},{3,259},{259,3},{4... | collective-permute-start | bytes 14155784 | tf_op jit(solution)/shard_map/ppermute | solution.py:246
  170.4 73.1 %copy-start.6 = (f32[4096]{0:T(1024)S(1)}, f32[4096]{0:T(1024)}, u32[]{:S(2)}) copy-start(f32[4096]{0:T(1024)} %param.16) | copy-start | bytes 49156
  185.4 58.1 %all-to-all-start.3 = ((bf16[16,128,256]{2,1,0:T(8,128)(2,1)}), bf16[16,128,256]{2,1,0:T(8,128)(2,1)S(1)}, u32[]{:S(2)}, u32[]{:S(2)}) async-start(bf16[16,128,256]{2,1,0:T(8,128)(2,1)} %bitcast.13), calls=%async_computation.3 | async-start | bytes 2097152 | tf_op jit(solution)/shard_map/all_to_all | solution.py:152
  243.5 2.3 copy-start.4
  289.9 23.3 %copy-start.9 = (f32[128,2]{0,1:T(2,128)S(1)}, f32[128,2]{0,1:T(2,128)}, u32[]{:S(2)}) copy-start(f32[128,2]{0,1:T(2,128)} %param.18) | copy-start | bytes 3076
Sparse Core Ops, SparseCore 0:
  10.5 102.9 all-gather.2

commit v3 on v2

v3 whole, which is shorter than its diff:
```python
import jax
import jax.numpy as jnp
from jax import lax
from jax.experimental import pallas as pl
from jax.experimental.pallas import tpu as pltpu
from jax.sharding import PartitionSpec as P

D = 4096
QUERY_HEADS = 64
KEY_VALUE_HEADS = 4
HEAD_WIDTH = 128
TOP = 2
SWAP = [(0, 1), (1, 0)]
CHUNK = 512


CONTRACT_LAST = (((1,), (1,)), ((), ()))


def attend(place_ref, query_ref, piece_ref, out_ref, score_ref):
    tokens = query_ref.shape[0]
    heads = query_ref.shape[1] // HEAD_WIDTH
    rows = heads * tokens
    blocks = CHUNK // tokens
    place = place_ref[0]
    stacked = jnp.concatenate(
        [query_ref[:, HEAD_WIDTH * h : HEAD_WIDTH * (h + 1)] for h in range(heads)], axis=0
    )
    token = place * tokens + lax.broadcasted_iota(jnp.int32, (rows, CHUNK), 0) % tokens
    offset = token - lax.broadcasted_iota(jnp.int32, (rows, CHUNK), 1)

    def score(step, row_max):
        keys = piece_ref[pl.ds(step * blocks, blocks), :, :HEAD_WIDTH].reshape(CHUNK, HEAD_WIDTH)
        scores = lax.dot_general(
            stacked, keys, CONTRACT_LAST, preferred_element_type=jnp.float32
        ) * HEAD_WIDTH ** (-0.5)
        masked = jnp.where(offset >= step * CHUNK, scores, -1e30)
        score_ref[step] = masked
        return jnp.maximum(row_max, jnp.max(masked, axis=1, keepdims=True))

    def weigh(step, carry):
        total, summed = carry
        exponent = jnp.exp(score_ref[step] - row_max)
        values = piece_ref[pl.ds(step * blocks, blocks), :, HEAD_WIDTH:].reshape(CHUNK, HEAD_WIDTH)
        return (
            total + jnp.sum(exponent, axis=1, keepdims=True),
            summed
            + jnp.dot(exponent.astype(jnp.bfloat16), values, preferred_element_type=jnp.float32),
        )

    steps = place // blocks + 1
    row_max = lax.fori_loop(0, steps, score, jnp.full((rows, 1), -1e30, jnp.float32))
    total, summed = lax.fori_loop(
        0,
        steps,
        weigh,
        (jnp.zeros((rows, 1), jnp.float32), jnp.zeros((rows, HEAD_WIDTH), jnp.float32)),
    )
    attended = (summed / total).astype(out_ref.dtype)
    halves = heads // 2
    for h in range(heads):
        out_ref[h // halves, :, HEAD_WIDTH * (h % halves) : HEAD_WIDTH * (h % halves + 1)] = (
            attended[tokens * h : tokens * (h + 1)]
        )


def project(core_ref, attended_ref, own_ref, other_ref, out_ref):
    core = core_ref[0]
    for block in range(own_ref.shape[0]):
        out_ref[block] = (
            jnp.dot(attended_ref[core], own_ref[block], preferred_element_type=jnp.float32)
            + jnp.dot(attended_ref[1 - core], other_ref[block], preferred_element_type=jnp.float32)
        ).astype(out_ref.dtype)


def gate_up(
    core_ref, rows_ref, gain_ref, routes_ref, own_ref, other_ref, out_ref, normed, first, second
):
    step = pl.program_id(0)
    experts, units, depth = own_ref.shape
    pieces, tokens, columns = rows_ref.shape
    per_step = depth // columns

    @pl.when(step == 0)
    def _():
        square = jnp.zeros((tokens, 1), jnp.float32)
        for piece in range(pieces):
            rows = rows_ref[piece].astype(jnp.float32)
            square += jnp.sum(rows * rows, axis=1, keepdims=True)
        scale = lax.rsqrt(square / D + 1e-06)
        for piece in range(pieces):
            start = piece % per_step * columns
            normed[piece // per_step, :, start : start + columns] = (
                rows_ref[piece].astype(jnp.float32) * scale * gain_ref[piece]
            ).astype(jnp.bfloat16)
        first[...] = jnp.zeros_like(first)
        second[...] = jnp.zeros_like(second)

    rows = normed[step]
    first[...] += lax.dot_general(
        own_ref[...].reshape(experts * units, depth),
        rows,
        CONTRACT_LAST,
        preferred_element_type=jnp.float32,
    )
    second[...] += lax.dot_general(
        other_ref[...].reshape(experts * units, depth),
        rows,
        CONTRACT_LAST,
        preferred_element_type=jnp.float32,
    )

    @pl.when(step == pl.num_programs(0) - 1)
    def _():
        gates_here = core_ref[0] == 0
        chosen = [jnp.zeros((units, tokens), jnp.float32) for _ in range(TOP)]
        for expert in range(experts):
            own = first[expert * units : (expert + 1) * units]
            other = second[expert * units : (expert + 1) * units]
            gate_values = jnp.where(gates_here, own, other)
            up_values = jnp.where(gates_here, other, own)
            activation = gate_values / (1.0 + jnp.exp(-gate_values)) * up_values
            for k in range(TOP):
                chosen[k] = jnp.where(routes_ref[k : k + 1] == expert, activation, chosen[k])
        for k in range(TOP):
            out_ref[k * units : (k + 1) * units] = chosen[k].astype(out_ref.dtype)


def down(
    core_ref,
    activation_ref,
    routes_ref,
    route_weight_ref,
    hidden_ref,
    own_ref,
    other_ref,
    out_ref,
    turned,
    mixed,
):
    step = pl.program_id(0)
    core = core_ref[0]
    per_step = own_ref.shape[0]
    pieces = activation_ref.shape[0] // 2
    units = activation_ref.shape[1] // TOP

    @pl.when(step == 0)
    def _():
        for half in range(2):
            for k in range(TOP):
                part = activation_ref[pieces * half : pieces * (half + 1), k * units : (k + 1) * units]
                part = part.reshape(pieces * units, part.shape[2]).astype(jnp.float32)
                turned[half, k] = jnp.transpose(part).astype(turned.dtype)
        mixed[...] = jnp.zeros_like(mixed)

    for place in range(per_step):
        expert = step * per_step + place
        here = [routes_ref[:, k : k + 1] == expert for k in range(TOP)]
        share = sum(jnp.where(here[k], route_weight_ref[:, k : k + 1], 0.0) for k in range(TOP))
        masks = [here[k].astype(jnp.bfloat16) for k in range(TOP)]
        total = jnp.zeros(mixed.shape, jnp.float32)
        for half, weight_ref in ((core, own_ref), (1 - core, other_ref)):
            rows = sum(turned[half, k] * masks[k] for k in range(TOP))
            total += jnp.dot(rows, weight_ref[place], preferred_element_type=jnp.float32)
        mixed[...] += total.astype(jnp.bfloat16).astype(jnp.float32) * share

    @pl.when(step == pl.num_programs(0) - 1)
    def _():
        out_ref[...] = (hidden_ref[...] + mixed[...]).astype(out_ref.dtype)


SCALAR = pl.BlockSpec(memory_space=pltpu.SMEM)
LIMIT = pltpu.CompilerParams(vmem_limit_bytes=40 * 1024 * 1024)


def exchange(message, axis):
    return lax.all_to_all(message, axis, split_axis=0, concat_axis=0, tiled=True)


def spread(rows, axis):
    return exchange(jnp.broadcast_to(rows[None], (lax.axis_size(axis),) + rows.shape), axis)


def local(
    queries,
    all_key_rows,
    all_value_rows,
    out_weight,
    residual,
    post_gain,
    routes,
    route_weight,
    gate_weight,
    up_weight,
    down_weight,
):
    tokens = queries.shape[0]
    local_heads = queries.shape[1] // HEAD_WIDTH
    group_width = QUERY_HEADS // KEY_VALUE_HEADS
    tensor_count = lax.axis_size("tensor")
    expert_count = lax.axis_size("expert")
    tensor_index = lax.axis_index("tensor")
    expert_index = lax.axis_index("expert")
    core = lax.axis_index("dp")
    columns = D // tensor_count
    core_scalar = core.astype(jnp.int32).reshape(1)
    hidden_units = down_weight.shape[1]
    half_units = hidden_units // 2
    local_units = gate_weight.shape[2]

    gate_or_up = jnp.where(core == 0, gate_weight[0], up_weight[0]).T
    down_half = lax.dynamic_slice_in_dim(down_weight[0], core * half_units, half_units, 0)

    shared = tensor_index * local_heads // group_width
    key_head = lax.dynamic_slice_in_dim(all_key_rows, shared * HEAD_WIDTH, HEAD_WIDTH, 1)
    value_head = lax.dynamic_slice_in_dim(all_value_rows, shared * HEAD_WIDTH, HEAD_WIDTH, 1)
    half_rows = out_weight.shape[0] // 2
    weight_half = lax.dynamic_slice_in_dim(out_weight, core * half_rows, half_rows, 0)
    message = jnp.concatenate([weight_half, jnp.concatenate([key_head, value_head], axis=1)], axis=0)
    message, gate_or_up, down_half = lax.optimization_barrier((message, gate_or_up, down_half))
    first_own = lax.all_gather(gate_or_up, "expert", axis=0)
    down_own = lax.all_gather(down_half, "expert", axis=0)
    gathered = spread(message, "expert")
    weight_own = gathered[:, :half_rows, :]
    weight_other = lax.ppermute(weight_own, "dp", SWAP)

    attended = pl.pallas_call(
        attend,
        out_shape=jax.ShapeDtypeStruct((2, tokens, half_rows), jnp.bfloat16),
        grid=(1,),
        in_specs=[
            SCALAR,
            pl.BlockSpec((tokens, local_heads * HEAD_WIDTH), lambda i: (0, 0)),
            pl.BlockSpec(
                (expert_count, tokens, 2 * HEAD_WIDTH), lambda i: (0, half_rows // tokens, 0)
            ),
        ],
        out_specs=pl.BlockSpec((2, tokens, half_rows), lambda i: (0, 0, 0)),
        scratch_shapes=[
            pltpu.VMEM((expert_count * tokens // CHUNK, local_heads * tokens, CHUNK), jnp.float32)
        ],
        compiler_params=LIMIT,
        name="attend",
    )(expert_index.astype(jnp.int32).reshape(1), queries, gathered)

    wide = 4
    partial_value = pl.pallas_call(
        project,
        out_shape=jax.ShapeDtypeStruct((tensor_count, tokens, columns), jnp.bfloat16),
        grid=(tensor_count // wide,),
        in_specs=[
            SCALAR,
            pl.BlockSpec((2, tokens, half_rows), lambda i: (0, 0, 0)),
            pl.BlockSpec((wide, half_rows, columns), lambda i: (i, 0, 0)),
            pl.BlockSpec((wide, half_rows, columns), lambda i: (i, 0, 0)),
        ],
        out_specs=pl.BlockSpec((wide, tokens, columns), lambda i: (i, 0, 0)),
        compiler_params=LIMIT,
        name="project",
    )(core_scalar, attended, gathered, weight_other)
    partial_sums = exchange(partial_value, "tensor")
    head_total = jnp.sum(partial_sums.astype(jnp.float32), axis=0)
    residual_share = lax.dynamic_slice_in_dim(residual, tensor_index * columns, columns, 1)
    hidden_share = residual_share.astype(jnp.float32) + head_total
    hidden_share, first_own = lax.optimization_barrier((hidden_share, first_own))
    full_rows = spread(hidden_share.astype(jnp.bfloat16), "tensor")

    first_other = lax.ppermute(first_own, "dp", SWAP)
    depth = 512
    steps = D // depth
    weight_spec = pl.BlockSpec((expert_count, local_units, depth), lambda i: (0, 0, i))
    activation = pl.pallas_call(
        gate_up,
        out_shape=jax.ShapeDtypeStruct((TOP * local_units, tokens), jnp.bfloat16),
        grid=(steps,),
        in_specs=[
            SCALAR,
            pl.BlockSpec((tensor_count, tokens, columns), lambda i: (0, 0, 0)),
            pl.BlockSpec((tensor_count, 1, columns), lambda i: (0, 0, 0)),
            pl.BlockSpec((TOP, tokens), lambda i: (0, 0)),
            weight_spec,
            weight_spec,
        ],
        out_specs=pl.BlockSpec((TOP * local_units, tokens), lambda i: (0, 0)),
        scratch_shapes=[
            pltpu.VMEM((steps, tokens, depth), jnp.bfloat16),
            pltpu.VMEM((expert_count * local_units, tokens), jnp.float32),
            pltpu.VMEM((expert_count * local_units, tokens), jnp.float32),
        ],
        compiler_params=LIMIT,
        name="gate_up",
    )(
        core_scalar,
        full_rows,
        post_gain.reshape(tensor_count, 1, columns),
        routes.T,
        first_own,
        first_other,
    )
    activation, down_own = lax.optimization_barrier((activation, down_own))
    activation = spread(activation, "tensor")

    down_other = lax.ppermute(down_own, "dp", SWAP)
    per_step = 2
    weight_spec = pl.BlockSpec((per_step, half_units, columns), lambda i: (i, 0, 0))
    return pl.pallas_call(
        down,
        out_shape=jax.ShapeDtypeStruct((tokens, columns), jnp.bfloat16),
        grid=(expert_count // per_step,),
        in_specs=[
            SCALAR,
            pl.BlockSpec((tensor_count, TOP * local_units, tokens), lambda i: (0, 0, 0)),
            pl.BlockSpec((tokens, TOP), lambda i: (0, 0)),
            pl.BlockSpec((tokens, TOP), lambda i: (0, 0)),
            pl.BlockSpec((tokens, columns), lambda i: (0, 0)),
            weight_spec,
            weight_spec,
        ],
        out_specs=pl.BlockSpec((tokens, columns), lambda i: (0, 0)),
        scratch_shapes=[
            pltpu.VMEM((2, TOP, tokens, half_units), jnp.bfloat16),
            pltpu.VMEM((tokens, columns), jnp.float32),
        ],
        compiler_params=LIMIT,
        name="down",
    )(core_scalar, activation, routes, route_weight, hidden_share, down_own, down_other)


def solution(mesh):
    return jax.shard_map(
        local,
        mesh=mesh,
        in_specs=(
            P(("dp", "expert"), "tensor"),
            P(("dp", "expert"), None),
            P(("dp", "expert"), None),
            P("tensor", "expert"),
            P(("dp", "expert"), None),
            P(),
            P(("dp", "expert"), None),
            P(("dp", "expert"), None),
            P("expert", None, "tensor"),
            P("expert", None, "tensor"),
            P("expert", None, "tensor"),
        ),
        out_specs=P(("dp", "expert"), "tensor"),
        check_vma=False,
    )
```

time: 323 us -> 296 us (0.916)
  waiting for transfers between devices: 129 us -> 82.8 us
  starting transfers between devices: 31.8 us -> 40.5 us
  Pallas kernels: 16.8 us -> 23.9 us
  local copies, waits for them, and re-layouts: 10.5 us -> 17 us
    all_gather x1 -> x2, waiting for transfers between devices: 42.2 us -> 0.04 us  [the longest x1 0.02 us: local(): first_own = lax.all_gather(gate_or_up, 'expert', axis=0)]
    ppermute x1 -> x2, starting transfers between devices: 2.86 us -> 14.9 us  [the longest x1 7.61 us: local(): down_other = lax.ppermute(down_own, 'dp', SWAP)]
    pallas_call x2, Pallas kernels: 13.3 us -> 20.3 us  [the longest x1 12.5 us: local(): pl.pallas_call(gate_up, out_shape=jax.ShapeDtypeStruct((TOP * local_units...]
    unnamed x22, local copies, waits for them, and re-layouts: 6.24 us -> 11.5 us
    all_to_all x2, waiting for transfers between devices: 85.7 us -> 81.7 us  [exchange(): lax.all_to_all(message, axis, split_axis=0, concat_axis=0, tiled=True)]
    all_to_all x2, starting transfers between devices: 24.5 us -> 20.7 us  [exchange(): lax.all_to_all(message, axis, split_axis=0, concat_axis=0, tiled=True)]
    all_to_all x4 -> x2, blocking collectives: 114 us -> 112 us  [exchange(): lax.all_to_all(message, axis, split_axis=0, concat_axis=0, tiled=True)]
  transfers between devices with their start and end apart: 5 -> 7, of which waited for: 4 -> 3; matrix products, arithmetic and copies ran while one was open for 1% -> 1% of each run, Pallas kernels for 1% -> 5%
where the time goes in v3:
time: 296 us; the launch traced here: 293 us
  blocking collectives  112 us (38%)
  waiting for transfers between devices  82.8 us (28%)
  starting transfers between devices  40.5 us (14%)
  Pallas kernels  23.9 us (8%)
  local copies, waits for them, and re-layouts  17 us (6%)
  between operations  13.6 us (5%)
  other arithmetic  3.17 us (1%)
    all_to_all x2, blocking collectives, exchange(): lax.all_to_all(message, axis, split_axis=0, concat_axis=0, tiled=True)  112 us
    all_to_all x2, waiting for transfers between devices, exchange(): lax.all_to_all(message, axis, split_axis=0, concat_axis=0, tiled=True)  81.7 us
    all_to_all x2, starting transfers between devices, exchange(): lax.all_to_all(message, axis, split_axis=0, concat_axis=0, tiled=True)  20.7 us
    pallas_call x1, Pallas kernels, local(): pl.pallas_call(gate_up, out_shape=jax.ShapeDtypeStruct((TOP * local_units...  12.5 us
    unnamed x22, local copies, waits for them, and re-layouts  11.5 us
    pallas_call x1, Pallas kernels, local(): pl.pallas_call(down, out_shape=jax.ShapeDtypeStruct((tokens, columns), jn...  7.88 us
    ppermute x1, starting transfers between devices, local(): down_other = lax.ppermute(down_own, 'dp', SWAP)  7.61 us
    ppermute x1, starting transfers between devices, local(): first_other = lax.ppermute(first_own, 'dp', SWAP)  7.26 us
  transfers between devices with their start and end apart: 7, of which 3 were waited for; matrix products, arithmetic and copies ran while one was open for 1% of the time, Pallas kernels for 5%

profile of v3, /device:TPU:1, one launch (start us, length us, event | category | flops | bytes accessed | tf_op | source)
XLA Modules:
  0.0 293.2 jit_solution(17657865457525971416)
XLA Ops:
  6.5 0.0 copy-start
  6.5 0.0 all-gather.5.cloned.1.call-start
  6.5 1.0 constant_dynamic-slice_fusion.2
  7.5 0.2 copy-done
  7.7 0.8 dynamic-slice_bitcast_fusion
  8.5 0.8 constant_dynamic-slice_fusion
  9.3 2.1 select_bitcast_fusion
  11.4 0.0 all-gather.5.cloned.1.call-update
  11.5 0.3 broadcast_in_dim.6
  11.8 58.2 %all_to_all.20.piece_ref.own_ref = bf16[16,384,256]{2,1,0:T(8,128)(2,1)S(1)} all-to-all(bf16[16,384,256]{2,1,0:T(8,128)(2,1)S(1)} %broadcast_in_dim.6), channel_id=1, replica_groups=mesh['dp'=2,'tensor'=16,'expert'=16] {'expert'}, dimensions={0} | all-to-all | bytes 6291456 | tf_op jit(solution)/shard_map/all_to_all | solution.py:177
  70.0 0.0 copy-start.6
  70.0 1.5 slice.4
  71.4 0.0 copy-start.1
  71.4 1.6 copy-done.1
  73.1 4.9 %collective-permute-start = (bf16[16,256,256]{2,1,0:T(8,128)(2,1)}, bf16[16,256,256]{2,1,0:T(8,128)(2,1)S(1)}, u32[]{:S(2)}, u32[]{:S(2)}) collective-permute-start(bf16[16,256,256]{2,1,0:T(8,128)(2,1)} %slice.4), channel_id=1, source_target_pairs={{0,256},{256,0},{1,257},{257,1},{2,258},{258,2},{3,259},{259,3},{4... | collective-permute-start | bytes 6291464 | tf_op jit(solution)/shard_map/ppermute | solution.py:225
  78.0 0.0 copy-done.6
  78.0 0.0 copy-start.2
  78.0 1.9 copy-done.2
  79.9 0.0 copy-start.3
  79.9 1.1 attend.1.attended_ref
  81.0 1.0 collective-permute-done.other_ref
  81.9 0.0 copy-done.3
  81.9 2.5 project.1
  84.5 14.3 %all-to-all-start.1 = ((bf16[16,128,256]{2,1,0:T(8,128)(2,1)}), bf16[16,128,256]{2,1,0:T(8,128)(2,1)S(1)}, u32[]{:S(2)}, u32[]{:S(2)}) async-start(bf16[16,128,256]{2,1,0:T(8,128)(2,1)} %project.1), calls=%async_computation.1 | async-start | bytes 2097152 | tf_op jit(solution)/shard_map/all_to_all | solution.py:177
  98.8 0.0 copy-start.7
  98.8 0.0 copy-start.8
  98.8 0.0 all-gather.7.cloned.1.call-start
  98.9 45.4 %all-to-all-done.1 = bf16[16,128,256]{2,1,0:T(8,128)(2,1)S(1)} async-done(((bf16[16,128,256]{2,1,0:T(8,128)(2,1)}), bf16[16,128,256]{2,1,0:T(8,128)(2,1)S(1)}, u32[]{:S(2)}, u32[]{:S(2)}) %all-to-all-start.1) | async-done | bytes 1048608 | tf_op jit(solution)/shard_map/all_to_all | solution.py:177
  144.3 0.1 convert_reduce_fusion
  144.4 0.9 convert_add_fusion.hidden_ref
  145.3 0.0 all-gather.5.cloned.1.call-done
  145.3 7.3 %collective-permute-start.1 = (bf16[16,96,4096]{2,1,0:T(8,128)(2,1)}, bf16[16,96,4096]{2,1,0:T(8,128)(2,1)}, u32[]{:S(2)}, u32[]{:S(2)}) collective-permute-start(bf16[16,96,4096]{2,1,0:T(8,128)(2,1)} %bitcast.12), channel_id=1, source_target_pairs={{0,256},{256,0},{1,257},{257,1},{2,258},{258,2},{3,259},{259,3},{4... | collective-permute-start | bytes 37748744 | tf_op jit(solution)/shard_map/ppermute | solution.py:268
  152.6 0.0 all-gather.7.cloned.1.call-update
  152.6 0.1 broadcast_in_dim.7
  152.7 54.1 %all_to_all.21.rows_ref = bf16[16,128,256]{2,1,0:T(8,128)(2,1)S(1)} all-to-all(bf16[16,128,256]{2,1,0:T(8,128)(2,1)S(1)} %broadcast_in_dim.7), channel_id=1, replica_groups=mesh['dp'=2,'tensor'=16,'expert'=16] {'tensor'}, dimensions={0} | all-to-all | bytes 2097152 | tf_op jit(solution)/shard_map/all_to_all | solution.py:177
  206.8 0.0 collective-permute-done.1.other_ref
  206.8 0.0 copy-done.7
  206.8 0.0 copy-done.8
  206.8 0.0 copy-start.4
  206.8 4.8 %copy-done.4 = bf16[1536,4096]{1,0:T(8,128)(2,1)S(1)} copy-done((bf16[1536,4096]{1,0:T(8,128)(2,1)S(1)}, bf16[1536,4096]{1,0:T(8,128)(2,1)}, u32[]{:S(2)}) %copy-start.4) | copy-done | bytes 12582936
  211.6 0.0 copy-start.9
  211.6 12.5 %gate_up.1 = bf16[192,128]{1,0:T(8,128)(2,1)S(1)} custom-call(s32[1]{0:T(128)} %bitcast.core_ref, bf16[16,128,256]{2,1,0:T(8,128)(2,1)S(1)} %all_to_all.21.rows_ref, f32[16,1,256]{2,1,0:T(1,128)S(1)} %bitcast.16, s32[2,128]{1,0:T(2,128)S(1)} %bitcast.17, bf16[16,96,4096]{2,1,0:T(8,128)(2,1)S(1)} %bitcast.13, ...), custom_call_target="tpu_custom_call" | custom-call | tf_op jit(solution)/shard_map/gate_up/pallas_call | solution.py:272
  224.1 0.0 all-gather.7.cloned.1.call-done
  224.1 7.6 %collective-permute-start.2 = (bf16[16,768,256]{2,1,0:T(8,128)(2,1)}, bf16[16,768,256]{2,1,0:T(8,128)(2,1)}, u32[]{:S(2)}, u32[]{:S(2)}) collective-permute-start(bf16[16,768,256]{2,1,0:T(8,128)(2,1)} %bitcast.14), channel_id=1, source_target_pairs={{0,256},{256,0},{1,257},{257,1},{2,258},{258,2},{3,259},{259,3},{4... | collective-permute-start | bytes 18874376 | tf_op jit(solution)/shard_map/ppermute | solution.py:303
  231.7 1.1 broadcast_in_dim.8
  232.8 6.3 %all-to-all-start.3 = ((bf16[16,192,128]{2,1,0:T(8,128)(2,1)}), bf16[16,192,128]{2,1,0:T(8,128)(2,1)S(1)}, u32[]{:S(2)}, u32[]{:S(2)}) async-start(bf16[16,192,128]{2,1,0:T(8,128)(2,1)} %broadcast_in_dim.8), calls=%async_computation.3 | async-start | bytes 1572864 | tf_op jit(solution)/shard_map/all_to_all | solution.py:177
  239.1 0.1 copy.12.routes_ref
  239.2 0.0 copy-done.9
  239.2 0.1 copy.13.route_weight_ref
  239.4 36.3 %all-to-all-done.3.activation_ref = bf16[16,192,128]{2,1,0:T(8,128)(2,1)S(1)} async-done(((bf16[16,192,128]{2,1,0:T(8,128)(2,1)}), bf16[16,192,128]{2,1,0:T(8,128)(2,1)S(1)}, u32[]{:S(2)}, u32[]{:S(2)}) %all-to-all-start.3) | async-done | bytes 786464 | tf_op jit(solution)/shard_map/all_to_all | solution.py:177
  275.7 0.0 collective-permute-done.2.other_ref
  275.7 0.0 copy-start.5
  275.7 2.8 copy-done.5
  278.5 7.9 %down.1 = bf16[128,256]{1,0:T(8,128)(2,1)} custom-call(s32[1]{0:T(128)} %bitcast.core_ref, bf16[16,192,128]{2,1,0:T(8,128)(2,1)S(1)} %all-to-all-done.3.activation_ref, s32[128,2]{1,0:T(8,128)S(1)} %copy.12.routes_ref, f32[128,2]{1,0:T(8,128)S(1)} %copy.13.route_weight_ref, f32[128,256]{1,0:T(8,128)S(1)} %convert_add_fusion.hidden_ref, ...), custom_call_target="tpu_custom_call" | custom-call | tf_op jit(solution)/shard_map/down/pallas_call | solution.py:306
  (2 shorter events, 0.0 us)
Async XLA Ops:
  6.5 1.2 copy-start
  6.5 138.8 %all-gather.5.cloned.1.call-start = ((), (), s32[]{:S(2)}) async-start(), calls=%async_computation.4 | async-start | bytes 13369344 | tf_op jit(solution)/shard_map/all_gather | solution.py:221
  70.0 8.0 %copy-start.6 = (bf16[128,512]{1,0:T(8,128)(2,1)S(1)}, bf16[128,512]{1,0:T(8,128)(2,1)}, u32[]{:S(2)}) copy-start(bf16[128,512]{1,0:T(8,128)(2,1)} %query_ref.1) | copy-start | bytes 393220
  71.4 1.6 copy-start.1
  73.1 8.9 %collective-permute-start = (bf16[16,256,256]{2,1,0:T(8,128)(2,1)}, bf16[16,256,256]{2,1,0:T(8,128)(2,1)S(1)}, u32[]{:S(2)}, u32[]{:S(2)}) collective-permute-start(bf16[16,256,256]{2,1,0:T(8,128)(2,1)} %slice.4), channel_id=1, source_target_pairs={{0,256},{256,0},{1,257},{257,1},{2,258},{258,2},{3,259},{259,3},{4... | collective-permute-start | bytes 6291464 | tf_op jit(solution)/shard_map/ppermute | solution.py:225
  78.0 1.9 copy-start.2
  79.9 2.1 copy-start.3
  84.5 59.8 %all-to-all-start.1 = ((bf16[16,128,256]{2,1,0:T(8,128)(2,1)}), bf16[16,128,256]{2,1,0:T(8,128)(2,1)S(1)}, u32[]{:S(2)}, u32[]{:S(2)}) async-start(bf16[16,128,256]{2,1,0:T(8,128)(2,1)} %project.1), calls=%async_computation.1 | async-start | bytes 2097152 | tf_op jit(solution)/shard_map/all_to_all | solution.py:177
  98.8 108.0 %copy-start.7 = (f32[4096]{0:T(1024)S(1)}, f32[4096]{0:T(1024)}, u32[]{:S(2)}) copy-start(f32[4096]{0:T(1024)} %param.16) | copy-start | bytes 49156
  98.8 108.0 %copy-start.8 = (s32[128,2]{0,1:T(2,128)S(1)}, s32[128,2]{0,1:T(2,128)}, u32[]{:S(2)}) copy-start(s32[128,2]{0,1:T(2,128)} %param.17) | copy-start | bytes 3076
  98.8 125.3 %all-gather.7.cloned.1.call-start = ((), (), s32[]{:S(2)}) async-start(), calls=%async_computation.5 | async-start | bytes 6684672 | tf_op jit(solution)/shard_map/all_gather | solution.py:222
  145.3 61.5 %collective-permute-start.1 = (bf16[16,96,4096]{2,1,0:T(8,128)(2,1)}, bf16[16,96,4096]{2,1,0:T(8,128)(2,1)}, u32[]{:S(2)}, u32[]{:S(2)}) collective-permute-start(bf16[16,96,4096]{2,1,0:T(8,128)(2,1)} %bitcast.12), channel_id=1, source_target_pairs={{0,256},{256,0},{1,257},{257,1},{2,258},{258,2},{3,259},{259,3},{4... | collective-permute-start | bytes 37748744 | tf_op jit(solution)/shard_map/ppermute | solution.py:268
  206.8 4.8 %copy-start.4 = (bf16[1536,4096]{1,0:T(8,128)(2,1)S(1)}, bf16[1536,4096]{1,0:T(8,128)(2,1)}, u32[]{:S(2)}) copy-start(bf16[1536,4096]{1,0:T(8,128)(2,1)} %all-gather.5.cloned.1.call-done) | copy-start | bytes 37748740
  211.6 27.6 %copy-start.9 = (f32[128,2]{0,1:T(2,128)S(1)}, f32[128,2]{0,1:T(2,128)}, u32[]{:S(2)}) copy-start(f32[128,2]{0,1:T(2,128)} %param.18) | copy-start | bytes 3076
  224.1 51.6 %collective-permute-start.2 = (bf16[16,768,256]{2,1,0:T(8,128)(2,1)}, bf16[16,768,256]{2,1,0:T(8,128)(2,1)}, u32[]{:S(2)}, u32[]{:S(2)}) collective-permute-start(bf16[16,768,256]{2,1,0:T(8,128)(2,1)} %bitcast.14), channel_id=1, source_target_pairs={{0,256},{256,0},{1,257},{257,1},{2,258},{258,2},{3,259},{259,3},{4... | collective-permute-start | bytes 18874376 | tf_op jit(solution)/shard_map/ppermute | solution.py:303
  232.8 42.9 %all-to-all-start.3 = ((bf16[16,192,128]{2,1,0:T(8,128)(2,1)}), bf16[16,192,128]{2,1,0:T(8,128)(2,1)S(1)}, u32[]{:S(2)}, u32[]{:S(2)}) async-start(bf16[16,192,128]{2,1,0:T(8,128)(2,1)} %broadcast_in_dim.8), calls=%async_computation.3 | async-start | bytes 1572864 | tf_op jit(solution)/shard_map/all_to_all | solution.py:177
  275.7 2.8 copy-start.5
Sparse Core Ops, SparseCore 0:
  11.6 130.0 all-gather.4
  152.7 70.1 all-gather.6

commit v4 on v3

--- a/solution.py
+++ b/solution.py
@@ -73,13 +73,13 @@
         ).astype(out_ref.dtype)
 
 
-def gate_up(
-    core_ref, rows_ref, gain_ref, routes_ref, own_ref, other_ref, out_ref, normed, first, second
-):
+def gate_up(rows_ref, gain_ref, routes_ref, *refs):
+    parts = (len(refs) - 4) // 2
+    gate_refs, up_refs = refs[:parts], refs[parts : 2 * parts]
+    out_ref, normed, first, second = refs[2 * parts :]
     step = pl.program_id(0)
-    experts, units, depth = own_ref.shape
-    pieces, tokens, columns = rows_ref.shape
-    per_step = depth // columns
+    experts, per_step, units, columns = gate_refs[0].shape
+    pieces, tokens, _ = rows_ref.shape
 
     @pl.when(step == 0)
     def _():
@@ -89,36 +89,31 @@
             square += jnp.sum(rows * rows, axis=1, keepdims=True)
         scale = lax.rsqrt(square / D + 1e-06)
         for piece in range(pieces):
-            start = piece % per_step * columns
-            normed[piece // per_step, :, start : start + columns] = (
+            normed[piece] = (
                 rows_ref[piece].astype(jnp.float32) * scale * gain_ref[piece]
             ).astype(jnp.bfloat16)
         first[...] = jnp.zeros_like(first)
         second[...] = jnp.zeros_like(second)
 
-    rows = normed[step]
-    first[...] += lax.dot_general(
-        own_ref[...].reshape(experts * units, depth),
-        rows,
-        CONTRACT_LAST,
-        preferred_element_type=jnp.float32,
-    )
-    second[...] += lax.dot_general(
-        other_ref[...].reshape(experts * units, depth),
-        rows,
-        CONTRACT_LAST,
-        preferred_element_type=jnp.float32,
-    )
+    for weight_refs, total in ((gate_refs, first), (up_refs, second)):
+        for part, weight_ref in enumerate(weight_refs):
+            place = pl.ds(part * experts * units, experts * units)
+            product = total[place]
+            for piece in range(per_step):
+                product += lax.dot_general(
+                    weight_ref[:, piece].reshape(experts * units, columns),
+                    normed[step * per_step + piece],
+                    CONTRACT_LAST,
+                    preferred_element_type=jnp.float32,
+                )
+            total[place] = product
 
     @pl.when(step == pl.num_programs(0) - 1)
     def _():
-        gates_here = core_ref[0] == 0
         chosen = [jnp.zeros((units, tokens), jnp.float32) for _ in range(TOP)]
-        for expert in range(experts):
-            own = first[expert * units : (expert + 1) * units]
-            other = second[expert * units : (expert + 1) * units]
-            gate_values = jnp.where(gates_here, own, other)
-            up_values = jnp.where(gates_here, other, own)
+        for expert in range(parts * experts):
+            gate_values = first[expert * units : (expert + 1) * units]
+            up_values = second[expert * units : (expert + 1) * units]
             activation = gate_values / (1.0 + jnp.exp(-gate_values)) * up_values
             for k in range(TOP):
                 chosen[k] = jnp.where(routes_ref[k : k + 1] == expert, activation, chosen[k])
@@ -126,43 +121,34 @@
             out_ref[k * units : (k + 1) * units] = chosen[k].astype(out_ref.dtype)
 
 
-def down(
-    core_ref,
-    activation_ref,
-    routes_ref,
-    route_weight_ref,
-    hidden_ref,
-    own_ref,
-    other_ref,
-    out_ref,
-    turned,
-    mixed,
-):
+def down(activation_ref, routes_ref, route_weight_ref, hidden_ref, *refs):
+    parts = (len(refs) - 3) // 2
+    half_refs = refs[:parts], refs[parts : 2 * parts]
+    out_ref, turned, mixed = refs[2 * parts :]
     step = pl.program_id(0)
-    core = core_ref[0]
-    per_step = own_ref.shape[0]
-    pieces = activation_ref.shape[0] // 2
-    units = activation_ref.shape[1] // TOP
+    per_part, blocks, units, columns = refs[0].shape
 
     @pl.when(step == 0)
     def _():
         for half in range(2):
             for k in range(TOP):
-                part = activation_ref[pieces * half : pieces * (half + 1), k * units : (k + 1) * units]
-                part = part.reshape(pieces * units, part.shape[2]).astype(jnp.float32)
+                part = activation_ref[blocks * half : blocks * (half + 1), k * units : (k + 1) * units]
+                part = part.reshape(blocks * units, part.shape[2]).astype(jnp.float32)
                 turned[half, k] = jnp.transpose(part).astype(turned.dtype)
         mixed[...] = jnp.zeros_like(mixed)
 
-    for place in range(per_step):
-        expert = step * per_step + place
-        here = [routes_ref[:, k : k + 1] == expert for k in range(TOP)]
-        share = sum(jnp.where(here[k], route_weight_ref[:, k : k + 1], 0.0) for k in range(TOP))
-        masks = [here[k].astype(jnp.bfloat16) for k in range(TOP)]
-        total = jnp.zeros(mixed.shape, jnp.float32)
-        for half, weight_ref in ((core, own_ref), (1 - core, other_ref)):
-            rows = sum(turned[half, k] * masks[k] for k in range(TOP))
-            total += jnp.dot(rows, weight_ref[place], preferred_element_type=jnp.float32)
-        mixed[...] += total.astype(jnp.bfloat16).astype(jnp.float32) * share
+    for part in range(parts):
+        for place in range(per_part):
+            expert = (step * parts + part) * per_part + place
+            here = [routes_ref[:, k : k + 1] == expert for k in range(TOP)]
+            share = sum(jnp.where(here[k], route_weight_ref[:, k : k + 1], 0.0) for k in range(TOP))
+            masks = [here[k].astype(jnp.bfloat16) for k in range(TOP)]
+            total = jnp.zeros(mixed.shape, jnp.float32)
+            for half in range(2):
+                rows = sum(turned[half, k] * masks[k] for k in range(TOP))
+                weight = half_refs[half][part][place].reshape(blocks * units, columns)
+                total += jnp.dot(rows, weight, preferred_element_type=jnp.float32)
+            mixed[...] += total.astype(jnp.bfloat16).astype(jnp.float32) * share
 
     @pl.when(step == pl.num_programs(0) - 1)
     def _():
@@ -170,7 +156,8 @@
 
 
 SCALAR = pl.BlockSpec(memory_space=pltpu.SMEM)
-LIMIT = pltpu.CompilerParams(vmem_limit_bytes=40 * 1024 * 1024)
+LIMIT = pltpu.CompilerParams(vmem_limit_bytes=32 * 1024 * 1024)
+WIDE = pltpu.CompilerParams(vmem_limit_bytes=56 * 1024 * 1024)
 
 
 def exchange(message, axis):
@@ -208,8 +195,16 @@
     half_units = hidden_units // 2
     local_units = gate_weight.shape[2]
 
+    first_blocks = D // columns
+    down_blocks = half_units // local_units
+    blocks = first_blocks + down_blocks
+
     gate_or_up = jnp.where(core == 0, gate_weight[0], up_weight[0]).T
+    gate_or_up = jnp.transpose(gate_or_up.reshape(local_units, first_blocks, columns), (1, 0, 2))
     down_half = lax.dynamic_slice_in_dim(down_weight[0], core * half_units, half_units, 0)
+    weights_here = jnp.concatenate(
+        [gate_or_up.reshape(first_blocks * local_units, columns), down_half], axis=0
+    )
 
     shared = tensor_index * local_heads // group_width
     key_head = lax.dynamic_slice_in_dim(all_key_rows, shared * HEAD_WIDTH, HEAD_WIDTH, 1)
@@ -217,9 +212,8 @@
     half_rows = out_weight.shape[0] // 2
     weight_half = lax.dynamic_slice_in_dim(out_weight, core * half_rows, half_rows, 0)
     message = jnp.concatenate([weight_half, jnp.concatenate([key_head, value_head], axis=1)], axis=0)
-    message, gate_or_up, down_half = lax.optimization_barrier((message, gate_or_up, down_half))
-    first_own = lax.all_gather(gate_or_up, "expert", axis=0)
-    down_own = lax.all_gather(down_half, "expert", axis=0)
+    message, weights_here = lax.optimization_barrier((message, weights_here))
+    weights = lax.all_gather(weights_here, ("dp", "expert"), axis=0)
     gathered = spread(message, "expert")
     weight_own = gathered[:, :half_rows, :]
     weight_other = lax.ppermute(weight_own, "dp", SWAP)
@@ -239,7 +233,7 @@
         scratch_shapes=[
             pltpu.VMEM((expert_count * tokens // CHUNK, local_heads * tokens, CHUNK), jnp.float32)
         ],
-        compiler_params=LIMIT,
+        compiler_params=WIDE,
         name="attend",
     )(expert_index.astype(jnp.int32).reshape(1), queries, gathered)
 
@@ -255,67 +249,70 @@
             pl.BlockSpec((wide, half_rows, columns), lambda i: (i, 0, 0)),
         ],
         out_specs=pl.BlockSpec((wide, tokens, columns), lambda i: (i, 0, 0)),
-        compiler_params=LIMIT,
+        compiler_params=WIDE,
         name="project",
     )(core_scalar, attended, gathered, weight_other)
     partial_sums = exchange(partial_value, "tensor")
     head_total = jnp.sum(partial_sums.astype(jnp.float32), axis=0)
     residual_share = lax.dynamic_slice_in_dim(residual, tensor_index * columns, columns, 1)
     hidden_share = residual_share.astype(jnp.float32) + head_total
-    hidden_share, first_own = lax.optimization_barrier((hidden_share, first_own))
     full_rows = spread(hidden_share.astype(jnp.bfloat16), "tensor")
-
-    first_other = lax.ppermute(first_own, "dp", SWAP)
-    depth = 512
-    steps = D // depth
-    weight_spec = pl.BlockSpec((expert_count, local_units, depth), lambda i: (0, 0, i))
+    full_rows, weights = lax.optimization_barrier((full_rows, weights))
+    weights = weights.reshape(2 * expert_count, blocks, local_units, columns)
+
+    parts = 2
+    per_part = expert_count // parts
+    per_step = 2
+
+    def first_spec(place):
+        return pl.BlockSpec((per_part, per_step, local_units, columns), lambda i: (place, i, 0, 0))
+
     activation = pl.pallas_call(
         gate_up,
         out_shape=jax.ShapeDtypeStruct((TOP * local_units, tokens), jnp.bfloat16),
-        grid=(steps,),
+        grid=(first_blocks // per_step,),
         in_specs=[
-            SCALAR,
             pl.BlockSpec((tensor_count, tokens, columns), lambda i: (0, 0, 0)),
             pl.BlockSpec((tensor_count, 1, columns), lambda i: (0, 0, 0)),
             pl.BlockSpec((TOP, tokens), lambda i: (0, 0)),
-            weight_spec,
-            weight_spec,
-        ],
+        ]
+        + [first_spec(place) for place in range(2 * parts)],
         out_specs=pl.BlockSpec((TOP * local_units, tokens), lambda i: (0, 0)),
         scratch_shapes=[
-            pltpu.VMEM((steps, tokens, depth), jnp.bfloat16),
+            pltpu.VMEM((first_blocks, tokens, columns), jnp.bfloat16),
             pltpu.VMEM((expert_count * local_units, tokens), jnp.float32),
             pltpu.VMEM((expert_count * local_units, tokens), jnp.float32),
         ],
         compiler_params=LIMIT,
         name="gate_up",
     )(
-        core_scalar,
         full_rows,
         post_gain.reshape(tensor_count, 1, columns),
         routes.T,
-        first_own,
-        first_other,
-    )
-    activation, down_own = lax.optimization_barrier((activation, down_own))
+        *[weights] * (2 * parts),
+    )
     activation = spread(activation, "tensor")
 
-    down_other = lax.ppermute(down_own, "dp", SWAP)
-    per_step = 2
-    weight_spec = pl.BlockSpec((per_step, half_units, columns), lambda i: (i, 0, 0))
+    per_part = 2
+    down_steps = expert_count // (parts * per_part)
+
+    def down_spec(half, part):
+        return pl.BlockSpec(
+            (per_part, down_blocks, local_units, columns),
+            lambda i: ((half * down_steps + i) * parts + part, first_blocks // down_blocks, 0, 0),
+        )
+
     return pl.pallas_call(
         down,
         out_shape=jax.ShapeDtypeStruct((tokens, columns), jnp.bfloat16),
-        grid=(expert_count // per_step,),
+        grid=(down_steps,),
         in_specs=[
-            SCALAR,
             pl.BlockSpec((tensor_count, TOP * local_units, tokens), lambda i: (0, 0, 0)),
             pl.BlockSpec((tokens, TOP), lambda i: (0, 0)),
             pl.BlockSpec((tokens, TOP), lambda i: (0, 0)),
             pl.BlockSpec((tokens, columns), lambda i: (0, 0)),
-            weight_spec,
-            weight_spec,
-        ],
+        ]
+        + [down_spec(half, part) for half in range(2) for part in range(parts)],
         out_specs=pl.BlockSpec((tokens, columns), lambda i: (0, 0)),
         scratch_shapes=[
             pltpu.VMEM((2, TOP, tokens, half_units), jnp.bfloat16),
@@ -323,7 +320,7 @@
         ],
         compiler_params=LIMIT,
         name="down",
-    )(core_scalar, activation, routes, route_weight, hidden_share, down_own, down_other)
+    )(activation, routes, route_weight, hidden_share, *[weights] * (2 * parts))
 
 
 def solution(mesh):

time: 296 us -> 294 us (level)
  local copies, waits for them, and re-layouts: 17 us -> 7.89 us
  blocking collectives: 112 us -> 119 us
  Pallas kernels: 23.9 us -> 28.5 us
  starting transfers between devices: 40.5 us -> 36 us
    ppermute x2 -> x0, starting transfers between devices: 14.9 us -> none  [the longest x1 7.61 us: local(): down_other = lax.ppermute(down_own, 'dp', SWAP)]
    unnamed x22 -> x17, local copies, waits for them, and re-layouts: 11.5 us -> 3.9 us
    all_to_all x2, starting transfers between devices: 20.7 us -> 27.5 us  [exchange(): lax.all_to_all(message, axis, split_axis=0, concat_axis=0, tiled=True)]
    all_to_all x2, blocking collectives: 112 us -> 119 us  [exchange(): lax.all_to_all(message, axis, split_axis=0, concat_axis=0, tiled=True)]
    ppermute x1, starting transfers between devices: 4.9 us -> 8.48 us  [local(): weight_other = lax.ppermute(weight_own, 'dp', SWAP)]
  transfers between devices with their start and end apart: 7 -> 4, of which waited for: 3 -> 3; matrix products, arithmetic and copies ran while one was open for 1% -> 1% of each run, Pallas kernels for 5% -> 3%
where the time goes in v4:
time: 294 us; the launch traced here: 289 us
  blocking collectives  119 us (40%)
  waiting for transfers between devices  80.7 us (27%)
  starting transfers between devices  36 us (12%)
  Pallas kernels  28.5 us (10%)
  between operations  13.5 us (5%)
  local copies, waits for them, and re-layouts  7.89 us (3%)
  other arithmetic  3.52 us (1%)
    all_to_all x2, blocking collectives, exchange(): lax.all_to_all(message, axis, split_axis=0, concat_axis=0, tiled=True)  119 us
    all_to_all x2, waiting for transfers between devices, exchange(): lax.all_to_all(message, axis, split_axis=0, concat_axis=0, tiled=True)  79.7 us
    all_to_all x2, starting transfers between devices, exchange(): lax.all_to_all(message, axis, split_axis=0, concat_axis=0, tiled=True)  27.5 us
    pallas_call x1, Pallas kernels, local(): pl.pallas_call(gate_up, out_shape=jax.ShapeDtypeStruct((TOP * local_units...  13.8 us
    ppermute x1, starting transfers between devices, local(): weight_other = lax.ppermute(weight_own, 'dp', SWAP)  8.48 us
    pallas_call x1, Pallas kernels, local(): pl.pallas_call(down, out_shape=jax.ShapeDtypeStruct((tokens, columns), jn...  7.16 us
  transfers between devices with their start and end apart: 4, of which 3 were waited for; matrix products, arithmetic and copies ran while one was open for 1% of the time, Pallas kernels for 3%

profile of v4, /device:TPU:1, one launch (start us, length us, event | category | flops | bytes accessed | tf_op | source)
XLA Modules:
  0.0 288.7 jit_solution(15368758134226415355)
XLA Ops:
  6.5 0.0 copy-start
  6.5 0.0 all-gather.3.cloned.1.call-start
  6.5 1.3 broadcast_select_fusion
  7.8 0.0 copy-start.5
  7.8 0.2 copy.19
  8.0 0.2 copy.16
  8.3 0.5 copy-done.5
  8.8 0.0 copy-done
  8.9 1.1 pad_maximum_fusion
  10.0 0.8 constant_dynamic-slice_fusion
  10.8 0.0 all-gather.3.cloned.1.call-update
  10.8 0.3 broadcast_in_dim.6
  11.1 60.9 %all_to_all.20.piece_ref.own_ref = bf16[16,384,256]{2,1,0:T(8,128)(2,1)S(1)} all-to-all(bf16[16,384,256]{2,1,0:T(8,128)(2,1)S(1)} %broadcast_in_dim.6), channel_id=1, replica_groups=mesh['dp'=2,'tensor'=16,'expert'=16] {'expert'}, dimensions={0} | all-to-all | bytes 6291456 | tf_op jit(solution)/shard_map/all_to_all | solution.py:164
  72.0 0.0 copy-start.3
  72.0 1.6 copy-done.3
  73.6 1.5 slice.4
  75.1 8.5 %collective-permute-start = (bf16[16,256,256]{2,1,0:T(8,128)(2,1)}, bf16[16,256,256]{2,1,0:T(8,128)(2,1)S(1)}, u32[]{:S(2)}, u32[]{:S(2)}) collective-permute-start(bf16[16,256,256]{2,1,0:T(8,128)(2,1)} %slice.4), channel_id=1, source_target_pairs={{0,256},{256,0},{1,257},{257,1},{2,258},{258,2},{3,259},{259,3},{4... | collective-permute-start | bytes 6291464 | tf_op jit(solution)/shard_map/ppermute | solution.py:219
  83.6 3.0 %attend.1.attended_ref = bf16[2,128,256]{2,1,0:T(8,128)(2,1)} custom-call(s32[1]{0:T(128)} %bitcast.1.place_ref, bf16[128,512]{1,0:T(8,128)(2,1)} %query_ref.1, bf16[16,384,256]{2,1,0:T(8,128)(2,1)} %copy-done.3), custom_call_target="tpu_custom_call" | custom-call | tf_op jit(solution)/shard_map/attend/pallas_call | solution.py:221
  86.6 1.0 collective-permute-done.other_ref
  87.6 0.0 copy-start.4
  87.6 1.4 copy-done.4
  89.0 4.5 %project.1 = bf16[16,128,256]{2,1,0:T(8,128)(2,1)} custom-call(s32[1]{0:T(128)} %bitcast.core_ref, bf16[2,128,256]{2,1,0:T(8,128)(2,1)} %attend.1.attended_ref, bf16[16,384,256]{2,1,0:T(8,128)(2,1)} %copy-done.3, bf16[16,256,256]{2,1,0:T(8,128)(2,1)} %copy-done.4), custom_call_target="tpu_custom_call" | custom-call | tf_op jit(solution)/shard_map/project/pallas_call | solution.py:241
  93.5 14.7 %all-to-all-start.1 = ((bf16[16,128,256]{2,1,0:T(8,128)(2,1)}), bf16[16,128,256]{2,1,0:T(8,128)(2,1)S(1)}, u32[]{:S(2)}, u32[]{:S(2)}) async-start(bf16[16,128,256]{2,1,0:T(8,128)(2,1)} %project.1), calls=%async_computation.1 | async-start | bytes 2097152 | tf_op jit(solution)/shard_map/all_to_all | solution.py:164
  108.3 45.5 %all-to-all-done.1 = bf16[16,128,256]{2,1,0:T(8,128)(2,1)S(1)} async-done(((bf16[16,128,256]{2,1,0:T(8,128)(2,1)}), bf16[16,128,256]{2,1,0:T(8,128)(2,1)S(1)}, u32[]{:S(2)}, u32[]{:S(2)}) %all-to-all-start.1) | async-done | bytes 1048608 | tf_op jit(solution)/shard_map/all_to_all | solution.py:164
  153.8 0.1 convert_reduce_fusion
  153.9 0.0 copy-start.1
  153.9 0.0 copy-start.2
  153.9 0.9 fusion
  154.9 0.1 broadcast_in_dim.7
  155.0 57.6 %all_to_all.21.rows_ref = bf16[16,128,256]{2,1,0:T(8,128)(2,1)S(1)} all-to-all(bf16[16,128,256]{2,1,0:T(8,128)(2,1)S(1)} %broadcast_in_dim.7), channel_id=1, replica_groups=mesh['dp'=2,'tensor'=16,'expert'=16] {'tensor'}, dimensions={0} | all-to-all | bytes 2097152 | tf_op jit(solution)/shard_map/all_to_all | solution.py:164
  212.6 0.0 all-gather.3.cloned.1.call-done
  212.6 0.0 copy-done.1
  212.6 0.0 copy-done.2
  212.6 13.8 %gate_up.1 = bf16[192,128]{1,0:T(8,128)(2,1)S(1)} custom-call(bf16[16,128,256]{2,1,0:T(8,128)(2,1)S(1)} %all_to_all.21.rows_ref, f32[16,1,256]{2,1,0:T(1,128)S(1)} %bitcast.16, s32[2,128]{1,0:T(2,128)S(1)} %bitcast.17, bf16[32,24,96,256]{3,2,1,0:T(8,128)(2,1)} %bitcast.18, bf16[32,24,96,256]{3,2,1,0:T(8,128)(2,1)} %bitcast.19, ...), custom_call_target="tpu_custom_call" | custom-call | tf_op jit(solution)/shard_map/gate_up/pallas_call | solution.py:270
  226.4 0.0 copy-start.6
  226.4 1.0 broadcast_in_dim.8
  227.5 12.8 %all-to-all-start.3 = ((bf16[16,192,128]{2,1,0:T(8,128)(2,1)}), bf16[16,192,128]{2,1,0:T(8,128)(2,1)S(1)}, u32[]{:S(2)}, u32[]{:S(2)}) async-start(bf16[16,192,128]{2,1,0:T(8,128)(2,1)} %broadcast_in_dim.8), calls=%async_computation.3 | async-start | bytes 1572864 | tf_op jit(solution)/shard_map/all_to_all | solution.py:164
  240.3 0.1 copy.17.routes_ref
  240.4 0.0 copy-done.6
  240.4 0.1 copy.18.route_weight_ref
  240.5 34.2 %all-to-all-done.3.activation_ref = bf16[16,192,128]{2,1,0:T(8,128)(2,1)S(1)} async-done(((bf16[16,192,128]{2,1,0:T(8,128)(2,1)}), bf16[16,192,128]{2,1,0:T(8,128)(2,1)S(1)}, u32[]{:S(2)}, u32[]{:S(2)}) %all-to-all-start.3) | async-done | bytes 786464 | tf_op jit(solution)/shard_map/all_to_all | solution.py:164
  274.7 7.2 %down.1 = bf16[128,256]{1,0:T(8,128)(2,1)} custom-call(bf16[16,192,128]{2,1,0:T(8,128)(2,1)S(1)} %all-to-all-done.3.activation_ref, s32[128,2]{1,0:T(8,128)S(1)} %copy.17.routes_ref, f32[128,2]{1,0:T(8,128)S(1)} %copy.18.route_weight_ref, f32[128,256]{1,0:T(8,128)S(1)} %get-tuple-element.14.hidden_ref, bf16[32,24,96,256]{3,2,1,0:T(8,128)(2,1)} %bitcast.22, ...), custom_call_target="tpu_custom_call" | custom-call | tf_op jit(solution)/shard_map/down/pallas_call | solution.py:305
  (3 shorter events, 0.1 us)
Async XLA Ops:
  6.5 2.3 copy-start
  6.5 206.0 %all-gather.3.cloned.1.call-start = ((), (), s32[]{:S(2)}) async-start(), calls=%async_computation.4 | async-start | bytes 38928384 | tf_op jit(solution)/shard_map/all_gather | solution.py:216
  7.8 1.0 copy-start.5
  72.0 1.6 copy-start.3
  75.1 12.5 %collective-permute-start = (bf16[16,256,256]{2,1,0:T(8,128)(2,1)}, bf16[16,256,256]{2,1,0:T(8,128)(2,1)S(1)}, u32[]{:S(2)}, u32[]{:S(2)}) collective-permute-start(bf16[16,256,256]{2,1,0:T(8,128)(2,1)} %slice.4), channel_id=1, source_target_pairs={{0,256},{256,0},{1,257},{257,1},{2,258},{258,2},{3,259},{259,3},{4... | collective-permute-start | bytes 6291464 | tf_op jit(solution)/shard_map/ppermute | solution.py:219
  87.6 1.4 copy-start.4
  93.5 60.3 %all-to-all-start.1 = ((bf16[16,128,256]{2,1,0:T(8,128)(2,1)}), bf16[16,128,256]{2,1,0:T(8,128)(2,1)S(1)}, u32[]{:S(2)}, u32[]{:S(2)}) async-start(bf16[16,128,256]{2,1,0:T(8,128)(2,1)} %project.1), calls=%async_computation.1 | async-start | bytes 2097152 | tf_op jit(solution)/shard_map/all_to_all | solution.py:164
  153.9 58.7 %copy-start.1 = (f32[4096]{0:T(1024)S(1)}, f32[4096]{0:T(1024)}, u32[]{:S(2)}) copy-start(f32[4096]{0:T(1024)} %param.16) | copy-start | bytes 49156
  153.9 58.7 %copy-start.2 = (s32[128,2]{0,1:T(2,128)S(1)}, s32[128,2]{0,1:T(2,128)}, u32[]{:S(2)}) copy-start(s32[128,2]{0,1:T(2,128)} %param.17) | copy-start | bytes 3076
  226.4 14.0 %copy-start.6 = (f32[128,2]{0,1:T(2,128)S(1)}, f32[128,2]{0,1:T(2,128)}, u32[]{:S(2)}) copy-start(f32[128,2]{0,1:T(2,128)} %param.18) | copy-start | bytes 3076
  227.5 47.3 %all-to-all-start.3 = ((bf16[16,192,128]{2,1,0:T(8,128)(2,1)}), bf16[16,192,128]{2,1,0:T(8,128)(2,1)S(1)}, u32[]{:S(2)}, u32[]{:S(2)}) async-start(bf16[16,192,128]{2,1,0:T(8,128)(2,1)} %broadcast_in_dim.8), calls=%async_computation.3 | async-start | bytes 1572864 | tf_op jit(solution)/shard_map/all_to_all | solution.py:164
Sparse Core Ops, SparseCore 0:
  10.9 164.7 all-gather.2

commit v5 on v4

--- a/solution.py
+++ b/solution.py
@@ -213,8 +213,9 @@
     weight_half = lax.dynamic_slice_in_dim(out_weight, core * half_rows, half_rows, 0)
     message = jnp.concatenate([weight_half, jnp.concatenate([key_head, value_head], axis=1)], axis=0)
     message, weights_here = lax.optimization_barrier((message, weights_here))
+    gathered = spread(message, "expert")
+    gathered, weights_here = lax.optimization_barrier((gathered, weights_here))
     weights = lax.all_gather(weights_here, ("dp", "expert"), axis=0)
-    gathered = spread(message, "expert")
     weight_own = gathered[:, :half_rows, :]
     weight_other = lax.ppermute(weight_own, "dp", SWAP)
 

time: 294 us -> 280 us (0.952)
  blocking collectives: 119 us -> 102 us
  waiting for transfers between devices: 80.7 us -> 87 us
  starting transfers between devices: 36 us -> 32.2 us
    all_to_all x2, blocking collectives: 119 us -> 102 us  [exchange(): lax.all_to_all(message, axis, split_axis=0, concat_axis=0, tiled=True)]
    all_gather x1, waiting for transfers between devices: 0.01 us -> 6.39 us  [local(): weights = lax.all_gather(weights_here, ('dp', 'expert'), axis=0)]
  transfers between devices with their start and end apart: 4 -> 4, of which waited for: 3 -> 4; matrix products, arithmetic and copies ran while one was open for 1% -> 2% of each run, Pallas kernels for 3% -> 3%
where the time goes in v5:
time: 280 us; the launch traced here: 275 us
  blocking collectives  102 us (36%)
  waiting for transfers between devices  87 us (31%)
  starting transfers between devices  32.2 us (12%)
  Pallas kernels  28.5 us (10%)
  between operations  13.5 us (5%)
  local copies, waits for them, and re-layouts  7.89 us (3%)
  other arithmetic  3.48 us (1%)
    all_to_all x2, blocking collectives, exchange(): lax.all_to_all(message, axis, split_axis=0, concat_axis=0, tiled=True)  102 us
    all_to_all x2, waiting for transfers between devices, exchange(): lax.all_to_all(message, axis, split_axis=0, concat_axis=0, tiled=True)  79.6 us
    all_to_all x2, starting transfers between devices, exchange(): lax.all_to_all(message, axis, split_axis=0, concat_axis=0, tiled=True)  26.7 us
    pallas_call x1, Pallas kernels, local(): pl.pallas_call(gate_up, out_shape=jax.ShapeDtypeStruct((TOP * local_units...  13.8 us
    pallas_call x1, Pallas kernels, local(): pl.pallas_call(down, out_shape=jax.ShapeDtypeStruct((tokens, columns), jn...  7.16 us
    all_gather x1, waiting for transfers between devices, local(): weights = lax.all_gather(weights_here, ('dp', 'expert'), axis=0)  6.39 us
  transfers between devices with their start and end apart: 4, of which 4 were waited for; matrix products, arithmetic and copies ran while one was open for 2% of the time, Pallas kernels for 3%

profile of v5, /device:TPU:1, one launch (start us, length us, event | category | flops | bytes accessed | tf_op | source)
XLA Modules:
  0.0 274.9 jit_solution(13984818847414705741)
XLA Ops:
  6.5 0.0 copy-start
  6.5 0.0 all-gather.3.cloned.1.call-start
  6.5 1.3 broadcast_select_fusion
  7.8 0.0 copy-start.4
  7.8 0.2 copy.19
  8.0 0.2 copy.16
  8.3 0.5 copy-done.4
  8.8 0.0 copy-done
  8.9 1.2 pad_maximum_fusion
  10.0 0.8 constant_dynamic-slice_fusion
  10.8 0.3 broadcast_in_dim.6
  11.1 44.7 %all_to_all.20.piece_ref.own_ref = bf16[16,384,256]{2,1,0:T(8,128)(2,1)} all-to-all(bf16[16,384,256]{2,1,0:T(8,128)(2,1)S(1)} %broadcast_in_dim.6), channel_id=1, replica_groups=mesh['dp'=2,'tensor'=16,'expert'=16] {'expert'}, dimensions={0} | all-to-all | bytes 6291456 | tf_op jit(solution)/shard_map/all_to_all | solution.py:164
  55.8 0.0 all-gather.3.cloned.1.call-update
  55.8 3.1 %slice.3 = bf16[16,256,256]{2,1,0:T(8,128)(2,1)} slice(bf16[16,384,256]{2,1,0:T(8,128)(2,1)} %all_to_all.20.piece_ref.own_ref), slice={[0:16], [0:256], [0:256]} | slice | bytes 4194304 | tf_op jit(solution)/shard_map/slice | solution.py:219
  58.9 5.6 %collective-permute-start = (bf16[16,256,256]{2,1,0:T(8,128)(2,1)}, bf16[16,256,256]{2,1,0:T(8,128)(2,1)S(1)}, u32[]{:S(2)}, u32[]{:S(2)}) collective-permute-start(bf16[16,256,256]{2,1,0:T(8,128)(2,1)} %slice.3), channel_id=1, source_target_pairs={{0,256},{256,0},{1,257},{257,1},{2,258},{258,2},{3,259},{259,3},{4... | collective-permute-start | bytes 6291464 | tf_op jit(solution)/shard_map/ppermute | solution.py:220
  64.5 3.0 %attend.1.attended_ref = bf16[2,128,256]{2,1,0:T(8,128)(2,1)} custom-call(s32[1]{0:T(128)} %bitcast.1.place_ref, bf16[128,512]{1,0:T(8,128)(2,1)} %query_ref.1, bf16[16,384,256]{2,1,0:T(8,128)(2,1)} %all_to_all.20.piece_ref.own_ref), custom_call_target="tpu_custom_call" | custom-call | tf_op jit(solution)/shard_map/attend/pallas_call | solution.py:222
  67.5 1.0 collective-permute-done.other_ref
  68.5 0.0 copy-start.3
  68.5 1.3 copy-done.3
  69.8 4.5 %project.1 = bf16[16,128,256]{2,1,0:T(8,128)(2,1)} custom-call(s32[1]{0:T(128)} %bitcast.core_ref, bf16[2,128,256]{2,1,0:T(8,128)(2,1)} %attend.1.attended_ref, bf16[16,384,256]{2,1,0:T(8,128)(2,1)} %all_to_all.20.piece_ref.own_ref, bf16[16,256,256]{2,1,0:T(8,128)(2,1)} %copy-done.3), custom_call_target="tpu_custom_call" | custom-call | tf_op jit(solution)/shard_map/project/pallas_call | solution.py:242
  74.3 14.7 %all-to-all-start.1 = ((bf16[16,128,256]{2,1,0:T(8,128)(2,1)}), bf16[16,128,256]{2,1,0:T(8,128)(2,1)S(1)}, u32[]{:S(2)}, u32[]{:S(2)}) async-start(bf16[16,128,256]{2,1,0:T(8,128)(2,1)} %project.1), calls=%async_computation.1 | async-start | bytes 2097152 | tf_op jit(solution)/shard_map/all_to_all | solution.py:164
  89.0 45.5 %all-to-all-done.1 = bf16[16,128,256]{2,1,0:T(8,128)(2,1)S(1)} async-done(((bf16[16,128,256]{2,1,0:T(8,128)(2,1)}), bf16[16,128,256]{2,1,0:T(8,128)(2,1)S(1)}, u32[]{:S(2)}, u32[]{:S(2)}) %all-to-all-start.1) | async-done | bytes 1048608 | tf_op jit(solution)/shard_map/all_to_all | solution.py:164
  134.5 0.1 convert_reduce_fusion
  134.7 0.0 copy-start.1
  134.7 0.0 copy-start.2
  134.7 0.9 fusion
  135.6 0.1 broadcast_in_dim.7
  135.7 57.6 %all_to_all.21.rows_ref = bf16[16,128,256]{2,1,0:T(8,128)(2,1)S(1)} all-to-all(bf16[16,128,256]{2,1,0:T(8,128)(2,1)S(1)} %broadcast_in_dim.7), channel_id=1, replica_groups=mesh['dp'=2,'tensor'=16,'expert'=16] {'tensor'}, dimensions={0} | all-to-all | bytes 2097152 | tf_op jit(solution)/shard_map/all_to_all | solution.py:164
  193.3 6.4 %all-gather.3.cloned.1.call-done = bf16[73728,256]{1,0:T(8,128)(2,1)} async-done(((bf16[2304,256]{1,0:T(8,128)(2,1)}), bf16[73728,256]{1,0:T(8,128)(2,1)}) %all-gather.3.cloned.1.call-update) | async-done | bytes 37748752 | tf_op jit(solution)/shard_map/all_gather | solution.py:218
  199.7 0.0 copy-done.1
  199.7 0.0 copy-done.2
  199.7 13.8 %gate_up.1 = bf16[192,128]{1,0:T(8,128)(2,1)S(1)} custom-call(bf16[16,128,256]{2,1,0:T(8,128)(2,1)S(1)} %all_to_all.21.rows_ref, f32[16,1,256]{2,1,0:T(1,128)S(1)} %bitcast.16, s32[2,128]{1,0:T(2,128)S(1)} %bitcast.17, bf16[32,24,96,256]{3,2,1,0:T(8,128)(2,1)} %bitcast.18, bf16[32,24,96,256]{3,2,1,0:T(8,128)(2,1)} %bitcast.19, ...), custom_call_target="tpu_custom_call" | custom-call | tf_op jit(solution)/shard_map/gate_up/pallas_call | solution.py:271
  213.5 0.0 copy-start.5
  213.6 1.0 broadcast_in_dim.8
  214.6 12.0 %all-to-all-start.3 = ((bf16[16,192,128]{2,1,0:T(8,128)(2,1)}), bf16[16,192,128]{2,1,0:T(8,128)(2,1)S(1)}, u32[]{:S(2)}, u32[]{:S(2)}) async-start(bf16[16,192,128]{2,1,0:T(8,128)(2,1)} %broadcast_in_dim.8), calls=%async_computation.3 | async-start | bytes 1572864 | tf_op jit(solution)/shard_map/all_to_all | solution.py:164
  226.6 0.1 copy.17.routes_ref
  226.7 0.0 copy-done.5
  226.7 0.1 copy.18.route_weight_ref
  226.8 34.1 %all-to-all-done.3.activation_ref = bf16[16,192,128]{2,1,0:T(8,128)(2,1)S(1)} async-done(((bf16[16,192,128]{2,1,0:T(8,128)(2,1)}), bf16[16,192,128]{2,1,0:T(8,128)(2,1)S(1)}, u32[]{:S(2)}, u32[]{:S(2)}) %all-to-all-start.3) | async-done | bytes 786464 | tf_op jit(solution)/shard_map/all_to_all | solution.py:164
  260.9 7.2 %down.1 = bf16[128,256]{1,0:T(8,128)(2,1)} custom-call(bf16[16,192,128]{2,1,0:T(8,128)(2,1)S(1)} %all-to-all-done.3.activation_ref, s32[128,2]{1,0:T(8,128)S(1)} %copy.17.routes_ref, f32[128,2]{1,0:T(8,128)S(1)} %copy.18.route_weight_ref, f32[128,256]{1,0:T(8,128)S(1)} %get-tuple-element.18.hidden_ref, bf16[32,24,96,256]{3,2,1,0:T(8,128)(2,1)} %bitcast.22, ...), custom_call_target="tpu_custom_call" | custom-call | tf_op jit(solution)/shard_map/down/pallas_call | solution.py:306
  (3 shorter events, 0.1 us)
Async XLA Ops:
  6.5 2.3 copy-start
  6.5 193.2 %all-gather.3.cloned.1.call-start = ((), (), s32[]{:S(2)}) async-start(), calls=%async_computation.4 | async-start | bytes 38928384 | tf_op jit(solution)/shard_map/all_gather | solution.py:218
  7.8 1.0 copy-start.4
  58.9 9.5 %collective-permute-start = (bf16[16,256,256]{2,1,0:T(8,128)(2,1)}, bf16[16,256,256]{2,1,0:T(8,128)(2,1)S(1)}, u32[]{:S(2)}, u32[]{:S(2)}) collective-permute-start(bf16[16,256,256]{2,1,0:T(8,128)(2,1)} %slice.3), channel_id=1, source_target_pairs={{0,256},{256,0},{1,257},{257,1},{2,258},{258,2},{3,259},{259,3},{4... | collective-permute-start | bytes 6291464 | tf_op jit(solution)/shard_map/ppermute | solution.py:220
  68.5 1.3 copy-start.3
  74.3 60.2 %all-to-all-start.1 = ((bf16[16,128,256]{2,1,0:T(8,128)(2,1)}), bf16[16,128,256]{2,1,0:T(8,128)(2,1)S(1)}, u32[]{:S(2)}, u32[]{:S(2)}) async-start(bf16[16,128,256]{2,1,0:T(8,128)(2,1)} %project.1), calls=%async_computation.1 | async-start | bytes 2097152 | tf_op jit(solution)/shard_map/all_to_all | solution.py:164
  134.7 65.0 %copy-start.1 = (f32[4096]{0:T(1024)S(1)}, f32[4096]{0:T(1024)}, u32[]{:S(2)}) copy-start(f32[4096]{0:T(1024)} %param.16) | copy-start | bytes 49156
  134.7 65.0 %copy-start.2 = (s32[128,2]{0,1:T(2,128)S(1)}, s32[128,2]{0,1:T(2,128)}, u32[]{:S(2)}) copy-start(s32[128,2]{0,1:T(2,128)} %param.17) | copy-start | bytes 3076
  213.5 13.2 %copy-start.5 = (f32[128,2]{0,1:T(2,128)S(1)}, f32[128,2]{0,1:T(2,128)}, u32[]{:S(2)}) copy-start(f32[128,2]{0,1:T(2,128)} %param.18) | copy-start | bytes 3076
  214.6 46.3 %all-to-all-start.3 = ((bf16[16,192,128]{2,1,0:T(8,128)(2,1)}), bf16[16,192,128]{2,1,0:T(8,128)(2,1)S(1)}, u32[]{:S(2)}, u32[]{:S(2)}) async-start(bf16[16,192,128]{2,1,0:T(8,128)(2,1)} %broadcast_in_dim.8), calls=%async_computation.3 | async-start | bytes 1572864 | tf_op jit(solution)/shard_map/all_to_all | solution.py:164
Sparse Core Ops, SparseCore 0:
  55.9 143.7 all-gather.2

commit v6 on v4

v6 whole, which is shorter than its diff:
```python
import functools

import jax
import jax.numpy as jnp
from jax import lax
from jax.experimental import pallas as pl
from jax.experimental.pallas import tpu as pltpu
from jax.sharding import PartitionSpec as P

D = 4096
QUERY_HEADS = 64
KEY_VALUE_HEADS = 4
HEAD_WIDTH = 128
TOP = 2
PAIRS = 8
SWAP = [(0, 1), (1, 0)]
NEIGHBOUR = [(i, i ^ 1) for i in range(2 * PAIRS)]
PARITY = [[2 * pair + odd for pair in range(PAIRS)] for odd in range(2)]
CHUNK = 512


CONTRACT_LAST = (((1,), (1,)), ((), ()))


def attend(place_ref, query_ref, piece_ref, out_ref, score_ref):
    tokens = query_ref.shape[0]
    heads = query_ref.shape[1] // HEAD_WIDTH
    rows = heads * tokens
    blocks = CHUNK // tokens
    place = place_ref[0]
    stacked = jnp.concatenate(
        [query_ref[:, HEAD_WIDTH * h : HEAD_WIDTH * (h + 1)] for h in range(heads)], axis=0
    )
    token = place * tokens + lax.broadcasted_iota(jnp.int32, (rows, CHUNK), 0) % tokens
    offset = token - lax.broadcasted_iota(jnp.int32, (rows, CHUNK), 1)

    def score(step, row_max):
        keys = piece_ref[pl.ds(step * blocks, blocks), :, :HEAD_WIDTH].reshape(CHUNK, HEAD_WIDTH)
        scores = lax.dot_general(
            stacked, keys, CONTRACT_LAST, preferred_element_type=jnp.float32
        ) * HEAD_WIDTH ** (-0.5)
        masked = jnp.where(offset >= step * CHUNK, scores, -1e30)
        score_ref[step] = masked
        return jnp.maximum(row_max, jnp.max(masked, axis=1, keepdims=True))

    def weigh(step, carry):
        total, summed = carry
        exponent = jnp.exp(score_ref[step] - row_max)
        values = piece_ref[pl.ds(step * blocks, blocks), :, HEAD_WIDTH:].reshape(CHUNK, HEAD_WIDTH)
        return (
            total + jnp.sum(exponent, axis=1, keepdims=True),
            summed
            + jnp.dot(exponent.astype(jnp.bfloat16), values, preferred_element_type=jnp.float32),
        )

    steps = place // blocks + 1
    row_max = lax.fori_loop(0, steps, score, jnp.full((rows, 1), -1e30, jnp.float32))
    total, summed = lax.fori_loop(
        0,
        steps,
        weigh,
        (jnp.zeros((rows, 1), jnp.float32), jnp.zeros((rows, HEAD_WIDTH), jnp.float32)),
    )
    attended = (summed / total).astype(out_ref.dtype)
    halves = heads // 2
    for h in range(heads):
        out_ref[h // halves, :, HEAD_WIDTH * (h % halves) : HEAD_WIDTH * (h % halves + 1)] = (
            attended[tokens * h : tokens * (h + 1)]
        )


def project(scalar_ref, attended_ref, own_ref, other_ref, out_ref):
    core = scalar_ref[0]
    for block in range(own_ref.shape[0]):
        out_ref[block] = (
            jnp.dot(attended_ref[core], own_ref[block, 0], preferred_element_type=jnp.float32)
            + jnp.dot(
                attended_ref[1 - core], other_ref[block, 0], preferred_element_type=jnp.float32
            )
        ).astype(out_ref.dtype)


def gate_up(last, parts, scalar_ref, rows_ref, gain_ref, *refs):
    gate_refs, up_refs, refs = refs[:parts], refs[parts : 2 * parts], refs[2 * parts :]
    if last:
        before, before_square, routes_ref, out_ref, scaled, totals, square = refs
    else:
        totals, square, scaled = refs
    step = pl.program_id(0)
    experts, per_step, _, units, columns = gate_refs[0].shape
    pieces, tokens, _ = rows_ref.shape

    @pl.when(step == 0)
    def _():
        if last:
            square[...] = before_square[...]
            totals[...] = before[...]
        else:
            square[...] = jnp.zeros_like(square)
            totals[...] = jnp.zeros_like(totals)
        for piece in range(pieces):
            rows = rows_ref[piece].astype(jnp.float32)
            square[...] += jnp.sum(rows * rows, axis=1, keepdims=True)
            scaled[piece] = (rows * gain_ref[piece, scalar_ref[0]]).astype(jnp.bfloat16)

    for which, weight_refs in enumerate((gate_refs, up_refs)):
        for part, weight_ref in enumerate(weight_refs):
            place = pl.ds(part * experts * units, experts * units)
            product = totals[which, place]
            for piece in range(per_step):
                product += lax.dot_general(
                    weight_ref[:, piece, 0].reshape(experts * units, columns),
                    scaled[step * per_step + piece],
                    CONTRACT_LAST,
                    preferred_element_type=jnp.float32,
                )
            totals[which, place] = product

    if last:

        @pl.when(step == pl.num_programs(0) - 1)
        def _():
            scale = lax.rsqrt(square[...] / D + 1e-06)
            scale = jnp.transpose(jnp.broadcast_to(scale, (tokens, tokens)))[:1]
            chosen = [jnp.zeros((units, tokens), jnp.float32) for _ in range(TOP)]
            for expert in range(parts * experts):
                gate_values = totals[0, expert * units : (expert + 1) * units] * scale
                up_values = totals[1, expert * units : (expert + 1) * units] * scale
                activation = gate_values / (1.0 + jnp.exp(-gate_values)) * up_values
                for k in range(TOP):
                    chosen[k] = jnp.where(routes_ref[k : k + 1] == expert, activation, chosen[k])
            for k in range(TOP):
                out_ref[k * units : (k + 1) * units] = chosen[k].astype(out_ref.dtype)


def down(parts, scalar_ref, activation_ref, routes_ref, route_weight_ref, start_ref, *refs):
    half_refs = refs[:parts], refs[parts : 2 * parts]
    out_ref, turned, mixed = refs[2 * parts :]
    step = pl.program_id(0)
    per_part, blocks, _, units, columns = refs[0].shape

    @pl.when(step == 0)
    def _():
        for half in range(2):
            for k in range(TOP):
                part = activation_ref[blocks * half : blocks * (half + 1), k * units : (k + 1) * units]
                part = part.reshape(blocks * units, part.shape[2]).astype(jnp.float32)
                turned[half, k] = jnp.transpose(part).astype(turned.dtype)
        mixed[...] = start_ref[...]

    for part in range(parts):
        for place in range(per_part):
            expert = (step * parts + part) * per_part + place
            here = [routes_ref[:, k : k + 1] == expert for k in range(TOP)]
            share = sum(jnp.where(here[k], route_weight_ref[:, k : k + 1], 0.0) for k in range(TOP))
            masks = [here[k].astype(jnp.bfloat16) for k in range(TOP)]
            total = jnp.zeros(mixed.shape, jnp.float32)
            for half in range(2):
                rows = sum(turned[half, k] * masks[k] for k in range(TOP))
                weight = half_refs[half][part][place].reshape(blocks * units, columns)
                total += jnp.dot(rows, weight, preferred_element_type=jnp.float32)
            mixed[...] += total * share

    @pl.when(step == pl.num_programs(0) - 1)
    def _():
        out_ref[...] = mixed[...].astype(out_ref.dtype)


SCALAR = pl.BlockSpec(memory_space=pltpu.SMEM)
LIMIT = pltpu.CompilerParams(vmem_limit_bytes=32 * 1024 * 1024)
WIDE = pltpu.CompilerParams(vmem_limit_bytes=56 * 1024 * 1024)


def whole(*shape):
    return pl.BlockSpec(shape, lambda i, scalar_ref: (0,) * len(shape))


def cost(flops, size):
    return pl.CostEstimate(flops=flops, bytes_accessed=size, transcendentals=0)


def exchange(message, axis, groups=None):
    return lax.all_to_all(
        message, axis, split_axis=0, concat_axis=0, tiled=True, axis_index_groups=groups
    )


def spread(rows, axis, count, groups=None):
    return exchange(jnp.broadcast_to(rows[None], (count,) + rows.shape), axis, groups)


def local(
    queries,
    all_key_rows,
    all_value_rows,
    out_weight,
    residual,
    post_gain,
    routes,
    route_weight,
    gate_weight,
    up_weight,
    down_weight,
):
    tokens = queries.shape[0]
    local_heads = queries.shape[1] // HEAD_WIDTH
    group_width = QUERY_HEADS // KEY_VALUE_HEADS
    tensor_count = lax.axis_size("tensor")
    expert_count = lax.axis_size("expert")
    tensor_index = lax.axis_index("tensor")
    expert_index = lax.axis_index("expert")
    core = lax.axis_index("dp")
    columns = D // tensor_count
    odd = (tensor_index % 2).astype(jnp.int32)
    core = core.astype(jnp.int32)
    hidden_units = down_weight.shape[1]
    half_units = hidden_units // 2
    local_units = gate_weight.shape[2]

    first_blocks = D // columns
    down_blocks = half_units // local_units
    blocks = first_blocks + down_blocks

    gate_or_up = jnp.where(core == 0, gate_weight[0], up_weight[0]).T
    gate_or_up = jnp.transpose(gate_or_up.reshape(local_units, first_blocks, columns), (1, 0, 2))
    down_half = lax.dynamic_slice_in_dim(down_weight[0], core * half_units, half_units, 0)
    weights_here = jnp.concatenate(
        [gate_or_up.reshape(first_blocks * local_units, columns), down_half], axis=0
    )

    shared = tensor_index * local_heads // group_width
    key_head = lax.dynamic_slice_in_dim(all_key_rows, shared * HEAD_WIDTH, HEAD_WIDTH, 1)
    value_head = lax.dynamic_slice_in_dim(all_value_rows, shared * HEAD_WIDTH, HEAD_WIDTH, 1)
    half_rows = out_weight.shape[0] // 2
    weight_half = lax.dynamic_slice_in_dim(out_weight, core * half_rows, half_rows, 0)
    message = jnp.concatenate([weight_half, jnp.concatenate([key_head, value_head], axis=1)], axis=0)
    message, weights_here = lax.optimization_barrier((message, weights_here))
    weights = lax.all_gather(weights_here, ("dp", "expert"), axis=0)
    gathered = spread(message, "expert", expert_count)
    gathered_other = lax.ppermute(gathered, "dp", SWAP)

    attended = pl.pallas_call(
        attend,
        out_shape=jax.ShapeDtypeStruct((2, tokens, half_rows), jnp.bfloat16),
        grid=(1,),
        in_specs=[
            SCALAR,
            pl.BlockSpec((tokens, local_heads * HEAD_WIDTH), lambda i: (0, 0)),
            pl.BlockSpec(
                (expert_count, tokens, 2 * HEAD_WIDTH), lambda i: (0, half_rows // tokens, 0)
            ),
        ],
        out_specs=pl.BlockSpec((2, tokens, half_rows), lambda i: (0, 0, 0)),
        scratch_shapes=[
            pltpu.VMEM((expert_count * tokens // CHUNK, local_heads * tokens, CHUNK), jnp.float32)
        ],
        compiler_params=WIDE,
        name="attend",
    )(expert_index.astype(jnp.int32).reshape(1), queries, gathered)

    message_rows = message.shape[0]
    pair_shape = (PAIRS, 2, message_rows, columns)
    gathered, gathered_other = gathered.reshape(pair_shape), gathered_other.reshape(pair_shape)
    wide = 4

    def projected(parity, dtype):
        weight_spec = pl.BlockSpec(
            (wide, 1, half_rows, columns), lambda i, scalar_ref: (i, scalar_ref[1], 0, 0)
        )
        return pl.pallas_call(
            project,
            out_shape=jax.ShapeDtypeStruct((PAIRS, tokens, columns), dtype),
            grid_spec=pltpu.PrefetchScalarGridSpec(
                num_scalar_prefetch=1,
                grid=(PAIRS // wide,),
                in_specs=[whole(2, tokens, half_rows), weight_spec, weight_spec],
                out_specs=pl.BlockSpec((wide, tokens, columns), lambda i, scalar_ref: (i, 0, 0)),
            ),
            compiler_params=WIDE,
            cost_estimate=cost(4 * tokens * half_rows * PAIRS * columns, 4 * half_rows * PAIRS * columns),
            name="project",
        )(jnp.stack([core, parity]), attended, gathered, gathered_other)

    given = lax.ppermute(projected(1 - odd, jnp.bfloat16), "tensor", NEIGHBOUR)
    kept = projected(odd, jnp.float32)
    pair_sums = (kept + given.astype(jnp.float32)).astype(jnp.bfloat16)
    partial_sums = exchange(pair_sums, "tensor", PARITY)
    head_total = jnp.sum(partial_sums.astype(jnp.float32), axis=0)
    residual_share = lax.dynamic_slice_in_dim(residual, tensor_index * columns, columns, 1)
    hidden_share = residual_share.astype(jnp.float32) + head_total
    rows_own = spread(hidden_share.astype(jnp.bfloat16), "tensor", PAIRS, PARITY)
    rows_own, weights = lax.optimization_barrier((rows_own, weights))
    rows_other = lax.ppermute(rows_own, "tensor", NEIGHBOUR)
    weights = weights.reshape(2 * expert_count, blocks // 2, 2, local_units, columns)

    parts = 2
    per_part = expert_count // parts
    per_step = 2
    gains = post_gain.reshape(PAIRS, 2, 1, columns)
    totals_shape = (2, expert_count * local_units, tokens)

    def first_spec(place):
        return pl.BlockSpec(
            (per_part, per_step, 1, local_units, columns),
            lambda i, scalar_ref: (place, i, scalar_ref[0], 0, 0),
        )

    def gated(parity, rows, *before):
        last = bool(before)
        totals_spec = [whole(*totals_shape), whole(tokens, 1)]
        totals_types = [
            jax.ShapeDtypeStruct(totals_shape, jnp.float32),
            jax.ShapeDtypeStruct((tokens, 1), jnp.float32),
        ]
        scaled = [pltpu.VMEM((PAIRS, tokens, columns), jnp.bfloat16)]
        totals_scratch = [pltpu.VMEM(kind.shape, kind.dtype) for kind in totals_types]
        out = (TOP * local_units, tokens)
        return pl.pallas_call(
            functools.partial(gate_up, last, parts),
            out_shape=jax.ShapeDtypeStruct(out, jnp.bfloat16) if last else totals_types,
            grid_spec=pltpu.PrefetchScalarGridSpec(
                num_scalar_prefetch=1,
                grid=(PAIRS // per_step,),
                in_specs=[whole(PAIRS, tokens, columns), whole(PAIRS, 2, 1, columns)]
                + [first_spec(place) for place in range(2 * parts)]
                + (totals_spec + [whole(TOP, tokens)] if last else []),
                out_specs=whole(*out) if last else totals_spec,
                scratch_shapes=scaled + totals_scratch if last else scaled,
            ),
            compiler_params=LIMIT,
            cost_estimate=cost(
                2 * tokens * 2 * expert_count * local_units * D // 2,
                2 * 2 * expert_count * local_units * D // 2,
            ),
            name="gate_up",
        )(parity.reshape(1), rows, gains, *[weights] * (2 * parts), *before)

    before = gated(odd, rows_own)
    activation = gated(1 - odd, rows_other, *before, routes.T)

    activation_own = spread(activation, "tensor", PAIRS, PARITY)
    activation_other = lax.ppermute(activation_own, "tensor", NEIGHBOUR)
    per_part = 2
    down_steps = expert_count // (parts * per_part)
    quarter = PAIRS // 2

    def down_spec(half, part):
        return pl.BlockSpec(
            (per_part, quarter, 1, local_units, columns),
            lambda i, scalar_ref: (
                (half * down_steps + i) * parts + part,
                first_blocks // (2 * quarter),
                scalar_ref[0],
                0,
                0,
            ),
        )

    def lowered(parity, rows, start, dtype):
        return pl.pallas_call(
            functools.partial(down, parts),
            out_shape=jax.ShapeDtypeStruct((tokens, columns), dtype),
            grid_spec=pltpu.PrefetchScalarGridSpec(
                num_scalar_prefetch=1,
                grid=(down_steps,),
                in_specs=[
                    whole(PAIRS, TOP * local_units, tokens),
                    whole(tokens, TOP),
                    whole(tokens, TOP),
                    whole(tokens, columns),
                ]
                + [down_spec(half, part) for half in range(2) for part in range(parts)],
                out_specs=whole(tokens, columns),
                scratch_shapes=[
                    pltpu.VMEM((2, TOP, tokens, quarter * local_units), jnp.bfloat16),
                    pltpu.VMEM((tokens, columns), jnp.float32),
                ],
            ),
            compiler_params=LIMIT,
            cost_estimate=cost(
                2 * tokens * expert_count * hidden_units * columns // 2,
                2 * expert_count * hidden_units * columns // 2,
            ),
            name="down",
        )(parity.reshape(1), rows, routes, route_weight, start, *[weights] * (2 * parts))

    mixed = lowered(odd, activation_own, hidden_share, jnp.float32)
    return lowered(1 - odd, activation_other, mixed, jnp.bfloat16)


def solution(mesh):
    return jax.shard_map(
        local,
        mesh=mesh,
        in_specs=(
            P(("dp", "expert"), "tensor"),
            P(("dp", "expert"), None),
            P(("dp", "expert"), None),
            P("tensor", "expert"),
            P(("dp", "expert"), None),
            P(),
            P(("dp", "expert"), None),
            P(("dp", "expert"), None),
            P("expert", None, "tensor"),
            P("expert", None, "tensor"),
            P("expert", None, "tensor"),
        ),
        out_specs=P(("dp", "expert"), "tensor"),
        check_vma=False,
    )
```

time: 294 us -> 263 us (0.89)
  waiting for transfers between devices: 80.7 us -> 36.6 us
  starting transfers between devices: 36 us -> 43.7 us
  Pallas kernels: 28.5 us -> 35.5 us
  local copies, waits for them, and re-layouts: 7.89 us -> 1.88 us
  other arithmetic: 3.52 us -> 6.82 us
    all_to_all x2 -> x1, waiting for transfers between devices: 79.7 us -> 25.7 us  [exchange(): lax.all_to_all(message, axis, split_axis=0, concat_axis=0, tiled=True, ax...]
    ppermute x1 -> x4, starting transfers between devices: 8.48 us -> 29 us  [the longest x1 10.4 us: local(): gathered_other = lax.ppermute(gathered, 'dp', SWAP)]
    all_to_all x2 -> x1, starting transfers between devices: 27.5 us -> 14.7 us  [exchange(): lax.all_to_all(message, axis, split_axis=0, concat_axis=0, tiled=True, ax...]
    ppermute x1 -> x4, waiting for transfers between devices: 0.99 us -> 10.9 us  [the longest x1 7.35 us: local(): given = lax.ppermute(projected(1 - odd, jnp.bfloat16), 'tensor', NEIGHBOUR)]
    pallas_call x3 -> x6, Pallas kernels: 25.5 us -> 32.5 us  [the longest x2 15 us: gated(): pl.pallas_call(functools.partial(gate_up, last, parts), out_shape=jax.Sha...]
    unnamed x17 -> x13, local copies, waits for them, and re-layouts: 3.9 us -> 0.42 us
    all_to_all x2 -> x3, blocking collectives: 119 us -> 121 us  [exchange(): lax.all_to_all(message, axis, split_axis=0, concat_axis=0, tiled=True, ax...]
  transfers between devices with their start and end apart: 4 -> 6, of which waited for: 3 -> 5; matrix products, arithmetic and copies ran while one was open for 1% -> 2% of each run, Pallas kernels for 3% -> 9%
where the time goes in v6:
time: 263 us; the launch traced here: 259 us
  blocking collectives  121 us (46%)
  starting transfers between devices  43.7 us (17%)
  waiting for transfers between devices  36.6 us (14%)
  Pallas kernels  35.5 us (13%)
  between operations  13.6 us (5%)
  other arithmetic  6.82 us (3%)
    all_to_all x3, blocking collectives, exchange(): lax.all_to_all(message, axis, split_axis=0, concat_axis=0, tiled=True, ax...  121 us
    all_to_all x1, waiting for transfers between devices, exchange(): lax.all_to_all(message, axis, split_axis=0, concat_axis=0, tiled=True, ax...  25.7 us
    pallas_call x2, Pallas kernels, gated(): pl.pallas_call(functools.partial(gate_up, last, parts), out_shape=jax.Sha...  15 us
    all_to_all x1, starting transfers between devices, exchange(): lax.all_to_all(message, axis, split_axis=0, concat_axis=0, tiled=True, ax...  14.7 us
    ppermute x1, starting transfers between devices, local(): gathered_other = lax.ppermute(gathered, 'dp', SWAP)  10.4 us
    pallas_call x2, Pallas kernels, lowered(): pl.pallas_call(functools.partial(down, parts), out_shape=jax.ShapeDtypeSt...  10.2 us
    ppermute x1, starting transfers between devices, local(): rows_other = lax.ppermute(rows_own, 'tensor', NEIGHBOUR)  8.83 us
    ppermute x1, waiting for transfers between devices, local(): given = lax.ppermute(projected(1 - odd, jnp.bfloat16), 'tensor', NEIGHBOUR)  7.35 us
  transfers between devices with their start and end apart: 6, of which 5 were waited for; matrix products, arithmetic and copies ran while one was open for 2% of the time, Pallas kernels for 9%

profile of v6, /device:TPU:1, one launch (start us, length us, event | category | flops | bytes accessed | tf_op | source)
XLA Modules:
  0.0 258.6 jit_solution(10052083010401361013)
XLA Ops:
  6.5 0.0 copy-start
  6.5 0.0 all-gather.3.cloned.1.call-start
  6.5 0.0 copy-start.3
  6.5 1.3 broadcast_select_fusion
  7.9 0.2 copy.25
  8.0 0.2 copy.20
  8.3 0.0 copy-done.3
  8.3 0.0 copy-done
  8.4 1.1 pad_maximum_fusion
  9.4 0.8 constant_dynamic-slice_fusion
  10.3 0.0 all-gather.3.cloned.1.call-update
  10.3 0.3 broadcast_in_dim.6
  10.6 58.6 %all_to_all.20.piece_ref = bf16[16,384,256]{2,1,0:T(8,128)(2,1)} all-to-all(bf16[16,384,256]{2,1,0:T(8,128)(2,1)S(1)} %broadcast_in_dim.6), channel_id=1, replica_groups=mesh['dp'=2,'tensor'=16,'expert'=16] {'expert'}, dimensions={0} | all-to-all | bytes 6291456 | tf_op jit(solution)/shard_map/all_to_all | solution.py:183
  69.2 10.4 %collective-permute-start = (bf16[16,384,256]{2,1,0:T(8,128)(2,1)}, bf16[16,384,256]{2,1,0:T(8,128)(2,1)}, u32[]{:S(2)}, u32[]{:S(2)}) collective-permute-start(bf16[16,384,256]{2,1,0:T(8,128)(2,1)} %all_to_all.20.piece_ref), channel_id=1, source_target_pairs={{0,256},{256,0},{1,257},{257,1},{2,258},{258,2},{3,259},{259,3},{4... | collective-permute-start | bytes 9437192 | tf_op jit(solution)/shard_map/ppermute | solution.py:240
  79.7 0.7 pad_add_fusion.1.scalar_ref
  80.3 3.0 %attend.1.attended_ref = bf16[2,128,256]{2,1,0:T(8,128)(2,1)} custom-call(s32[1]{0:T(128)} %bitcast.3.place_ref, bf16[128,512]{1,0:T(8,128)(2,1)} %query_ref.1, bf16[16,384,256]{2,1,0:T(8,128)(2,1)} %all_to_all.20.piece_ref), custom_call_target="tpu_custom_call" | custom-call | tf_op jit(solution)/shard_map/attend/pallas_call | solution.py:242
  83.3 1.9 collective-permute-done
  85.3 3.3 %project.3 = bf16[8,128,256]{2,1,0:T(8,128)(2,1)} custom-call(s32[2]{0:T(128)} %pad_add_fusion.1.scalar_ref, bf16[2,128,256]{2,1,0:T(8,128)(2,1)} %attend.1.attended_ref, bf16[8,2,384,256]{3,2,1,0:T(8,128)(2,1)} %bitcast.9.own_ref, bf16[8,2,384,256]{3,2,1,0:T(8,128)(2,1)} %bitcast.10.other_ref), custom_call_target="tpu_custom_call" | custom-call | flops 268435456 | bytes 2097152 | tf_op jit(solution)/shard_map/project/pallas_call | solution.py:270
  88.5 3.4 %collective-permute-start.1 = (bf16[8,128,256]{2,1,0:T(8,128)(2,1)}, bf16[8,128,256]{2,1,0:T(8,128)(2,1)S(1)}, u32[]{:S(2)}, u32[]{:S(2)}) collective-permute-start(bf16[8,128,256]{2,1,0:T(8,128)(2,1)} %project.3), channel_id=1, source_target_pairs={{0,16},{16,0},{32,48},{48,32},{64,80},{80,64},{96,112},{112,96},{1... | collective-permute-start | bytes 1572872 | tf_op jit(solution)/shard_map/ppermute | solution.py:284
  91.9 0.7 pad_add_fusion.scalar_ref
  92.6 4.0 %project.2 = f32[8,128,256]{2,1,0:T(8,128)} custom-call(s32[2]{0:T(128)} %pad_add_fusion.scalar_ref, bf16[2,128,256]{2,1,0:T(8,128)(2,1)} %attend.1.attended_ref, bf16[8,2,384,256]{3,2,1,0:T(8,128)(2,1)} %bitcast.9.own_ref, bf16[8,2,384,256]{3,2,1,0:T(8,128)(2,1)} %bitcast.10.other_ref), custom_call_target="tpu_custom_call" | custom-call | flops 268435456 | bytes 2097152 | tf_op jit(solution)/shard_map/project/pallas_call | solution.py:270
  96.6 7.3 %collective-permute-done.1 = bf16[8,128,256]{2,1,0:T(8,128)(2,1)S(1)} collective-permute-done((bf16[8,128,256]{2,1,0:T(8,128)(2,1)}, bf16[8,128,256]{2,1,0:T(8,128)(2,1)S(1)}, u32[]{:S(2)}, u32[]{:S(2)}) %collective-permute-start.1) | collective-permute-done | bytes 524320 | tf_op jit(solution)/shard_map/ppermute | solution.py:284
  104.0 2.2 add_convert_fusion
  106.2 0.0 copy-start.1
  106.2 14.7 %all-to-all-start.1 = ((bf16[8,128,256]{2,1,0:T(8,128)(2,1)}), bf16[8,128,256]{2,1,0:T(8,128)(2,1)S(1)}, u32[]{:S(2)}, u32[]{:S(2)}) async-start(bf16[8,128,256]{2,1,0:T(8,128)(2,1)} %add_convert_fusion), calls=%async_computation.1 | async-start | bytes 1048576 | tf_op jit(solution)/shard_map/all_to_all | solution.py:183
  120.8 25.7 %all-to-all-done.1 = bf16[8,128,256]{2,1,0:T(8,128)(2,1)S(1)} async-done(((bf16[8,128,256]{2,1,0:T(8,128)(2,1)}), bf16[8,128,256]{2,1,0:T(8,128)(2,1)S(1)}, u32[]{:S(2)}, u32[]{:S(2)}) %all-to-all-start.1) | async-done | bytes 524320 | tf_op jit(solution)/shard_map/all_to_all | solution.py:183
  146.5 0.1 convert_reduce_fusion
  146.6 0.9 fusion
  147.5 32.6 %all_to_all.21.rows_ref = bf16[8,128,256]{2,1,0:T(8,128)(2,1)S(1)} all-to-all(bf16[8,128,256]{2,1,0:T(8,128)(2,1)S(1)} %broadcast_in_dim.7), channel_id=1, replica_groups={{0,32,64,96,128,160,192,224},{16,48,80,112,144,176,208,240},{1,33,65,97..., dimensions={0} | all-to-all | bytes 1048576 | tf_op jit(solution)/shard_map/all_to_all | solution.py:183
  180.1 0.0 all-gather.3.cloned.1.call-done
  180.1 8.8 %collective-permute-start.2 = (bf16[8,128,256]{2,1,0:T(8,128)(2,1)S(1)}, bf16[8,128,256]{2,1,0:T(8,128)(2,1)S(1)}, u32[]{:S(2)}, u32[]{:S(2)}) collective-permute-start(bf16[8,128,256]{2,1,0:T(8,128)(2,1)S(1)} %all_to_all.21.rows_ref), channel_id=1, source_target_pairs={{0,16},{16,0},{32,48},{48,32},{64,80},{80,64},{96,112},{112,96},{1... | collective-permute-start | bytes 1572872 | tf_op jit(solution)/shard_map/ppermute | solution.py:293
  189.0 0.0 copy-done.1
  189.0 0.0 copy-start.2
  189.0 7.3 %gate_up.2 = (f32[2,1536,128]{2,1,0:T(8,128)S(1)}, f32[128,1]{1,0:T(8,128)S(1)}) custom-call(s32[1]{0:T(128)} %bitcast.2.scalar_ref, bf16[8,128,256]{2,1,0:T(8,128)(2,1)S(1)} %all_to_all.21.rows_ref, f32[8,2,1,256]{3,2,1,0:T(1,128)S(1)} %bitcast.20, bf16[32,12,2,96,256]{4,3,2,1,0:T(8,128)(2,1)} %bitcast.23, bf16[32,12,2,96,256]{4,3,2,1,0:T(8,128)(2,1)} %bitcast.24, ...), custom_call_target="tpu_custom_call" | custom-call | flops 1610612736 | bytes 12582912 | tf_op jit(solution)/shard_map/gate_up/pallas_call | solution.py:318
  196.3 1.5 collective-permute-done.2.rows_ref
  197.8 0.0 copy-done.2
  197.8 0.0 copy-start.4
  197.8 7.7 %gate_up.3 = bf16[192,128]{1,0:T(8,128)(2,1)S(1)} custom-call(s32[1]{0:T(128)} %bitcast.scalar_ref, bf16[8,128,256]{2,1,0:T(8,128)(2,1)S(1)} %collective-permute-done.2.rows_ref, f32[8,2,1,256]{3,2,1,0:T(1,128)S(1)} %bitcast.21, bf16[32,12,2,96,256]{4,3,2,1,0:T(8,128)(2,1)} %bitcast.27, bf16[32,12,2,96,256]{4,3,2,1,0:T(8,128)(2,1)} %bitcast.28, ...), custom_call_target="tpu_custom_call" | custom-call | flops 1610612736 | bytes 12582912 | tf_op jit(solution)/shard_map/gate_up/pallas_call | solution.py:318
  205.5 0.1 broadcast_in_dim.8
  205.6 29.3 %all_to_all.22.activation_ref = bf16[8,192,128]{2,1,0:T(8,128)(2,1)S(1)} all-to-all(bf16[8,192,128]{2,1,0:T(8,128)(2,1)S(1)} %broadcast_in_dim.8), channel_id=1, replica_groups={{0,32,64,96,128,160,192,224},{16,48,80,112,144,176,208,240},{1,33,65,97..., dimensions={0} | all-to-all | bytes 786432 | tf_op jit(solution)/shard_map/all_to_all | solution.py:183
  234.9 6.4 %collective-permute-start.3 = (bf16[8,192,128]{2,1,0:T(8,128)(2,1)S(1)}, bf16[8,192,128]{2,1,0:T(8,128)(2,1)S(1)}, u32[]{:S(2)}, u32[]{:S(2)}) collective-permute-start(bf16[8,192,128]{2,1,0:T(8,128)(2,1)S(1)} %all_to_all.22.activation_ref), channel_id=1, source_target_pairs={{0,16},{16,0},{32,48},{48,32},{64,80},{80,64},{96,112},{112,96},{1... | collective-permute-start | bytes 1179656 | tf_op jit(solution)/shard_map/ppermute | solution.py:342
  241.2 0.1 copy.23.routes_ref
  241.3 0.0 copy-done.4
  241.3 0.1 copy.24.route_weight_ref
  241.4 4.8 %down.2.start_ref = f32[128,256]{1,0:T(8,128)S(1)} custom-call(s32[1]{0:T(128)} %bitcast.2.scalar_ref, bf16[8,192,128]{2,1,0:T(8,128)(2,1)S(1)} %all_to_all.22.activation_ref, s32[128,2]{1,0:T(8,128)S(1)} %copy.23.routes_ref, f32[128,2]{1,0:T(8,128)S(1)} %copy.24.route_weight_ref, f32[128,256]{1,0:T(8,128)S(1)} %get-tuple-element.18.start_ref, ...), custom_call_target="tpu_custom_call" | custom-call | flops 805306368 | bytes 6291456 | tf_op jit(solution)/shard_map/down/pallas_call | solution.py:360
  246.3 0.1 collective-permute-done.3.activation_ref
  246.4 5.4 %down.3 = bf16[128,256]{1,0:T(8,128)(2,1)} custom-call(s32[1]{0:T(128)} %bitcast.scalar_ref, bf16[8,192,128]{2,1,0:T(8,128)(2,1)S(1)} %collective-permute-done.3.activation_ref, s32[128,2]{1,0:T(8,128)S(1)} %copy.23.routes_ref, f32[128,2]{1,0:T(8,128)S(1)} %copy.24.route_weight_ref, f32[128,256]{1,0:T(8,128)S(1)} %down.2.start_ref, ...), custom_call_target="tpu_custom_call" | custom-call | flops 805306368 | bytes 6291456 | tf_op jit(solution)/shard_map/down/pallas_call | solution.py:360
  (4 shorter events, 0.1 us)
Async XLA Ops:
  6.5 1.8 copy-start
  6.5 173.6 %all-gather.3.cloned.1.call-start = ((), (), s32[]{:S(2)}) async-start(), calls=%async_computation.4 | async-start | bytes 38928384 | tf_op jit(solution)/shard_map/all_gather | solution.py:238
  6.5 1.8 copy-start.3
  69.2 16.1 %collective-permute-start = (bf16[16,384,256]{2,1,0:T(8,128)(2,1)}, bf16[16,384,256]{2,1,0:T(8,128)(2,1)}, u32[]{:S(2)}, u32[]{:S(2)}) collective-permute-start(bf16[16,384,256]{2,1,0:T(8,128)(2,1)} %all_to_all.20.piece_ref), channel_id=1, source_target_pairs={{0,256},{256,0},{1,257},{257,1},{2,258},{258,2},{3,259},{259,3},{4... | collective-permute-start | bytes 9437192 | tf_op jit(solution)/shard_map/ppermute | solution.py:240
  88.5 15.4 %collective-permute-start.1 = (bf16[8,128,256]{2,1,0:T(8,128)(2,1)}, bf16[8,128,256]{2,1,0:T(8,128)(2,1)S(1)}, u32[]{:S(2)}, u32[]{:S(2)}) collective-permute-start(bf16[8,128,256]{2,1,0:T(8,128)(2,1)} %project.3), channel_id=1, source_target_pairs={{0,16},{16,0},{32,48},{48,32},{64,80},{80,64},{96,112},{112,96},{1... | collective-permute-start | bytes 1572872 | tf_op jit(solution)/shard_map/ppermute | solution.py:284
  106.2 82.8 %copy-start.1 = (f32[4096]{0:T(1024)S(1)}, f32[4096]{0:T(1024)}, u32[]{:S(2)}) copy-start(f32[4096]{0:T(1024)} %param.16) | copy-start | bytes 49156
  106.2 40.4 %all-to-all-start.1 = ((bf16[8,128,256]{2,1,0:T(8,128)(2,1)}), bf16[8,128,256]{2,1,0:T(8,128)(2,1)S(1)}, u32[]{:S(2)}, u32[]{:S(2)}) async-start(bf16[8,128,256]{2,1,0:T(8,128)(2,1)} %add_convert_fusion), calls=%async_computation.1 | async-start | bytes 1048576 | tf_op jit(solution)/shard_map/all_to_all | solution.py:183
  180.1 17.7 %collective-permute-start.2 = (bf16[8,128,256]{2,1,0:T(8,128)(2,1)S(1)}, bf16[8,128,256]{2,1,0:T(8,128)(2,1)S(1)}, u32[]{:S(2)}, u32[]{:S(2)}) collective-permute-start(bf16[8,128,256]{2,1,0:T(8,128)(2,1)S(1)} %all_to_all.21.rows_ref), channel_id=1, source_target_pairs={{0,16},{16,0},{32,48},{48,32},{64,80},{80,64},{96,112},{112,96},{1... | collective-permute-start | bytes 1572872 | tf_op jit(solution)/shard_map/ppermute | solution.py:293
  189.0 8.8 %copy-start.2 = (s32[128,2]{0,1:T(2,128)S(1)}, s32[128,2]{0,1:T(2,128)}, u32[]{:S(2)}) copy-start(s32[128,2]{0,1:T(2,128)} %param.17) | copy-start | bytes 3076
  197.8 43.5 %copy-start.4 = (f32[128,2]{0,1:T(2,128)S(1)}, f32[128,2]{0,1:T(2,128)}, u32[]{:S(2)}) copy-start(f32[128,2]{0,1:T(2,128)} %param.18) | copy-start | bytes 3076
  234.9 11.5 %collective-permute-start.3 = (bf16[8,192,128]{2,1,0:T(8,128)(2,1)S(1)}, bf16[8,192,128]{2,1,0:T(8,128)(2,1)S(1)}, u32[]{:S(2)}, u32[]{:S(2)}) collective-permute-start(bf16[8,192,128]{2,1,0:T(8,128)(2,1)S(1)} %all_to_all.22.activation_ref), channel_id=1, source_target_pairs={{0,16},{16,0},{32,48},{48,32},{64,80},{80,64},{96,112},{112,96},{1... | collective-permute-start | bytes 1179656 | tf_op jit(solution)/shard_map/ppermute | solution.py:342
Sparse Core Ops, SparseCore 0:
  10.5 164.6 all-gather.2

commit v7 on v6

--- a/solution.py
+++ b/solution.py
@@ -16,51 +16,53 @@
 SWAP = [(0, 1), (1, 0)]
 NEIGHBOUR = [(i, i ^ 1) for i in range(2 * PAIRS)]
 PARITY = [[2 * pair + odd for pair in range(PAIRS)] for odd in range(2)]
-CHUNK = 512
+CHUNK = 1024
+LOG2_E = 1.4426950408889634
 
 
 CONTRACT_LAST = (((1,), (1,)), ((), ()))
 
 
-def attend(place_ref, query_ref, piece_ref, out_ref, score_ref):
+def attend(place_ref, query_ref, piece_ref, out_ref):
     tokens = query_ref.shape[0]
     heads = query_ref.shape[1] // HEAD_WIDTH
     rows = heads * tokens
     blocks = CHUNK // tokens
     place = place_ref[0]
+    rate = HEAD_WIDTH ** (-0.5) * LOG2_E
     stacked = jnp.concatenate(
         [query_ref[:, HEAD_WIDTH * h : HEAD_WIDTH * (h + 1)] for h in range(heads)], axis=0
     )
-    token = place * tokens + lax.broadcasted_iota(jnp.int32, (rows, CHUNK), 0) % tokens
-    offset = token - lax.broadcasted_iota(jnp.int32, (rows, CHUNK), 1)
-
-    def score(step, row_max):
-        keys = piece_ref[pl.ds(step * blocks, blocks), :, :HEAD_WIDTH].reshape(CHUNK, HEAD_WIDTH)
+
+    def take(step, carry, masked):
+        row_max, total, summed = carry
+        place_here = pl.ds(step * blocks, blocks)
+        keys = piece_ref[place_here, :, :HEAD_WIDTH].reshape(CHUNK, HEAD_WIDTH)
+        values = piece_ref[place_here, :, HEAD_WIDTH:].reshape(CHUNK, HEAD_WIDTH)
         scores = lax.dot_general(
             stacked, keys, CONTRACT_LAST, preferred_element_type=jnp.float32
-        ) * HEAD_WIDTH ** (-0.5)
-        masked = jnp.where(offset >= step * CHUNK, scores, -1e30)
-        score_ref[step] = masked
-        return jnp.maximum(row_max, jnp.max(masked, axis=1, keepdims=True))
-
-    def weigh(step, carry):
-        total, summed = carry
-        exponent = jnp.exp(score_ref[step] - row_max)
-        values = piece_ref[pl.ds(step * blocks, blocks), :, HEAD_WIDTH:].reshape(CHUNK, HEAD_WIDTH)
-        return (
-            total + jnp.sum(exponent, axis=1, keepdims=True),
-            summed
-            + jnp.dot(exponent.astype(jnp.bfloat16), values, preferred_element_type=jnp.float32),
-        )
-
-    steps = place // blocks + 1
-    row_max = lax.fori_loop(0, steps, score, jnp.full((rows, 1), -1e30, jnp.float32))
-    total, summed = lax.fori_loop(
-        0,
-        steps,
-        weigh,
-        (jnp.zeros((rows, 1), jnp.float32), jnp.zeros((rows, HEAD_WIDTH), jnp.float32)),
+        )
+        if masked:
+            token = place * tokens + lax.broadcasted_iota(jnp.int32, (rows, CHUNK), 0) % tokens
+            offset = token - lax.broadcasted_iota(jnp.int32, (rows, CHUNK), 1)
+            scores = jnp.where(offset >= step * CHUNK, scores, -1e30)
+        new_max = jnp.maximum(row_max, jnp.max(scores, axis=1, keepdims=True))
+        shrink = jnp.exp2((row_max - new_max) * rate)
+        exponent = jnp.exp2((scores - new_max) * rate)
+        total = total * shrink + jnp.sum(exponent, axis=1, keepdims=True)
+        summed = summed * shrink + jnp.dot(
+            exponent.astype(jnp.bfloat16), values, preferred_element_type=jnp.float32
+        )
+        return new_max, total, summed
+
+    full = place // blocks
+    carry = (
+        jnp.full((rows, 1), -1e30, jnp.float32),
+        jnp.zeros((rows, 1), jnp.float32),
+        jnp.zeros((rows, HEAD_WIDTH), jnp.float32),
     )
+    carry = lax.fori_loop(0, full, lambda step, held: take(step, held, False), carry)
+    _, total, summed = take(full, carry, True)
     attended = (summed / total).astype(out_ref.dtype)
     halves = heads // 2
     for h in range(heads):
@@ -69,8 +71,8 @@
         )
 
 
-def project(scalar_ref, attended_ref, own_ref, other_ref, out_ref):
-    core = scalar_ref[0]
+def project(core_ref, parity_ref, attended_ref, own_ref, other_ref, out_ref):
+    core = core_ref[0]
     for block in range(own_ref.shape[0]):
         out_ref[block] = (
             jnp.dot(attended_ref[core], own_ref[block, 0], preferred_element_type=jnp.float32)
@@ -80,41 +82,48 @@
         ).astype(out_ref.dtype)
 
 
-def gate_up(last, parts, scalar_ref, rows_ref, gain_ref, *refs):
-    gate_refs, up_refs, refs = refs[:parts], refs[parts : 2 * parts], refs[2 * parts :]
+def gate_up(last, scalar_ref, rows_ref, gain_ref, gate_ref, up_ref, *refs):
     if last:
         before, before_square, routes_ref, out_ref, scaled, totals, square = refs
     else:
         totals, square, scaled = refs
     step = pl.program_id(0)
-    experts, per_step, _, units, columns = gate_refs[0].shape
+    experts, per_step, _, units, columns = gate_ref.shape
     pieces, tokens, _ = rows_ref.shape
+    together = 2 * units
 
     @pl.when(step == 0)
     def _():
-        if last:
-            square[...] = before_square[...]
-            totals[...] = before[...]
-        else:
-            square[...] = jnp.zeros_like(square)
-            totals[...] = jnp.zeros_like(totals)
+        squares = jnp.zeros((tokens, columns), jnp.float32)
         for piece in range(pieces):
             rows = rows_ref[piece].astype(jnp.float32)
-            square[...] += jnp.sum(rows * rows, axis=1, keepdims=True)
+            squares += rows * rows
             scaled[piece] = (rows * gain_ref[piece, scalar_ref[0]]).astype(jnp.bfloat16)
-
-    for which, weight_refs in enumerate((gate_refs, up_refs)):
-        for part, weight_ref in enumerate(weight_refs):
-            place = pl.ds(part * experts * units, experts * units)
-            product = totals[which, place]
-            for piece in range(per_step):
-                product += lax.dot_general(
-                    weight_ref[:, piece, 0].reshape(experts * units, columns),
-                    scaled[step * per_step + piece],
-                    CONTRACT_LAST,
-                    preferred_element_type=jnp.float32,
-                )
-            totals[which, place] = product
+        sums = jnp.sum(squares, axis=1, keepdims=True)
+        square[...] = before_square[...] + sums if last else sums
+
+    def multiply(start):
+        for which, weight_ref in enumerate((gate_ref, up_ref)):
+            for expert in range(0, experts, 2):
+                place = pl.ds(expert * units, together)
+                product = None if start is None else start[which, place]
+                for piece in range(per_step):
+                    part = lax.dot_general(
+                        weight_ref[expert : expert + 2, piece, 0].reshape(together, columns),
+                        scaled[step * per_step + piece],
+                        CONTRACT_LAST,
+                        preferred_element_type=jnp.float32,
+                    )
+                    product = part if product is None else product + part
+                totals[which, place] = product
+
+    @pl.when(step == 0)
+    def _():
+        multiply(before if last else None)
+
+    @pl.when(step > 0)
+    def _():
+        multiply(totals)
 
     if last:
 
@@ -123,7 +132,7 @@
             scale = lax.rsqrt(square[...] / D + 1e-06)
             scale = jnp.transpose(jnp.broadcast_to(scale, (tokens, tokens)))[:1]
             chosen = [jnp.zeros((units, tokens), jnp.float32) for _ in range(TOP)]
-            for expert in range(parts * experts):
+            for expert in range(experts):
                 gate_values = totals[0, expert * units : (expert + 1) * units] * scale
                 up_values = totals[1, expert * units : (expert + 1) * units] * scale
                 activation = gate_values / (1.0 + jnp.exp(-gate_values)) * up_values
@@ -167,12 +176,13 @@
 
 
 SCALAR = pl.BlockSpec(memory_space=pltpu.SMEM)
+HERE = pl.BlockSpec(memory_space=pltpu.VMEM)
 LIMIT = pltpu.CompilerParams(vmem_limit_bytes=32 * 1024 * 1024)
 WIDE = pltpu.CompilerParams(vmem_limit_bytes=56 * 1024 * 1024)
 
 
 def whole(*shape):
-    return pl.BlockSpec(shape, lambda i, scalar_ref: (0,) * len(shape))
+    return pl.BlockSpec(shape, lambda i, *_: (0,) * len(shape))
 
 
 def cost(flops, size):
@@ -234,7 +244,6 @@
     half_rows = out_weight.shape[0] // 2
     weight_half = lax.dynamic_slice_in_dim(out_weight, core * half_rows, half_rows, 0)
     message = jnp.concatenate([weight_half, jnp.concatenate([key_head, value_head], axis=1)], axis=0)
-    message, weights_here = lax.optimization_barrier((message, weights_here))
     weights = lax.all_gather(weights_here, ("dp", "expert"), axis=0)
     gathered = spread(message, "expert", expert_count)
     gathered_other = lax.ppermute(gathered, "dp", SWAP)
@@ -251,9 +260,6 @@
             ),
         ],
         out_specs=pl.BlockSpec((2, tokens, half_rows), lambda i: (0, 0, 0)),
-        scratch_shapes=[
-            pltpu.VMEM((expert_count * tokens // CHUNK, local_heads * tokens, CHUNK), jnp.float32)
-        ],
         compiler_params=WIDE,
         name="attend",
     )(expert_index.astype(jnp.int32).reshape(1), queries, gathered)
@@ -265,21 +271,21 @@
 
     def projected(parity, dtype):
         weight_spec = pl.BlockSpec(
-            (wide, 1, half_rows, columns), lambda i, scalar_ref: (i, scalar_ref[1], 0, 0)
+            (wide, 1, half_rows, columns), lambda i, core_ref, parity_ref: (i, parity_ref[0], 0, 0)
         )
         return pl.pallas_call(
             project,
             out_shape=jax.ShapeDtypeStruct((PAIRS, tokens, columns), dtype),
             grid_spec=pltpu.PrefetchScalarGridSpec(
-                num_scalar_prefetch=1,
+                num_scalar_prefetch=2,
                 grid=(PAIRS // wide,),
                 in_specs=[whole(2, tokens, half_rows), weight_spec, weight_spec],
-                out_specs=pl.BlockSpec((wide, tokens, columns), lambda i, scalar_ref: (i, 0, 0)),
-            ),
-            compiler_params=WIDE,
+                out_specs=pl.BlockSpec((wide, tokens, columns), lambda i, *_: (i, 0, 0)),
+            ),
+            compiler_params=LIMIT,
             cost_estimate=cost(4 * tokens * half_rows * PAIRS * columns, 4 * half_rows * PAIRS * columns),
             name="project",
-        )(jnp.stack([core, parity]), attended, gathered, gathered_other)
+        )(core.reshape(1), parity.reshape(1), attended, gathered, gathered_other)
 
     given = lax.ppermute(projected(1 - odd, jnp.bfloat16), "tensor", NEIGHBOUR)
     kept = projected(odd, jnp.float32)
@@ -293,39 +299,34 @@
     rows_other = lax.ppermute(rows_own, "tensor", NEIGHBOUR)
     weights = weights.reshape(2 * expert_count, blocks // 2, 2, local_units, columns)
 
-    parts = 2
-    per_part = expert_count // parts
-    per_step = 2
+    per_step = 4
     gains = post_gain.reshape(PAIRS, 2, 1, columns)
-    totals_shape = (2, expert_count * local_units, tokens)
-
-    def first_spec(place):
+    totals_types = [
+        jax.ShapeDtypeStruct((2, expert_count * local_units, tokens), jnp.float32),
+        jax.ShapeDtypeStruct((tokens, 1), jnp.float32),
+    ]
+    out_type = jax.ShapeDtypeStruct((TOP * local_units, tokens), jnp.bfloat16)
+
+    def first_spec(which):
         return pl.BlockSpec(
-            (per_part, per_step, 1, local_units, columns),
-            lambda i, scalar_ref: (place, i, scalar_ref[0], 0, 0),
+            (expert_count, per_step, 1, local_units, columns),
+            lambda i, parity_ref: (which, i, parity_ref[0], 0, 0),
         )
 
     def gated(parity, rows, *before):
         last = bool(before)
-        totals_spec = [whole(*totals_shape), whole(tokens, 1)]
-        totals_types = [
-            jax.ShapeDtypeStruct(totals_shape, jnp.float32),
-            jax.ShapeDtypeStruct((tokens, 1), jnp.float32),
-        ]
-        scaled = [pltpu.VMEM((PAIRS, tokens, columns), jnp.bfloat16)]
-        totals_scratch = [pltpu.VMEM(kind.shape, kind.dtype) for kind in totals_types]
-        out = (TOP * local_units, tokens)
+        scratch = [pltpu.VMEM((PAIRS, tokens, columns), jnp.bfloat16)]
+        if last:
+            scratch += [pltpu.VMEM(kind.shape, kind.dtype) for kind in totals_types]
         return pl.pallas_call(
-            functools.partial(gate_up, last, parts),
-            out_shape=jax.ShapeDtypeStruct(out, jnp.bfloat16) if last else totals_types,
+            functools.partial(gate_up, last),
+            out_shape=out_type if last else totals_types,
             grid_spec=pltpu.PrefetchScalarGridSpec(
                 num_scalar_prefetch=1,
                 grid=(PAIRS // per_step,),
-                in_specs=[whole(PAIRS, tokens, columns), whole(PAIRS, 2, 1, columns)]
-                + [first_spec(place) for place in range(2 * parts)]
-                + (totals_spec + [whole(TOP, tokens)] if last else []),
-                out_specs=whole(*out) if last else totals_spec,
-                scratch_shapes=scaled + totals_scratch if last else scaled,
+                in_specs=[HERE, HERE, first_spec(0), first_spec(1)] + [HERE] * len(before),
+                out_specs=HERE if last else [HERE] * 2,
+                scratch_shapes=scratch,
             ),
             compiler_params=LIMIT,
             cost_estimate=cost(
@@ -333,14 +334,15 @@
                 2 * 2 * expert_count * local_units * D // 2,
             ),
             name="gate_up",
-        )(parity.reshape(1), rows, gains, *[weights] * (2 * parts), *before)
+        )(parity.reshape(1), rows, gains, weights, weights, *before)
 
     before = gated(odd, rows_own)
     activation = gated(1 - odd, rows_other, *before, routes.T)
 
     activation_own = spread(activation, "tensor", PAIRS, PARITY)
     activation_other = lax.ppermute(activation_own, "tensor", NEIGHBOUR)
-    per_part = 2
+    parts = 2
+    per_part = 4
     down_steps = expert_count // (parts * per_part)
     quarter = PAIRS // 2
 

time: 263 us -> 260 us (0.989)
  Pallas kernels: 35.5 us -> 29.7 us
  waiting for transfers between devices: 36.6 us -> 40.6 us
    pallas_call x2, Pallas kernels: 7.32 us -> 3.74 us  [projected(): pl.pallas_call(project, out_shape=jax.ShapeDtypeStruct((PAIRS, tokens, co...]
  transfers between devices with their start and end apart: 6 -> 6, of which waited for: 5 -> 5; matrix products, arithmetic and copies ran while one was open for 2% -> 1% of each run, Pallas kernels for 9% -> 7%
where the time goes in v7:
time: 260 us; the launch traced here: 255 us
  blocking collectives  121 us (47%)
  starting transfers between devices  43.9 us (17%)
  waiting for transfers between devices  40.6 us (16%)
  Pallas kernels  29.7 us (11%)
  between operations  13.6 us (5%)
  other arithmetic  4.25 us (2%)
  local copies, waits for them, and re-layouts  2.79 us (1%)
    all_to_all x3, blocking collectives, exchange(): lax.all_to_all(message, axis, split_axis=0, concat_axis=0, tiled=True, ax...  121 us
    all_to_all x1, waiting for transfers between devices, exchange(): lax.all_to_all(message, axis, split_axis=0, concat_axis=0, tiled=True, ax...  25.6 us
    all_to_all x1, starting transfers between devices, exchange(): lax.all_to_all(message, axis, split_axis=0, concat_axis=0, tiled=True, ax...  14.7 us
    pallas_call x2, Pallas kernels, gated(): pl.pallas_call(functools.partial(gate_up, last), out_shape=out_type if la...  13.7 us
    ppermute x1, starting transfers between devices, local(): gathered_other = lax.ppermute(gathered, 'dp', SWAP)  10.4 us
    ppermute x1, waiting for transfers between devices, local(): given = lax.ppermute(projected(1 - odd, jnp.bfloat16), 'tensor', NEIGHBOUR)  9.93 us
    pallas_call x2, Pallas kernels, lowered(): pl.pallas_call(functools.partial(down, parts), out_shape=jax.ShapeDtypeSt...  8.98 us
    ppermute x1, starting transfers between devices, local(): rows_other = lax.ppermute(rows_own, 'tensor', NEIGHBOUR)  8.85 us
  transfers between devices with their start and end apart: 6, of which 5 were waited for; matrix products, arithmetic and copies ran while one was open for 1% of the time, Pallas kernels for 7%

profile of v7, /device:TPU:1, one launch (start us, length us, event | category | flops | bytes accessed | tf_op | source)
XLA Modules:
  0.0 255.4 jit_solution(7164627893947582300)
XLA Ops:
  6.5 0.0 copy-start
  6.5 0.0 all-gather.3.cloned.1.call-start
  6.5 1.3 broadcast_select_fusion
  7.8 0.2 copy.25
  8.0 0.2 copy.20
  8.3 0.0 copy-start.4
  8.3 0.0 copy-done
  8.3 1.1 pad_maximum_fusion
  9.4 0.0 all-gather.3.cloned.1.call-update
  9.4 0.8 constant_dynamic-slice_fusion
  10.2 0.0 copy-done.4
  10.3 0.3 broadcast_in_dim.6
  10.6 58.6 %all_to_all.20.piece_ref = bf16[16,384,256]{2,1,0:T(8,128)(2,1)} all-to-all(bf16[16,384,256]{2,1,0:T(8,128)(2,1)S(1)} %broadcast_in_dim.6), channel_id=1, replica_groups=mesh['dp'=2,'tensor'=16,'expert'=16] {'expert'}, dimensions={0} | all-to-all | bytes 6291456 | tf_op jit(solution)/shard_map/all_to_all | solution.py:193
  69.2 10.4 %collective-permute-start = (bf16[16,384,256]{2,1,0:T(8,128)(2,1)}, bf16[16,384,256]{2,1,0:T(8,128)(2,1)}, u32[]{:S(2)}, u32[]{:S(2)}) collective-permute-start(bf16[16,384,256]{2,1,0:T(8,128)(2,1)} %all_to_all.20.piece_ref), channel_id=1, source_target_pairs={{0,256},{256,0},{1,257},{257,1},{2,258},{258,2},{3,259},{259,3},{4... | collective-permute-start | bytes 9437192 | tf_op jit(solution)/shard_map/ppermute | solution.py:249
  79.7 3.2 %attend.1.attended_ref = bf16[2,128,256]{2,1,0:T(8,128)(2,1)} custom-call(s32[1]{0:T(128)} %bitcast.3.place_ref, bf16[128,512]{1,0:T(8,128)(2,1)} %query_ref.1, bf16[16,384,256]{2,1,0:T(8,128)(2,1)} %all_to_all.20.piece_ref), custom_call_target="tpu_custom_call" | custom-call | tf_op jit(solution)/shard_map/attend/pallas_call | solution.py:251
  82.9 2.4 collective-permute-done
  85.3 0.0 copy-start.1
  85.3 0.9 copy-done.1
  86.2 1.9 project.3
  88.0 3.4 %collective-permute-start.1 = (bf16[8,128,256]{2,1,0:T(8,128)(2,1)S(1)}, bf16[8,128,256]{2,1,0:T(8,128)(2,1)S(1)}, u32[]{:S(2)}, u32[]{:S(2)}) collective-permute-start(bf16[8,128,256]{2,1,0:T(8,128)(2,1)S(1)} %project.3), channel_id=1, source_target_pairs={{0,16},{16,0},{32,48},{48,32},{64,80},{80,64},{96,112},{112,96},{1... | collective-permute-start | bytes 1572872 | tf_op jit(solution)/shard_map/ppermute | solution.py:290
  91.5 1.9 project.2
  93.3 9.9 %collective-permute-done.1 = bf16[8,128,256]{2,1,0:T(8,128)(2,1)S(1)} collective-permute-done((bf16[8,128,256]{2,1,0:T(8,128)(2,1)S(1)}, bf16[8,128,256]{2,1,0:T(8,128)(2,1)S(1)}, u32[]{:S(2)}, u32[]{:S(2)}) %collective-permute-start.1) | collective-permute-done | bytes 524320 | tf_op jit(solution)/shard_map/ppermute | solution.py:290
  103.3 0.9 add_convert_fusion
  104.2 0.0 copy-start.2
  104.2 14.7 %all-to-all-start.1 = ((bf16[8,128,256]{2,1,0:T(8,128)(2,1)}), bf16[8,128,256]{2,1,0:T(8,128)(2,1)S(1)}, u32[]{:S(2)}, u32[]{:S(2)}) async-start(bf16[8,128,256]{2,1,0:T(8,128)(2,1)} %add_convert_fusion), calls=%async_computation.1 | async-start | bytes 1048576 | tf_op jit(solution)/shard_map/all_to_all | solution.py:193
  118.9 25.6 %all-to-all-done.1 = bf16[8,128,256]{2,1,0:T(8,128)(2,1)S(1)} async-done(((bf16[8,128,256]{2,1,0:T(8,128)(2,1)}), bf16[8,128,256]{2,1,0:T(8,128)(2,1)S(1)}, u32[]{:S(2)}, u32[]{:S(2)}) %all-to-all-start.1) | async-done | bytes 524320 | tf_op jit(solution)/shard_map/all_to_all | solution.py:193
  144.5 0.1 convert_reduce_fusion
  144.6 0.9 fusion
  145.5 32.7 %all_to_all.21.rows_ref = bf16[8,128,256]{2,1,0:T(8,128)(2,1)S(1)} all-to-all(bf16[8,128,256]{2,1,0:T(8,128)(2,1)S(1)} %broadcast_in_dim.7), channel_id=1, replica_groups={{0,32,64,96,128,160,192,224},{16,48,80,112,144,176,208,240},{1,33,65,97..., dimensions={0} | all-to-all | bytes 1048576 | tf_op jit(solution)/shard_map/all_to_all | solution.py:193
  178.2 0.0 all-gather.3.cloned.1.call-done
  178.2 8.9 %collective-permute-start.2 = (bf16[8,128,256]{2,1,0:T(8,128)(2,1)S(1)}, bf16[8,128,256]{2,1,0:T(8,128)(2,1)S(1)}, u32[]{:S(2)}, u32[]{:S(2)}) collective-permute-start(bf16[8,128,256]{2,1,0:T(8,128)(2,1)S(1)} %all_to_all.21.rows_ref), channel_id=1, source_target_pairs={{0,16},{16,0},{32,48},{48,32},{64,80},{80,64},{96,112},{112,96},{1... | collective-permute-start | bytes 1572872 | tf_op jit(solution)/shard_map/ppermute | solution.py:299
  187.0 0.0 copy-done.2
  187.1 0.0 copy-start.3
  187.1 6.6 %gate_up.2 = (f32[2,1536,128]{2,1,0:T(8,128)S(1)}, f32[128,1]{1,0:T(8,128)S(1)}) custom-call(s32[1]{0:T(128)} %bitcast.2.parity_ref.scalar_ref, bf16[8,128,256]{2,1,0:T(8,128)(2,1)S(1)} %all_to_all.21.rows_ref, f32[8,2,1,256]{3,2,1,0:T(1,128)S(1)} %bitcast.20, bf16[32,12,2,96,256]{4,3,2,1,0:T(8,128)(2,1)} %bitcast.23, bf16[32,12,2,96,256]{4,3,2,1,0:T(8,128)(2,1)} %bitcast.24), custom_call_target="tpu_custom_call" | custom-call | flops 1610612736 | bytes 12582912 | tf_op jit(solution)/shard_map/gate_up/pallas_call | solution.py:321
  193.7 2.2 collective-permute-done.2.rows_ref
  195.9 0.0 copy-done.3
  195.9 0.0 copy-start.5
  195.9 7.1 %gate_up.3 = bf16[192,128]{1,0:T(8,128)(2,1)S(1)} custom-call(s32[1]{0:T(128)} %bitcast.parity_ref.scalar_ref, bf16[8,128,256]{2,1,0:T(8,128)(2,1)S(1)} %collective-permute-done.2.rows_ref, f32[8,2,1,256]{3,2,1,0:T(1,128)S(1)} %bitcast.21, bf16[32,12,2,96,256]{4,3,2,1,0:T(8,128)(2,1)} %bitcast.25, bf16[32,12,2,96,256]{4,3,2,1,0:T(8,128)(2,1)} %bitcast.26, ...), custom_call_target="tpu_custom_call" | custom-call | flops 1610612736 | bytes 12582912 | tf_op jit(solution)/shard_map/gate_up/pallas_call | solution.py:321
  203.0 0.1 broadcast_in_dim.8
  203.0 29.3 %all_to_all.22.activation_ref = bf16[8,192,128]{2,1,0:T(8,128)(2,1)S(1)} all-to-all(bf16[8,192,128]{2,1,0:T(8,128)(2,1)S(1)} %broadcast_in_dim.8), channel_id=1, replica_groups={{0,32,64,96,128,160,192,224},{16,48,80,112,144,176,208,240},{1,33,65,97..., dimensions={0} | all-to-all | bytes 786432 | tf_op jit(solution)/shard_map/all_to_all | solution.py:193
  232.4 6.5 %collective-permute-start.3 = (bf16[8,192,128]{2,1,0:T(8,128)(2,1)S(1)}, bf16[8,192,128]{2,1,0:T(8,128)(2,1)S(1)}, u32[]{:S(2)}, u32[]{:S(2)}) collective-permute-start(bf16[8,192,128]{2,1,0:T(8,128)(2,1)S(1)} %all_to_all.22.activation_ref), channel_id=1, source_target_pairs={{0,16},{16,0},{32,48},{48,32},{64,80},{80,64},{96,112},{112,96},{1... | collective-permute-start | bytes 1179656 | tf_op jit(solution)/shard_map/ppermute | solution.py:343
  238.9 0.1 copy.23.routes_ref
  239.0 0.0 copy-done.5
  239.0 0.1 copy.24.route_weight_ref
  239.1 4.2 %down.2.start_ref = f32[128,256]{1,0:T(8,128)S(1)} custom-call(s32[1]{0:T(128)} %bitcast.2.parity_ref.scalar_ref, bf16[8,192,128]{2,1,0:T(8,128)(2,1)S(1)} %all_to_all.22.activation_ref, s32[128,2]{1,0:T(8,128)S(1)} %copy.23.routes_ref, f32[128,2]{1,0:T(8,128)S(1)} %copy.24.route_weight_ref, f32[128,256]{1,0:T(8,128)S(1)} %get-tuple-element.14.start_ref, ...), custom_call_target="tpu_custom_call" | custom-call | flops 805306368 | bytes 6291456 | tf_op jit(solution)/shard_map/down/pallas_call | solution.py:362
  243.3 0.5 collective-permute-done.3.activation_ref
  243.8 4.8 %down.3 = bf16[128,256]{1,0:T(8,128)(2,1)} custom-call(s32[1]{0:T(128)} %bitcast.parity_ref.scalar_ref, bf16[8,192,128]{2,1,0:T(8,128)(2,1)S(1)} %collective-permute-done.3.activation_ref, s32[128,2]{1,0:T(8,128)S(1)} %copy.23.routes_ref, f32[128,2]{1,0:T(8,128)S(1)} %copy.24.route_weight_ref, f32[128,256]{1,0:T(8,128)S(1)} %down.2.start_ref, ...), custom_call_target="tpu_custom_call" | custom-call | flops 805306368 | bytes 6291456 | tf_op jit(solution)/shard_map/down/pallas_call | solution.py:362
  (4 shorter events, 0.1 us)
Async XLA Ops:
  6.5 1.7 copy-start
  6.5 171.6 %all-gather.3.cloned.1.call-start = ((), (), s32[]{:S(2)}) async-start(), calls=%async_computation.4 | async-start | bytes 38928384 | tf_op jit(solution)/shard_map/all_gather | solution.py:247
  8.3 2.0 copy-start.4
  69.2 16.1 %collective-permute-start = (bf16[16,384,256]{2,1,0:T(8,128)(2,1)}, bf16[16,384,256]{2,1,0:T(8,128)(2,1)}, u32[]{:S(2)}, u32[]{:S(2)}) collective-permute-start(bf16[16,384,256]{2,1,0:T(8,128)(2,1)} %all_to_all.20.piece_ref), channel_id=1, source_target_pairs={{0,256},{256,0},{1,257},{257,1},{2,258},{258,2},{3,259},{259,3},{4... | collective-permute-start | bytes 9437192 | tf_op jit(solution)/shard_map/ppermute | solution.py:249
  85.3 0.9 copy-start.1
  88.0 15.2 %collective-permute-start.1 = (bf16[8,128,256]{2,1,0:T(8,128)(2,1)S(1)}, bf16[8,128,256]{2,1,0:T(8,128)(2,1)S(1)}, u32[]{:S(2)}, u32[]{:S(2)}) collective-permute-start(bf16[8,128,256]{2,1,0:T(8,128)(2,1)S(1)} %project.3), channel_id=1, source_target_pairs={{0,16},{16,0},{32,48},{48,32},{64,80},{80,64},{96,112},{112,96},{1... | collective-permute-start | bytes 1572872 | tf_op jit(solution)/shard_map/ppermute | solution.py:290
  104.2 82.8 %copy-start.2 = (f32[4096]{0:T(1024)S(1)}, f32[4096]{0:T(1024)}, u32[]{:S(2)}) copy-start(f32[4096]{0:T(1024)} %param.16) | copy-start | bytes 49156
  104.2 40.3 %all-to-all-start.1 = ((bf16[8,128,256]{2,1,0:T(8,128)(2,1)}), bf16[8,128,256]{2,1,0:T(8,128)(2,1)S(1)}, u32[]{:S(2)}, u32[]{:S(2)}) async-start(bf16[8,128,256]{2,1,0:T(8,128)(2,1)} %add_convert_fusion), calls=%async_computation.1 | async-start | bytes 1048576 | tf_op jit(solution)/shard_map/all_to_all | solution.py:193
  178.2 17.7 %collective-permute-start.2 = (bf16[8,128,256]{2,1,0:T(8,128)(2,1)S(1)}, bf16[8,128,256]{2,1,0:T(8,128)(2,1)S(1)}, u32[]{:S(2)}, u32[]{:S(2)}) collective-permute-start(bf16[8,128,256]{2,1,0:T(8,128)(2,1)S(1)} %all_to_all.21.rows_ref), channel_id=1, source_target_pairs={{0,16},{16,0},{32,48},{48,32},{64,80},{80,64},{96,112},{112,96},{1... | collective-permute-start | bytes 1572872 | tf_op jit(solution)/shard_map/ppermute | solution.py:299
  187.1 8.8 %copy-start.3 = (s32[128,2]{0,1:T(2,128)S(1)}, s32[128,2]{0,1:T(2,128)}, u32[]{:S(2)}) copy-start(s32[128,2]{0,1:T(2,128)} %param.17) | copy-start | bytes 3076
  195.9 43.1 %copy-start.5 = (f32[128,2]{0,1:T(2,128)S(1)}, f32[128,2]{0,1:T(2,128)}, u32[]{:S(2)}) copy-start(f32[128,2]{0,1:T(2,128)} %param.18) | copy-start | bytes 3076
  232.4 11.5 %collective-permute-start.3 = (bf16[8,192,128]{2,1,0:T(8,128)(2,1)S(1)}, bf16[8,192,128]{2,1,0:T(8,128)(2,1)S(1)}, u32[]{:S(2)}, u32[]{:S(2)}) collective-permute-start(bf16[8,192,128]{2,1,0:T(8,128)(2,1)S(1)} %all_to_all.22.activation_ref), channel_id=1, source_target_pairs={{0,16},{16,0},{32,48},{48,32},{64,80},{80,64},{96,112},{112,96},{1... | collective-permute-start | bytes 1179656 | tf_op jit(solution)/shard_map/ppermute | solution.py:343
Sparse Core Ops, SparseCore 0:
  10.5 164.6 all-gather.2

commit v8 on v7

--- a/solution.py
+++ b/solution.py
@@ -27,6 +27,7 @@
     tokens = query_ref.shape[0]
     heads = query_ref.shape[1] // HEAD_WIDTH
     rows = heads * tokens
+    half = tokens // 2
     blocks = CHUNK // tokens
     place = place_ref[0]
     rate = HEAD_WIDTH ** (-0.5) * LOG2_E
@@ -37,15 +38,17 @@
     def take(step, carry, masked):
         row_max, total, summed = carry
         place_here = pl.ds(step * blocks, blocks)
-        keys = piece_ref[place_here, :, :HEAD_WIDTH].reshape(CHUNK, HEAD_WIDTH)
-        values = piece_ref[place_here, :, HEAD_WIDTH:].reshape(CHUNK, HEAD_WIDTH)
+        keys = piece_ref[:, place_here, :half].reshape(CHUNK, HEAD_WIDTH)
+        values = piece_ref[:, place_here, half:].reshape(CHUNK, HEAD_WIDTH)
         scores = lax.dot_general(
             stacked, keys, CONTRACT_LAST, preferred_element_type=jnp.float32
         )
         if masked:
-            token = place * tokens + lax.broadcasted_iota(jnp.int32, (rows, CHUNK), 0) % tokens
-            offset = token - lax.broadcasted_iota(jnp.int32, (rows, CHUNK), 1)
-            scores = jnp.where(offset >= step * CHUNK, scores, -1e30)
+            token = lax.broadcasted_iota(jnp.int32, (rows, 1), 0) % tokens + place * tokens
+            key = lax.broadcasted_iota(jnp.int32, (1, CHUNK), 1)
+            odd_half, rest = key // (blocks * half), key % (blocks * half)
+            key_place = (step * blocks + rest // half) * tokens + odd_half * half + rest % half
+            scores = jnp.where(token >= key_place, scores, -1e30)
         new_max = jnp.maximum(row_max, jnp.max(scores, axis=1, keepdims=True))
         shrink = jnp.exp2((row_max - new_max) * rate)
         exponent = jnp.exp2((scores - new_max) * rate)
@@ -71,15 +74,18 @@
         )
 
 
-def project(core_ref, parity_ref, attended_ref, own_ref, other_ref, out_ref):
+def project(last, core_ref, source_ref, attended_ref, own_ref, other_ref, *refs):
     core = core_ref[0]
-    for block in range(own_ref.shape[0]):
-        out_ref[block] = (
-            jnp.dot(attended_ref[core], own_ref[block, 0], preferred_element_type=jnp.float32)
-            + jnp.dot(
-                attended_ref[1 - core], other_ref[block, 0], preferred_element_type=jnp.float32
-            )
-        ).astype(out_ref.dtype)
+    out_ref = refs[-1]
+    for block in range(own_ref.shape[1]):
+        own = jnp.concatenate([own_ref[0, block, 0], own_ref[0, block, 1]], axis=1)
+        other = jnp.concatenate([other_ref[0, block, 0], other_ref[0, block, 1]], axis=1)
+        total = jnp.dot(attended_ref[core], own, preferred_element_type=jnp.float32) + jnp.dot(
+            attended_ref[1 - core], other, preferred_element_type=jnp.float32
+        )
+        if last:
+            total += refs[0][block]
+        out_ref[block] = total.astype(out_ref.dtype)
 
 
 def gate_up(last, scalar_ref, rows_ref, gain_ref, gate_ref, up_ref, *refs):
@@ -232,7 +238,9 @@
     blocks = first_blocks + down_blocks
 
     gate_or_up = jnp.where(core == 0, gate_weight[0], up_weight[0]).T
-    gate_or_up = jnp.transpose(gate_or_up.reshape(local_units, first_blocks, columns), (1, 0, 2))
+    gate_or_up = jnp.transpose(
+        gate_or_up.reshape(local_units, PAIRS, 2, 2, columns // 2), (1, 3, 0, 2, 4)
+    )
     down_half = lax.dynamic_slice_in_dim(down_weight[0], core * half_units, half_units, 0)
     weights_here = jnp.concatenate(
         [gate_or_up.reshape(first_blocks * local_units, columns), down_half], axis=0
@@ -243,9 +251,32 @@
     value_head = lax.dynamic_slice_in_dim(all_value_rows, shared * HEAD_WIDTH, HEAD_WIDTH, 1)
     half_rows = out_weight.shape[0] // 2
     weight_half = lax.dynamic_slice_in_dim(out_weight, core * half_rows, half_rows, 0)
-    message = jnp.concatenate([weight_half, jnp.concatenate([key_head, value_head], axis=1)], axis=0)
+    half_tokens = tokens // 2
+    half_columns = columns // 2
+    key_half = lax.dynamic_slice_in_dim(key_head, odd * half_tokens, half_tokens, 0)
+    value_half = lax.dynamic_slice_in_dim(value_head, odd * half_tokens, half_tokens, 0)
+    message = jnp.stack(
+        [
+            jnp.concatenate(
+                [weight_half[:, side * half_columns : (side + 1) * half_columns], key_half, value_half],
+                axis=0,
+            )
+            for side in range(2)
+        ]
+    )
+    message_rows = message.shape[1]
+    both = [
+        [(2 * pair + side) * expert_count + place for side in range(2) for place in range(expert_count)]
+        for pair in range(PAIRS)
+    ]
     weights = lax.all_gather(weights_here, ("dp", "expert"), axis=0)
-    gathered = spread(message, "expert", expert_count)
+    gathered = exchange(
+        jnp.broadcast_to(message[:, None], (2, expert_count) + message.shape[1:]).reshape(
+            2 * expert_count, message_rows, half_columns
+        ),
+        ("tensor", "expert"),
+        both,
+    )
     gathered_other = lax.ppermute(gathered, "dp", SWAP)
 
     attended = pl.pallas_call(
@@ -256,43 +287,54 @@
             SCALAR,
             pl.BlockSpec((tokens, local_heads * HEAD_WIDTH), lambda i: (0, 0)),
             pl.BlockSpec(
-                (expert_count, tokens, 2 * HEAD_WIDTH), lambda i: (0, half_rows // tokens, 0)
+                (2, expert_count, tokens, HEAD_WIDTH), lambda i: (0, 0, half_rows // tokens, 0)
             ),
         ],
         out_specs=pl.BlockSpec((2, tokens, half_rows), lambda i: (0, 0, 0)),
         compiler_params=WIDE,
         name="attend",
-    )(expert_index.astype(jnp.int32).reshape(1), queries, gathered)
-
-    message_rows = message.shape[0]
-    pair_shape = (PAIRS, 2, message_rows, columns)
+    )(
+        expert_index.astype(jnp.int32).reshape(1),
+        queries,
+        gathered.reshape(2, expert_count, message_rows, half_columns),
+    )
+
+    attended_other = lax.ppermute(attended, "tensor", NEIGHBOUR)
+    pair_shape = (2, PAIRS, 2, message_rows, half_columns)
     gathered, gathered_other = gathered.reshape(pair_shape), gathered_other.reshape(pair_shape)
-    wide = 4
-
-    def projected(parity, dtype):
+    wide = 8
+
+    def projected(source, rows, dtype, *before):
         weight_spec = pl.BlockSpec(
-            (wide, 1, half_rows, columns), lambda i, core_ref, parity_ref: (i, parity_ref[0], 0, 0)
+            (1, wide, 2, half_rows, half_columns),
+            lambda i, core_ref, source_ref: (source_ref[0], i, 0, 0, 0),
         )
         return pl.pallas_call(
-            project,
+            functools.partial(project, bool(before)),
             out_shape=jax.ShapeDtypeStruct((PAIRS, tokens, columns), dtype),
             grid_spec=pltpu.PrefetchScalarGridSpec(
                 num_scalar_prefetch=2,
                 grid=(PAIRS // wide,),
-                in_specs=[whole(2, tokens, half_rows), weight_spec, weight_spec],
-                out_specs=pl.BlockSpec((wide, tokens, columns), lambda i, *_: (i, 0, 0)),
+                in_specs=[HERE, weight_spec, weight_spec] + [HERE] * len(before),
+                out_specs=HERE,
             ),
             compiler_params=LIMIT,
             cost_estimate=cost(4 * tokens * half_rows * PAIRS * columns, 4 * half_rows * PAIRS * columns),
             name="project",
-        )(core.reshape(1), parity.reshape(1), attended, gathered, gathered_other)
-
-    given = lax.ppermute(projected(1 - odd, jnp.bfloat16), "tensor", NEIGHBOUR)
-    kept = projected(odd, jnp.float32)
-    pair_sums = (kept + given.astype(jnp.float32)).astype(jnp.bfloat16)
+        )(core.reshape(1), source.reshape(1), rows, gathered, gathered_other, *before)
+
+    kept = projected(odd, attended, jnp.float32)
+    pair_sums = projected(1 - odd, attended_other, jnp.bfloat16, kept)
     partial_sums = exchange(pair_sums, "tensor", PARITY)
     head_total = jnp.sum(partial_sums.astype(jnp.float32), axis=0)
-    residual_share = lax.dynamic_slice_in_dim(residual, tensor_index * columns, columns, 1)
+    pair_start = tensor_index // 2 * 2 * columns + odd * half_columns
+    residual_share = jnp.concatenate(
+        [
+            lax.dynamic_slice_in_dim(residual, pair_start + side * columns, half_columns, 1)
+            for side in range(2)
+        ],
+        axis=1,
+    )
     hidden_share = residual_share.astype(jnp.float32) + head_total
     rows_own = spread(hidden_share.astype(jnp.bfloat16), "tensor", PAIRS, PARITY)
     rows_own, weights = lax.optimization_barrier((rows_own, weights))
@@ -300,7 +342,9 @@
     weights = weights.reshape(2 * expert_count, blocks // 2, 2, local_units, columns)
 
     per_step = 4
-    gains = post_gain.reshape(PAIRS, 2, 1, columns)
+    gains = jnp.transpose(post_gain.reshape(PAIRS, 2, 2, half_columns), (0, 2, 1, 3)).reshape(
+        PAIRS, 2, 1, columns
+    )
     totals_types = [
         jax.ShapeDtypeStruct((2, expert_count * local_units, tokens), jnp.float32),
         jax.ShapeDtypeStruct((tokens, 1), jnp.float32),
@@ -386,7 +430,16 @@
             name="down",
         )(parity.reshape(1), rows, routes, route_weight, start, *[weights] * (2 * parts))
 
-    mixed = lowered(odd, activation_own, hidden_share, jnp.float32)
+    shares = [
+        lax.dynamic_slice(
+            rows, (tensor_index // 2, 0, odd * half_columns), (1, tokens, half_columns)
+        )[0].astype(jnp.float32)
+        for rows in (rows_own, rows_other)
+    ]
+    hidden_here = jnp.where(
+        odd == 0, jnp.concatenate(shares, axis=1), jnp.concatenate(shares[::-1], axis=1)
+    )
+    mixed = lowered(odd, activation_own, hidden_here, jnp.float32)
     return lowered(1 - odd, activation_other, mixed, jnp.bfloat16)
 
 

time: 260 us -> 263 us (1.012)
  the two profiles are of different devices: /device:TPU:1 before, /device:TPU:64 now
where the time goes in v8:
time: 263 us
  waiting for transfers between devices  87.6 us (33%)
  blocking collectives  83 us (32%)
  starting transfers between devices  38.6 us (15%)
  Pallas kernels  30.6 us (12%)
  between operations  13.7 us (5%)
  local copies, waits for them, and re-layouts  6.54 us (2%)
    all_to_all x2, blocking collectives, exchange(): lax.all_to_all(message, axis, split_axis=0, concat_axis=0, tiled=True, ax...  83 us
    all_to_all x2, waiting for transfers between devices, exchange(): lax.all_to_all(message, axis, split_axis=0, concat_axis=0, tiled=True, ax...  54.7 us
    all_to_all x2, starting transfers between devices, exchange(): lax.all_to_all(message, axis, split_axis=0, concat_axis=0, tiled=True, ax...  27.6 us
    all_gather x1, waiting for transfers between devices, local(): weights = lax.all_gather(weights_here, ('dp', 'expert'), axis=0)  19.1 us
    pallas_call x2, Pallas kernels, gated(): pl.pallas_call(functools.partial(gate_up, last), out_shape=out_type if la...  13.7 us
    pallas_call x2, Pallas kernels, lowered(): pl.pallas_call(functools.partial(down, parts), out_shape=jax.ShapeDtypeSt...  8.98 us
    ppermute x1, waiting for transfers between devices, local(): activation_other = lax.ppermute(activation_own, 'tensor', NEIGHBOUR)  6.44 us
    ppermute x1, waiting for transfers between devices, local(): rows_other = lax.ppermute(rows_own, 'tensor', NEIGHBOUR)  5.86 us
  transfers between devices with their start and end apart: 7, of which 6 were waited for; matrix products, arithmetic and copies ran while one was open for 1% of the time, Pallas kernels for 7%

profile of v8, /device:TPU:64, one launch (start us, length us, event | category | flops | bytes accessed | tf_op | source)
XLA Modules:
  0.0 262.6 jit_solution(3499789698847067595)
XLA Ops:
  6.5 0.0 copy-start
  6.5 0.0 all-gather.3.cloned.1.call-start
  6.5 1.3 select_bitcast_fusion
  7.8 0.6 reshape.80
  8.4 0.6 copy.16
  9.0 0.1 copy.24
  9.1 0.0 copy-start.3
  9.1 0.0 copy-done
  9.2 1.1 pad_maximum_fusion
  10.3 0.0 all-gather.3.cloned.1.call-update
  10.3 0.9 dynamic_slice.32
  11.2 0.8 dynamic_slice.31
  12.0 0.0 copy-done.3
  12.1 0.7 broadcast_in_dim.6
  12.8 58.1 %all_to_all.20 = bf16[32,384,128]{2,1,0:T(8,128)(2,1)} all-to-all(bf16[32,384,128]{2,1,0:T(8,128)(2,1)S(1)} %bitcast.52), channel_id=1, replica_groups={{0,1,2,3,4,5,6,7,8,9,10,11,12,13,14,15,16,17,18,19,20,21,22,23,24,25,26..., dimensions={0} | all-to-all | bytes 6291456 | tf_op jit(solution)/shard_map/all_to_all | solution.py:199
  70.9 1.9 collective-permute-start.1
  72.9 3.1 %attend.1.attended_ref = bf16[2,128,256]{2,1,0:T(8,128)(2,1)} custom-call(s32[1]{0:T(128)} %bitcast.2.place_ref, bf16[128,512]{1,0:T(8,128)(2,1)} %query_ref.1, bf16[2,16,384,128]{3,2,1,0:T(8,128)(2,1)} %bitcast.6.piece_ref), custom_call_target="tpu_custom_call" | custom-call | tf_op jit(solution)/shard_map/attend/pallas_call | solution.py:282
  76.0 3.5 %collective-permute-start = (bf16[2,128,256]{2,1,0:T(8,128)(2,1)}, bf16[2,128,256]{2,1,0:T(8,128)(2,1)S(1)}, u32[]{:S(2)}, u32[]{:S(2)}) collective-permute-start(bf16[2,128,256]{2,1,0:T(8,128)(2,1)} %attend.1.attended_ref), channel_id=1, source_target_pairs={{0,16},{16,0},{32,48},{48,32},{64,80},{80,64},{96,112},{112,96},{1... | collective-permute-start | bytes 393224 | tf_op jit(solution)/shard_map/ppermute | solution.py:302
  79.5 0.0 collective-permute-done.1
  79.5 0.0 copy-start.1
  79.6 0.9 copy-done.1
  80.5 2.0 project.2.refs_0_
  82.5 1.5 collective-permute-done.attended_ref
  84.0 2.9 %project.3 = bf16[8,128,256]{2,1,0:T(8,128)(2,1)} custom-call(s32[1]{0:T(128)} %bitcast.1.core_ref, s32[1]{0:T(128)} %bitcast.source_ref.scalar_ref, bf16[2,128,256]{2,1,0:T(8,128)(2,1)S(1)} %collective-permute-done.attended_ref, bf16[2,8,2,384,128]{4,3,2,1,0:T(8,128)(2,1)} %bitcast.7.own_ref, bf16[2,8,2,384,128]{4,3,2,1,0:T(8,128)(2,1)} %bitcast.8.other_ref, ...), custom_call_target="tpu_custom_call" | custom-call | flops 268435456 | bytes 2097152 | tf_op jit(solution)/shard_map/project/pallas_call | solution.py:312
  86.8 0.0 copy-start.4
  86.8 15.1 %all-to-all-start.1 = ((bf16[8,128,256]{2,1,0:T(8,128)(2,1)}), bf16[8,128,256]{2,1,0:T(8,128)(2,1)S(1)}, u32[]{:S(2)}, u32[]{:S(2)}) async-start(bf16[8,128,256]{2,1,0:T(8,128)(2,1)} %project.3), calls=%async_computation.1 | async-start | bytes 1048576 | tf_op jit(solution)/shard_map/all_to_all | solution.py:199
  101.9 0.8 constant_dynamic-slice_fusion.2
  102.7 29.7 %all-to-all-done.1 = bf16[8,128,256]{2,1,0:T(8,128)(2,1)S(1)} async-done(((bf16[8,128,256]{2,1,0:T(8,128)(2,1)}), bf16[8,128,256]{2,1,0:T(8,128)(2,1)S(1)}, u32[]{:S(2)}, u32[]{:S(2)}) %all-to-all-start.1) | async-done | bytes 524320 | tf_op jit(solution)/shard_map/all_to_all | solution.py:199
  132.4 0.1 convert_reduce_fusion
  132.5 24.9 %all_to_all.21.rows_ref = bf16[8,128,256]{2,1,0:T(8,128)(2,1)S(1)} all-to-all(bf16[8,128,256]{2,1,0:T(8,128)(2,1)S(1)} %broadcast_in_dim.7), channel_id=1, replica_groups={{0,32,64,96,128,160,192,224},{16,48,80,112,144,176,208,240},{1,33,65,97..., dimensions={0} | all-to-all | bytes 1048576 | tf_op jit(solution)/shard_map/all_to_all | solution.py:199
  157.4 19.1 %all-gather.3.cloned.1.call-done = bf16[73728,256]{1,0:T(8,128)(2,1)} async-done(((bf16[2304,256]{1,0:T(8,128)(2,1)}), bf16[73728,256]{1,0:T(8,128)(2,1)}) %all-gather.3.cloned.1.call-update) | async-done | bytes 37748752 | tf_op jit(solution)/shard_map/all_gather | solution.py:272
  176.6 3.5 %collective-permute-start.2 = (bf16[8,128,256]{2,1,0:T(8,128)(2,1)S(1)}, bf16[8,128,256]{2,1,0:T(8,128)(2,1)S(1)}, u32[]{:S(2)}, u32[]{:S(2)}) collective-permute-start(bf16[8,128,256]{2,1,0:T(8,128)(2,1)S(1)} %all_to_all.21.rows_ref), channel_id=1, source_target_pairs={{0,16},{16,0},{32,48},{48,32},{64,80},{80,64},{96,112},{112,96},{1... | collective-permute-start | bytes 1572872 | tf_op jit(solution)/shard_map/ppermute | solution.py:341
  180.0 0.0 copy-done.4
  180.0 0.0 copy-start.2
  180.1 6.6 %gate_up.2 = (f32[2,1536,128]{2,1,0:T(8,128)S(1)}, f32[128,1]{1,0:T(8,128)S(1)}) custom-call(s32[1]{0:T(128)} %bitcast.9.source_ref.scalar_ref, bf16[8,128,256]{2,1,0:T(8,128)(2,1)S(1)} %all_to_all.21.rows_ref, f32[8,2,1,256]{3,2,1,0:T(1,128)S(1)} %bitcast.37, bf16[32,12,2,96,256]{4,3,2,1,0:T(8,128)(2,1)} %bitcast.40, bf16[32,12,2,96,256]{4,3,2,1,0:T(8,128)(2,1)} %bitcast.41), custom_call_target="tpu_custom_call" | custom-call | flops 1610612736 | bytes 12582912 | tf_op jit(solution)/shard_map/gate_up/pallas_call | solution.py:365
  186.7 5.9 %collective-permute-done.2.rows_ref = bf16[8,128,256]{2,1,0:T(8,128)(2,1)S(1)} collective-permute-done((bf16[8,128,256]{2,1,0:T(8,128)(2,1)S(1)}, bf16[8,128,256]{2,1,0:T(8,128)(2,1)S(1)}, u32[]{:S(2)}, u32[]{:S(2)}) %collective-permute-start.2) | collective-permute-done | bytes 524320 | tf_op jit(solution)/shard_map/ppermute | solution.py:341
  192.5 0.0 copy-done.2
  192.5 0.0 copy-start.5
  192.5 7.1 %gate_up.3 = bf16[192,128]{1,0:T(8,128)(2,1)S(1)} custom-call(s32[1]{0:T(128)} %bitcast.source_ref.scalar_ref, bf16[8,128,256]{2,1,0:T(8,128)(2,1)S(1)} %collective-permute-done.2.rows_ref, f32[8,2,1,256]{3,2,1,0:T(1,128)S(1)} %bitcast.38, bf16[32,12,2,96,256]{4,3,2,1,0:T(8,128)(2,1)} %bitcast.42, bf16[32,12,2,96,256]{4,3,2,1,0:T(8,128)(2,1)} %bitcast.43, ...), custom_call_target="tpu_custom_call" | custom-call | flops 1610612736 | bytes 12582912 | tf_op jit(solution)/shard_map/gate_up/pallas_call | solution.py:365
  199.6 0.8 broadcast_in_dim.8
  200.4 12.6 %all-to-all-start.3 = ((bf16[8,192,128]{2,1,0:T(8,128)(2,1)}), bf16[8,192,128]{2,1,0:T(8,128)(2,1)S(1)}, u32[]{:S(2)}, u32[]{:S(2)}) async-start(bf16[8,192,128]{2,1,0:T(8,128)(2,1)} %broadcast_in_dim.8), calls=%async_computation.3 | async-start | bytes 786432 | tf_op jit(solution)/shard_map/all_to_all | solution.py:199
  213.0 0.1 copy.20.routes_ref
  213.1 0.0 copy-done.5
  213.1 0.1 copy.21.route_weight_ref
  213.2 24.9 %all-to-all-done.3.activation_ref = bf16[8,192,128]{2,1,0:T(8,128)(2,1)S(1)} async-done(((bf16[8,192,128]{2,1,0:T(8,128)(2,1)}), bf16[8,192,128]{2,1,0:T(8,128)(2,1)S(1)}, u32[]{:S(2)}, u32[]{:S(2)}) %all-to-all-start.3) | async-done | bytes 393248 | tf_op jit(solution)/shard_map/all_to_all | solution.py:199
  238.1 2.1 collective-permute-start.3
  240.3 4.2 %down.2.start_ref = f32[128,256]{1,0:T(8,128)S(1)} custom-call(s32[1]{0:T(128)} %bitcast.9.source_ref.scalar_ref, bf16[8,192,128]{2,1,0:T(8,128)(2,1)S(1)} %all-to-all-done.3.activation_ref, s32[128,2]{1,0:T(8,128)S(1)} %copy.20.routes_ref, f32[128,2]{1,0:T(8,128)S(1)} %copy.21.route_weight_ref, f32[128,256]{1,0:T(8,128)S(1)} %maximum_select_fusion.start_ref, ...), custom_call_target="tpu_custom_call" | custom-call | flops 805306368 | bytes 6291456 | tf_op jit(solution)/shard_map/down/pallas_call | solution.py:406
  244.5 6.4 %collective-permute-done.3.activation_ref = bf16[8,192,128]{2,1,0:T(8,128)(2,1)S(1)} collective-permute-done((bf16[8,192,128]{2,1,0:T(8,128)(2,1)S(1)}, bf16[8,192,128]{2,1,0:T(8,128)(2,1)S(1)}, u32[]{:S(2)}, u32[]{:S(2)}) %collective-permute-start.3) | collective-permute-done | bytes 393248 | tf_op jit(solution)/shard_map/ppermute | solution.py:387
  251.0 4.8 %down.3 = bf16[128,256]{1,0:T(8,128)(2,1)} custom-call(s32[1]{0:T(128)} %bitcast.source_ref.scalar_ref, bf16[8,192,128]{2,1,0:T(8,128)(2,1)S(1)} %collective-permute-done.3.activation_ref, s32[128,2]{1,0:T(8,128)S(1)} %copy.20.routes_ref, f32[128,2]{1,0:T(8,128)S(1)} %copy.21.route_weight_ref, f32[128,256]{1,0:T(8,128)S(1)} %down.2.start_ref, ...), custom_call_target="tpu_custom_call" | custom-call | flops 805306368 | bytes 6291456 | tf_op jit(solution)/shard_map/down/pallas_call | solution.py:406
  (10 shorter events, 0.2 us)
Async XLA Ops:
  6.5 2.6 copy-start
  6.5 170.0 %all-gather.3.cloned.1.call-start = ((), (), s32[]{:S(2)}) async-start(), calls=%async_computation.4 | async-start | bytes 38928384 | tf_op jit(solution)/shard_map/all_gather | solution.py:272
  9.1 2.9 %copy-start.3 = (bf16[512,256]{1,0:T(8,128)(2,1)S(1)}, bf16[512,256]{1,0:T(8,128)(2,1)}, u32[]{:S(2)}) copy-start(bf16[512,256]{1,0:T(8,128)(2,1)} %param.14) | copy-start | bytes 786436
  70.9 8.6 %collective-permute-start.1 = (bf16[32,384,128]{2,1,0:T(8,128)(2,1)}, bf16[32,384,128]{2,1,0:T(8,128)(2,1)}, u32[]{:S(2)}, u32[]{:S(2)}) collective-permute-start(bf16[32,384,128]{2,1,0:T(8,128)(2,1)} %all_to_all.20), channel_id=1, source_target_pairs={{0,256},{256,0},{1,257},{257,1},{2,258},{258,2},{3,259},{259,3},{4... | collective-permute-start | bytes 9437192 | tf_op jit(solution)/shard_map/ppermute | solution.py:280
  76.0 8.0 %collective-permute-start = (bf16[2,128,256]{2,1,0:T(8,128)(2,1)}, bf16[2,128,256]{2,1,0:T(8,128)(2,1)S(1)}, u32[]{:S(2)}, u32[]{:S(2)}) collective-permute-start(bf16[2,128,256]{2,1,0:T(8,128)(2,1)} %attend.1.attended_ref), channel_id=1, source_target_pairs={{0,16},{16,0},{32,48},{48,32},{64,80},{80,64},{96,112},{112,96},{1... | collective-permute-start | bytes 393224 | tf_op jit(solution)/shard_map/ppermute | solution.py:302
  79.5 0.9 copy-start.1
  86.8 93.2 %copy-start.4 = (f32[4096]{0:T(1024)S(1)}, f32[4096]{0:T(1024)}, u32[]{:S(2)}) copy-start(f32[4096]{0:T(1024)} %param.16) | copy-start | bytes 49156
  86.8 45.6 %all-to-all-start.1 = ((bf16[8,128,256]{2,1,0:T(8,128)(2,1)}), bf16[8,128,256]{2,1,0:T(8,128)(2,1)S(1)}, u32[]{:S(2)}, u32[]{:S(2)}) async-start(bf16[8,128,256]{2,1,0:T(8,128)(2,1)} %project.3), calls=%async_computation.1 | async-start | bytes 1048576 | tf_op jit(solution)/shard_map/all_to_all | solution.py:199
  176.6 16.0 %collective-permute-start.2 = (bf16[8,128,256]{2,1,0:T(8,128)(2,1)S(1)}, bf16[8,128,256]{2,1,0:T(8,128)(2,1)S(1)}, u32[]{:S(2)}, u32[]{:S(2)}) collective-permute-start(bf16[8,128,256]{2,1,0:T(8,128)(2,1)S(1)} %all_to_all.21.rows_ref), channel_id=1, source_target_pairs={{0,16},{16,0},{32,48},{48,32},{64,80},{80,64},{96,112},{112,96},{1... | collective-permute-start | bytes 1572872 | tf_op jit(solution)/shard_map/ppermute | solution.py:341
  180.0 12.5 %copy-start.2 = (s32[128,2]{0,1:T(2,128)S(1)}, s32[128,2]{0,1:T(2,128)}, u32[]{:S(2)}) copy-start(s32[128,2]{0,1:T(2,128)} %param.17) | copy-start | bytes 3076
  192.5 20.6 %copy-start.5 = (f32[128,2]{0,1:T(2,128)S(1)}, f32[128,2]{0,1:T(2,128)}, u32[]{:S(2)}) copy-start(f32[128,2]{0,1:T(2,128)} %param.18) | copy-start | bytes 3076
  200.4 37.7 %all-to-all-start.3 = ((bf16[8,192,128]{2,1,0:T(8,128)(2,1)}), bf16[8,192,128]{2,1,0:T(8,128)(2,1)S(1)}, u32[]{:S(2)}, u32[]{:S(2)}) async-start(bf16[8,192,128]{2,1,0:T(8,128)(2,1)} %broadcast_in_dim.8), calls=%async_computation.3 | async-start | bytes 786432 | tf_op jit(solution)/shard_map/all_to_all | solution.py:199
  238.1 12.8 %collective-permute-start.3 = (bf16[8,192,128]{2,1,0:T(8,128)(2,1)S(1)}, bf16[8,192,128]{2,1,0:T(8,128)(2,1)S(1)}, u32[]{:S(2)}, u32[]{:S(2)}) collective-permute-start(bf16[8,192,128]{2,1,0:T(8,128)(2,1)S(1)} %all-to-all-done.3.activation_ref), channel_id=1, source_target_pairs={{0,16},{16,0},{32,48},{48,32},{64,80},{80,64},{96,112},{112,96},{1... | collective-permute-start | bytes 1179656 | tf_op jit(solution)/shard_map/ppermute | solution.py:387
Sparse Core Ops, SparseCore 0:
  10.5 166.0 all-gather.2

commit v9 on v8

--- a/solution.py
+++ b/solution.py
@@ -234,17 +234,13 @@
     local_units = gate_weight.shape[2]
 
     first_blocks = D // columns
-    down_blocks = half_units // local_units
-    blocks = first_blocks + down_blocks
 
     gate_or_up = jnp.where(core == 0, gate_weight[0], up_weight[0]).T
     gate_or_up = jnp.transpose(
         gate_or_up.reshape(local_units, PAIRS, 2, 2, columns // 2), (1, 3, 0, 2, 4)
     )
     down_half = lax.dynamic_slice_in_dim(down_weight[0], core * half_units, half_units, 0)
-    weights_here = jnp.concatenate(
-        [gate_or_up.reshape(first_blocks * local_units, columns), down_half], axis=0
-    )
+    gate_or_up = gate_or_up.reshape(first_blocks * local_units, columns)
 
     shared = tensor_index * local_heads // group_width
     key_head = lax.dynamic_slice_in_dim(all_key_rows, shared * HEAD_WIDTH, HEAD_WIDTH, 1)
@@ -269,7 +265,8 @@
         [(2 * pair + side) * expert_count + place for side in range(2) for place in range(expert_count)]
         for pair in range(PAIRS)
     ]
-    weights = lax.all_gather(weights_here, ("dp", "expert"), axis=0)
+    weights = lax.all_gather(gate_or_up, ("dp", "expert"), axis=0)
+    down_weights = lax.all_gather(down_half, ("dp", "expert"), axis=0)
     gathered = exchange(
         jnp.broadcast_to(message[:, None], (2, expert_count) + message.shape[1:]).reshape(
             2 * expert_count, message_rows, half_columns
@@ -339,7 +336,7 @@
     rows_own = spread(hidden_share.astype(jnp.bfloat16), "tensor", PAIRS, PARITY)
     rows_own, weights = lax.optimization_barrier((rows_own, weights))
     rows_other = lax.ppermute(rows_own, "tensor", NEIGHBOUR)
-    weights = weights.reshape(2 * expert_count, blocks // 2, 2, local_units, columns)
+    weights = weights.reshape(2 * expert_count, PAIRS, 2, local_units, columns)
 
     per_step = 4
     gains = jnp.transpose(post_gain.reshape(PAIRS, 2, 2, half_columns), (0, 2, 1, 3)).reshape(
@@ -389,13 +386,14 @@
     per_part = 4
     down_steps = expert_count // (parts * per_part)
     quarter = PAIRS // 2
+    down_weights = down_weights.reshape(2 * expert_count, quarter, 2, local_units, columns)
 
     def down_spec(half, part):
         return pl.BlockSpec(
             (per_part, quarter, 1, local_units, columns),
             lambda i, scalar_ref: (
                 (half * down_steps + i) * parts + part,
-                first_blocks // (2 * quarter),
+                0,
                 scalar_ref[0],
                 0,
                 0,
@@ -428,7 +426,7 @@
                 2 * expert_count * hidden_units * columns // 2,
             ),
             name="down",
-        )(parity.reshape(1), rows, routes, route_weight, start, *[weights] * (2 * parts))
+        )(parity.reshape(1), rows, routes, route_weight, start, *[down_weights] * (2 * parts))
 
     shares = [
         lax.dynamic_slice(

time: 263 us -> 249 us (0.947)
  the two profiles are of different devices: /device:TPU:64 before, /device:TPU:1 now
where the time goes in v9:
time: 249 us; the launch traced here: 248 us
  blocking collectives  85.5 us (34%)
  waiting for transfers between devices  56.4 us (23%)
  starting transfers between devices  47.9 us (19%)
  Pallas kernels  27.8 us (11%)
  local copies, waits for them, and re-layouts  14.9 us (6%)
  between operations  13.7 us (6%)
    all_to_all x2, blocking collectives, exchange(): lax.all_to_all(message, axis, split_axis=0, concat_axis=0, tiled=True, ax...  85.5 us
    all_to_all x2, waiting for transfers between devices, exchange(): lax.all_to_all(message, axis, split_axis=0, concat_axis=0, tiled=True, ax...  43.2 us
    all_to_all x2, starting transfers between devices, exchange(): lax.all_to_all(message, axis, split_axis=0, concat_axis=0, tiled=True, ax...  18.4 us
    ppermute x1, starting transfers between devices, local(): rows_other = lax.ppermute(rows_own, 'tensor', NEIGHBOUR)  14.5 us
    pallas_call x2, Pallas kernels, gated(): pl.pallas_call(functools.partial(gate_up, last), out_shape=out_type if la...  13.7 us
    ppermute x1, starting transfers between devices, local(): gathered_other = lax.ppermute(gathered, 'dp', SWAP)  8.34 us
    unnamed x18, local copies, waits for them, and re-layouts  7.55 us
    all_gather x1, waiting for transfers between devices, local(): down_weights = lax.all_gather(down_half, ('dp', 'expert'), axis=0)  6.65 us
  transfers between devices with their start and end apart: 8, of which 5 were waited for; matrix products, arithmetic and copies ran while one was open for 2% of the time, Pallas kernels for 10%

profile of v9, /device:TPU:1, one launch (start us, length us, event | category | flops | bytes accessed | tf_op | source)
XLA Modules:
  0.0 247.7 jit_solution(8400164791509554025)
XLA Ops:
  6.5 0.0 copy-start
  6.5 0.0 all-gather.3.cloned.1.call-start
  6.5 1.3 select_bitcast_fusion
  7.8 0.0 copy-start.5
  7.8 0.6 reshape.81
  8.4 0.6 copy.30
  9.0 1.4 all_gather_reshape.3
  10.4 0.0 all-gather.3.cloned.1.call-update
  10.4 0.0 all-gather.5.cloned.1.call-start
  10.5 0.0 copy-done
  10.5 0.8 constant_dynamic-slice_fusion.1
  11.3 0.0 all-gather.5.cloned.1.call-update
  11.3 0.9 dynamic_slice.30
  12.2 0.8 dynamic_slice.29
  13.0 0.0 copy-done.5
  13.1 0.7 broadcast_in_dim.6
  13.8 53.6 %all_to_all.20 = bf16[32,384,128]{2,1,0:T(8,128)(2,1)} all-to-all(bf16[32,384,128]{2,1,0:T(8,128)(2,1)S(1)} %bitcast.47), channel_id=1, replica_groups={{0,1,2,3,4,5,6,7,8,9,10,11,12,13,14,15,16,17,18,19,20,21,22,23,24,25,26..., dimensions={0} | all-to-all | bytes 6291456 | tf_op jit(solution)/shard_map/all_to_all | solution.py:199
  67.5 8.3 %collective-permute-start.1 = (bf16[32,384,128]{2,1,0:T(8,128)(2,1)}, bf16[32,384,128]{2,1,0:T(8,128)(2,1)}, u32[]{:S(2)}, u32[]{:S(2)}) collective-permute-start(bf16[32,384,128]{2,1,0:T(8,128)(2,1)} %all_to_all.20), channel_id=1, source_target_pairs={{0,256},{256,0},{1,257},{257,1},{2,258},{258,2},{3,259},{259,3},{4... | collective-permute-start | bytes 9437192 | tf_op jit(solution)/shard_map/ppermute | solution.py:277
  75.8 3.1 %attend.1.attended_ref = bf16[2,128,256]{2,1,0:T(8,128)(2,1)} custom-call(s32[1]{0:T(128)} %bitcast.2.place_ref, bf16[128,512]{1,0:T(8,128)(2,1)} %query_ref.1, bf16[2,16,384,128]{3,2,1,0:T(8,128)(2,1)} %bitcast.6.piece_ref), custom_call_target="tpu_custom_call" | custom-call | tf_op jit(solution)/shard_map/attend/pallas_call | solution.py:279
  78.9 2.8 %collective-permute-start = (bf16[2,128,256]{2,1,0:T(8,128)(2,1)}, bf16[2,128,256]{2,1,0:T(8,128)(2,1)S(1)}, u32[]{:S(2)}, u32[]{:S(2)}) collective-permute-start(bf16[2,128,256]{2,1,0:T(8,128)(2,1)} %attend.1.attended_ref), channel_id=1, source_target_pairs={{0,16},{16,0},{32,48},{48,32},{64,80},{80,64},{96,112},{112,96},{1... | collective-permute-start | bytes 393224 | tf_op jit(solution)/shard_map/ppermute | solution.py:299
  81.8 0.0 collective-permute-done.1
  81.8 0.0 copy-start.3
  81.8 0.9 copy-done.3
  82.7 2.0 project.2.refs_0_
  84.7 1.4 collective-permute-done.attended_ref
  86.1 2.8 %project.3 = bf16[8,128,256]{2,1,0:T(8,128)(2,1)} custom-call(s32[1]{0:T(128)} %bitcast.1.core_ref, s32[1]{0:T(128)} %bitcast.source_ref.scalar_ref, bf16[2,128,256]{2,1,0:T(8,128)(2,1)S(1)} %collective-permute-done.attended_ref, bf16[2,8,2,384,128]{4,3,2,1,0:T(8,128)(2,1)} %bitcast.7.own_ref, bf16[2,8,2,384,128]{4,3,2,1,0:T(8,128)(2,1)} %bitcast.8.other_ref, ...), custom_call_target="tpu_custom_call" | custom-call | flops 268435456 | bytes 2097152 | tf_op jit(solution)/shard_map/project/pallas_call | solution.py:309
  89.0 0.0 copy-start.6
  89.0 14.8 %all-to-all-start.1 = ((bf16[8,128,256]{2,1,0:T(8,128)(2,1)}), bf16[8,128,256]{2,1,0:T(8,128)(2,1)S(1)}, u32[]{:S(2)}, u32[]{:S(2)}) async-start(bf16[8,128,256]{2,1,0:T(8,128)(2,1)} %project.3), calls=%async_computation.1 | async-start | bytes 1048576 | tf_op jit(solution)/shard_map/all_to_all | solution.py:199
  103.7 0.8 constant_dynamic-slice_fusion.3
  104.5 22.7 %all-to-all-done.1 = bf16[8,128,256]{2,1,0:T(8,128)(2,1)S(1)} async-done(((bf16[8,128,256]{2,1,0:T(8,128)(2,1)}), bf16[8,128,256]{2,1,0:T(8,128)(2,1)S(1)}, u32[]{:S(2)}, u32[]{:S(2)}) %all-to-all-start.1) | async-done | bytes 524320 | tf_op jit(solution)/shard_map/all_to_all | solution.py:199
  127.2 0.1 convert_reduce_fusion
  127.3 31.9 %all_to_all.21.rows_ref = bf16[8,128,256]{2,1,0:T(8,128)(2,1)S(1)} all-to-all(bf16[8,128,256]{2,1,0:T(8,128)(2,1)S(1)} %broadcast_in_dim.7), channel_id=1, replica_groups={{0,32,64,96,128,160,192,224},{16,48,80,112,144,176,208,240},{1,33,65,97..., dimensions={0} | all-to-all | bytes 1048576 | tf_op jit(solution)/shard_map/all_to_all | solution.py:199
  159.2 0.0 all-gather.3.cloned.1.call-done
  159.2 14.5 %collective-permute-start.2 = (bf16[8,128,256]{2,1,0:T(8,128)(2,1)S(1)}, bf16[8,128,256]{2,1,0:T(8,128)(2,1)S(1)}, u32[]{:S(2)}, u32[]{:S(2)}) collective-permute-start(bf16[8,128,256]{2,1,0:T(8,128)(2,1)S(1)} %all_to_all.21.rows_ref), channel_id=1, source_target_pairs={{0,16},{16,0},{32,48},{48,32},{64,80},{80,64},{96,112},{112,96},{1... | collective-permute-start | bytes 1572872 | tf_op jit(solution)/shard_map/ppermute | solution.py:338
  173.7 0.0 copy-done.6
  173.7 0.0 copy-start.4
  173.7 6.6 %gate_up.2 = (f32[2,1536,128]{2,1,0:T(8,128)S(1)}, f32[128,1]{1,0:T(8,128)S(1)}) custom-call(s32[1]{0:T(128)} %bitcast.9.source_ref.scalar_ref, bf16[8,128,256]{2,1,0:T(8,128)(2,1)S(1)} %all_to_all.21.rows_ref, f32[8,2,1,256]{3,2,1,0:T(1,128)S(1)} %bitcast.40, bf16[32,8,2,96,256]{4,3,2,1,0:T(8,128)(2,1)} %bitcast.43, bf16[32,8,2,96,256]{4,3,2,1,0:T(8,128)(2,1)} %bitcast.44), custom_call_target="tpu_custom_call" | custom-call | flops 1610612736 | bytes 12582912 | tf_op jit(solution)/shard_map/gate_up/pallas_call | solution.py:362
  180.4 5.1 %collective-permute-done.2.rows_ref = bf16[8,128,256]{2,1,0:T(8,128)(2,1)S(1)} collective-permute-done((bf16[8,128,256]{2,1,0:T(8,128)(2,1)S(1)}, bf16[8,128,256]{2,1,0:T(8,128)(2,1)S(1)}, u32[]{:S(2)}, u32[]{:S(2)}) %collective-permute-start.2) | collective-permute-done | bytes 524320 | tf_op jit(solution)/shard_map/ppermute | solution.py:338
  185.5 0.0 copy-done.4
  185.5 0.0 copy-start.7
  185.5 7.1 %gate_up.3 = bf16[192,128]{1,0:T(8,128)(2,1)S(1)} custom-call(s32[1]{0:T(128)} %bitcast.source_ref.scalar_ref, bf16[8,128,256]{2,1,0:T(8,128)(2,1)S(1)} %collective-permute-done.2.rows_ref, f32[8,2,1,256]{3,2,1,0:T(1,128)S(1)} %bitcast.41, bf16[32,8,2,96,256]{4,3,2,1,0:T(8,128)(2,1)} %bitcast.45, bf16[32,8,2,96,256]{4,3,2,1,0:T(8,128)(2,1)} %bitcast.46, ...), custom_call_target="tpu_custom_call" | custom-call | flops 1610612736 | bytes 12582912 | tf_op jit(solution)/shard_map/gate_up/pallas_call | solution.py:362
  192.6 0.8 broadcast_in_dim.8
  193.4 3.6 %all-to-all-start.3 = ((bf16[8,192,128]{2,1,0:T(8,128)(2,1)}), bf16[8,192,128]{2,1,0:T(8,128)(2,1)S(1)}, u32[]{:S(2)}, u32[]{:S(2)}) async-start(bf16[8,192,128]{2,1,0:T(8,128)(2,1)} %broadcast_in_dim.8), calls=%async_computation.3 | async-start | bytes 786432 | tf_op jit(solution)/shard_map/all_to_all | solution.py:199
  197.0 0.1 copy.27.routes_ref
  197.2 0.0 copy-done.7
  197.2 0.1 copy.28.route_weight_ref
  197.3 20.5 %all-to-all-done.3.activation_ref = bf16[8,192,128]{2,1,0:T(8,128)(2,1)S(1)} async-done(((bf16[8,192,128]{2,1,0:T(8,128)(2,1)}), bf16[8,192,128]{2,1,0:T(8,128)(2,1)S(1)}, u32[]{:S(2)}, u32[]{:S(2)}) %all-to-all-start.3) | async-done | bytes 393248 | tf_op jit(solution)/shard_map/all_to_all | solution.py:199
  217.8 3.8 %collective-permute-start.3 = (bf16[8,192,128]{2,1,0:T(8,128)(2,1)S(1)}, bf16[8,192,128]{2,1,0:T(8,128)(2,1)S(1)}, u32[]{:S(2)}, u32[]{:S(2)}) collective-permute-start(bf16[8,192,128]{2,1,0:T(8,128)(2,1)S(1)} %all-to-all-done.3.activation_ref), channel_id=1, source_target_pairs={{0,16},{16,0},{32,48},{48,32},{64,80},{80,64},{96,112},{112,96},{1... | collective-permute-start | bytes 1179656 | tf_op jit(solution)/shard_map/ppermute | solution.py:384
  221.6 6.7 %all-gather.5.cloned.1.call-done = bf16[32,768,256]{2,1,0:T(8,128)(2,1)} async-done(((bf16[1,768,256]{2,1,0:T(8,128)(2,1)}), bf16[32,768,256]{2,1,0:T(8,128)(2,1)}) %all-gather.5.cloned.1.call-update) | async-done | bytes 12582928 | tf_op jit(solution)/shard_map/all_gather | solution.py:269
  228.3 0.0 copy-start.1
  228.3 4.6 %copy-done.1 = bf16[32,768,256]{2,1,0:T(8,128)(2,1)S(1)} copy-done((bf16[32,768,256]{2,1,0:T(8,128)(2,1)S(1)}, bf16[32,768,256]{2,1,0:T(8,128)(2,1)}, u32[]{:S(2)}) %copy-start.1) | copy-done | bytes 12582936
  232.9 0.0 copy-start.2
  232.9 2.8 %down.2.start_ref = f32[128,256]{1,0:T(8,128)S(1)} custom-call(s32[1]{0:T(128)} %bitcast.9.source_ref.scalar_ref, bf16[8,192,128]{2,1,0:T(8,128)(2,1)S(1)} %all-to-all-done.3.activation_ref, s32[128,2]{1,0:T(8,128)S(1)} %copy.27.routes_ref, f32[128,2]{1,0:T(8,128)S(1)} %copy.28.route_weight_ref, f32[128,256]{1,0:T(8,128)S(1)} %maximum_select_fusion.start_ref, ...), custom_call_target="tpu_custom_call" | custom-call | flops 805306368 | bytes 6291456 | tf_op jit(solution)/shard_map/down/pallas_call | solution.py:404
  235.7 0.0 collective-permute-done.3.activation_ref
  235.7 1.8 copy-done.2
  237.5 3.4 %down.3 = bf16[128,256]{1,0:T(8,128)(2,1)} custom-call(s32[1]{0:T(128)} %bitcast.source_ref.scalar_ref, bf16[8,192,128]{2,1,0:T(8,128)(2,1)S(1)} %collective-permute-done.3.activation_ref, s32[128,2]{1,0:T(8,128)S(1)} %copy.27.routes_ref, f32[128,2]{1,0:T(8,128)S(1)} %copy.28.route_weight_ref, f32[128,256]{1,0:T(8,128)S(1)} %down.2.start_ref, ...), custom_call_target="tpu_custom_call" | custom-call | flops 805306368 | bytes 6291456 | tf_op jit(solution)/shard_map/down/pallas_call | solution.py:404
  (9 shorter events, 0.2 us)
Async XLA Ops:
  6.5 4.0 %copy-start = (bf16[1,1536,256]{2,1,0:T(8,128)(2,1)S(1)}, bf16[1,1536,256]{2,1,0:T(8,128)(2,1)}, u32[]{:S(2)}) copy-start(bf16[1,1536,256]{2,1,0:T(8,128)(2,1)} %param.21) | copy-start | bytes 2359300
  6.5 152.6 %all-gather.3.cloned.1.call-start = ((), (), s32[]{:S(2)}) async-start(), calls=%async_computation.4 | async-start | bytes 25952256 | tf_op jit(solution)/shard_map/all_gather | solution.py:268
  7.8 5.2 %copy-start.5 = (bf16[512,256]{1,0:T(8,128)(2,1)S(1)}, bf16[512,256]{1,0:T(8,128)(2,1)}, u32[]{:S(2)}) copy-start(bf16[512,256]{1,0:T(8,128)(2,1)} %param.14) | copy-start | bytes 786436
  10.4 217.9 %all-gather.5.cloned.1.call-start = ((), (), s32[]{:S(2)}) async-start(), calls=%async_computation.5 | async-start | bytes 12976128 | tf_op jit(solution)/shard_map/all_gather | solution.py:269
  67.5 14.3 %collective-permute-start.1 = (bf16[32,384,128]{2,1,0:T(8,128)(2,1)}, bf16[32,384,128]{2,1,0:T(8,128)(2,1)}, u32[]{:S(2)}, u32[]{:S(2)}) collective-permute-start(bf16[32,384,128]{2,1,0:T(8,128)(2,1)} %all_to_all.20), channel_id=1, source_target_pairs={{0,256},{256,0},{1,257},{257,1},{2,258},{258,2},{3,259},{259,3},{4... | collective-permute-start | bytes 9437192 | tf_op jit(solution)/shard_map/ppermute | solution.py:277
  78.9 7.2 %collective-permute-start = (bf16[2,128,256]{2,1,0:T(8,128)(2,1)}, bf16[2,128,256]{2,1,0:T(8,128)(2,1)S(1)}, u32[]{:S(2)}, u32[]{:S(2)}) collective-permute-start(bf16[2,128,256]{2,1,0:T(8,128)(2,1)} %attend.1.attended_ref), channel_id=1, source_target_pairs={{0,16},{16,0},{32,48},{48,32},{64,80},{80,64},{96,112},{112,96},{1... | collective-permute-start | bytes 393224 | tf_op jit(solution)/shard_map/ppermute | solution.py:299
  81.8 0.9 copy-start.3
  89.0 84.7 %copy-start.6 = (f32[4096]{0:T(1024)S(1)}, f32[4096]{0:T(1024)}, u32[]{:S(2)}) copy-start(f32[4096]{0:T(1024)} %param.16) | copy-start | bytes 49156
  89.0 38.2 %all-to-all-start.1 = ((bf16[8,128,256]{2,1,0:T(8,128)(2,1)}), bf16[8,128,256]{2,1,0:T(8,128)(2,1)S(1)}, u32[]{:S(2)}, u32[]{:S(2)}) async-start(bf16[8,128,256]{2,1,0:T(8,128)(2,1)} %project.3), calls=%async_computation.1 | async-start | bytes 1048576 | tf_op jit(solution)/shard_map/all_to_all | solution.py:199
  159.2 26.4 %collective-permute-start.2 = (bf16[8,128,256]{2,1,0:T(8,128)(2,1)S(1)}, bf16[8,128,256]{2,1,0:T(8,128)(2,1)S(1)}, u32[]{:S(2)}, u32[]{:S(2)}) collective-permute-start(bf16[8,128,256]{2,1,0:T(8,128)(2,1)S(1)} %all_to_all.21.rows_ref), channel_id=1, source_target_pairs={{0,16},{16,0},{32,48},{48,32},{64,80},{80,64},{96,112},{112,96},{1... | collective-permute-start | bytes 1572872 | tf_op jit(solution)/shard_map/ppermute | solution.py:338
  173.7 11.8 %copy-start.4 = (s32[128,2]{0,1:T(2,128)S(1)}, s32[128,2]{0,1:T(2,128)}, u32[]{:S(2)}) copy-start(s32[128,2]{0,1:T(2,128)} %param.17) | copy-start | bytes 3076
  185.5 11.6 %copy-start.7 = (f32[128,2]{0,1:T(2,128)S(1)}, f32[128,2]{0,1:T(2,128)}, u32[]{:S(2)}) copy-start(f32[128,2]{0,1:T(2,128)} %param.18) | copy-start | bytes 3076
  193.4 24.4 %all-to-all-start.3 = ((bf16[8,192,128]{2,1,0:T(8,128)(2,1)}), bf16[8,192,128]{2,1,0:T(8,128)(2,1)S(1)}, u32[]{:S(2)}, u32[]{:S(2)}) async-start(bf16[8,192,128]{2,1,0:T(8,128)(2,1)} %broadcast_in_dim.8), calls=%async_computation.3 | async-start | bytes 786432 | tf_op jit(solution)/shard_map/all_to_all | solution.py:199
  217.8 17.8 %collective-permute-start.3 = (bf16[8,192,128]{2,1,0:T(8,128)(2,1)S(1)}, bf16[8,192,128]{2,1,0:T(8,128)(2,1)S(1)}, u32[]{:S(2)}, u32[]{:S(2)}) collective-permute-start(bf16[8,192,128]{2,1,0:T(8,128)(2,1)S(1)} %all-to-all-done.3.activation_ref), channel_id=1, source_target_pairs={{0,16},{16,0},{32,48},{48,32},{64,80},{80,64},{96,112},{112,96},{1... | collective-permute-start | bytes 1179656 | tf_op jit(solution)/shard_map/ppermute | solution.py:384
  228.3 4.6 %copy-start.1 = (bf16[32,768,256]{2,1,0:T(8,128)(2,1)S(1)}, bf16[32,768,256]{2,1,0:T(8,128)(2,1)}, u32[]{:S(2)}) copy-start(bf16[32,768,256]{2,1,0:T(8,128)(2,1)} %all-gather.5.cloned.1.call-done) | copy-start | bytes 37748740
  232.9 4.6 %copy-start.2 = (bf16[32,768,256]{2,1,0:T(8,128)(2,1)S(1)}, bf16[32,768,256]{2,1,0:T(8,128)(2,1)}, u32[]{:S(2)}) copy-start(bf16[32,768,256]{2,1,0:T(8,128)(2,1)} %all-gather.5.cloned.1.call-done) | copy-start | bytes 37748740
Sparse Core Ops, SparseCore 0:
  10.6 136.8 all-gather.2
  150.5 77.7 all-gather.4

commit v10 on v9

--- a/solution.py
+++ b/solution.py
@@ -21,6 +21,42 @@
 
 
 CONTRACT_LAST = (((1,), (1,)), ((), ()))
+
+
+def pack(core_ref, gate_ref, up_ref, out_ref):
+    units = gate_ref.shape[0]
+    columns = out_ref.shape[1]
+    half = columns // 2
+
+    def store(source_ref):
+        for pair in range(gate_ref.shape[1] // (2 * columns)):
+            for odd in range(2):
+                row = (2 * pair + odd) * units
+                for side in range(2):
+                    start = (2 * pair + side) * columns + odd * half
+                    out_ref[row : row + units, side * half : (side + 1) * half] = source_ref[
+                        :, start : start + half
+                    ]
+
+    @pl.when(core_ref[0] == 0)
+    def _():
+        store(gate_ref)
+
+    @pl.when(core_ref[0] != 0)
+    def _():
+        store(up_ref)
+
+
+def compose(core_ref, odd_ref, shared_ref, weight_ref, key_ref, value_ref, out_ref):
+    rows = weight_ref.shape[0]
+    half = key_ref.shape[0]
+    places = out_ref.shape[0] // 2
+    width = out_ref.shape[2]
+    for side in range(2):
+        for place in range(side * places, (side + 1) * places):
+            out_ref[place, :rows] = weight_ref[:, side * width : (side + 1) * width]
+            out_ref[place, rows : rows + half] = key_ref[...]
+            out_ref[place, rows + half :] = value_ref[...]
 
 
 def attend(place_ref, query_ref, piece_ref, out_ref):
@@ -184,6 +220,7 @@
 SCALAR = pl.BlockSpec(memory_space=pltpu.SMEM)
 HERE = pl.BlockSpec(memory_space=pltpu.VMEM)
 LIMIT = pltpu.CompilerParams(vmem_limit_bytes=32 * 1024 * 1024)
+LARGE = pltpu.CompilerParams(vmem_limit_bytes=52 * 1024 * 1024)
 WIDE = pltpu.CompilerParams(vmem_limit_bytes=56 * 1024 * 1024)
 
 
@@ -235,45 +272,61 @@
 
     first_blocks = D // columns
 
-    gate_or_up = jnp.where(core == 0, gate_weight[0], up_weight[0]).T
-    gate_or_up = jnp.transpose(
-        gate_or_up.reshape(local_units, PAIRS, 2, 2, columns // 2), (1, 3, 0, 2, 4)
-    )
+    span = 1024
+    gate_or_up = pl.pallas_call(
+        pack,
+        out_shape=jax.ShapeDtypeStruct((first_blocks * local_units, columns), jnp.bfloat16),
+        grid_spec=pltpu.PrefetchScalarGridSpec(
+            num_scalar_prefetch=1,
+            grid=(D // span,),
+            in_specs=[pl.BlockSpec((local_units, span), lambda i, core_ref: (0, i))] * 2,
+            out_specs=pl.BlockSpec((span // columns * local_units, columns), lambda i, core_ref: (i, 0)),
+        ),
+        compiler_params=WIDE,
+        name="pack",
+    )(core.reshape(1), gate_weight[0].T, up_weight[0].T)
     down_half = lax.dynamic_slice_in_dim(down_weight[0], core * half_units, half_units, 0)
-    gate_or_up = gate_or_up.reshape(first_blocks * local_units, columns)
 
     shared = tensor_index * local_heads // group_width
-    key_head = lax.dynamic_slice_in_dim(all_key_rows, shared * HEAD_WIDTH, HEAD_WIDTH, 1)
-    value_head = lax.dynamic_slice_in_dim(all_value_rows, shared * HEAD_WIDTH, HEAD_WIDTH, 1)
     half_rows = out_weight.shape[0] // 2
-    weight_half = lax.dynamic_slice_in_dim(out_weight, core * half_rows, half_rows, 0)
     half_tokens = tokens // 2
     half_columns = columns // 2
-    key_half = lax.dynamic_slice_in_dim(key_head, odd * half_tokens, half_tokens, 0)
-    value_half = lax.dynamic_slice_in_dim(value_head, odd * half_tokens, half_tokens, 0)
-    message = jnp.stack(
-        [
-            jnp.concatenate(
-                [weight_half[:, side * half_columns : (side + 1) * half_columns], key_half, value_half],
-                axis=0,
-            )
-            for side in range(2)
-        ]
-    )
-    message_rows = message.shape[1]
+    message_rows = half_rows + 2 * half_tokens
+    half_spec = pl.BlockSpec(
+        (half_tokens, HEAD_WIDTH), lambda i, core_ref, odd_ref, shared_ref: (odd_ref[0], shared_ref[0])
+    )
+    message = pl.pallas_call(
+        compose,
+        out_shape=jax.ShapeDtypeStruct((2 * expert_count, message_rows, half_columns), jnp.bfloat16),
+        grid_spec=pltpu.PrefetchScalarGridSpec(
+            num_scalar_prefetch=3,
+            grid=(1,),
+            in_specs=[
+                pl.BlockSpec(
+                    (half_rows, columns), lambda i, core_ref, odd_ref, shared_ref: (core_ref[0], 0)
+                ),
+                half_spec,
+                half_spec,
+            ],
+            out_specs=HERE,
+        ),
+        compiler_params=LIMIT,
+        name="compose",
+    )(
+        core.reshape(1),
+        odd.reshape(1),
+        shared.astype(jnp.int32).reshape(1),
+        out_weight,
+        all_key_rows,
+        all_value_rows,
+    )
     both = [
         [(2 * pair + side) * expert_count + place for side in range(2) for place in range(expert_count)]
         for pair in range(PAIRS)
     ]
     weights = lax.all_gather(gate_or_up, ("dp", "expert"), axis=0)
     down_weights = lax.all_gather(down_half, ("dp", "expert"), axis=0)
-    gathered = exchange(
-        jnp.broadcast_to(message[:, None], (2, expert_count) + message.shape[1:]).reshape(
-            2 * expert_count, message_rows, half_columns
-        ),
-        ("tensor", "expert"),
-        both,
-    )
+    gathered = exchange(message, ("tensor", "expert"), both)
     gathered_other = lax.ppermute(gathered, "dp", SWAP)
 
     attended = pl.pallas_call(
@@ -420,7 +473,7 @@
                     pltpu.VMEM((tokens, columns), jnp.float32),
                 ],
             ),
-            compiler_params=LIMIT,
+            compiler_params=LARGE,
             cost_estimate=cost(
                 2 * tokens * expert_count * hidden_units * columns // 2,
                 2 * expert_count * hidden_units * columns // 2,

time: 249 us -> 243 us (0.976)
  local copies, waits for them, and re-layouts: 14.9 us -> 3.57 us
  Pallas kernels: 27.8 us -> 34.6 us
  starting transfers between devices: 47.9 us -> 51.2 us
  blocking collectives: 85.5 us -> 82.5 us
    unnamed x18, local copies, waits for them, and re-layouts: 7.55 us -> 1.19 us
    pallas_call x0 -> x2, Pallas kernels: none -> 4.01 us  [the longest x1 3.6 us: local(): pl.pallas_call(pack, out_shape=jax.ShapeDtypeStruct((first_blocks * local...]
    all_to_all x2, blocking collectives: 85.5 us -> 82.5 us  [exchange(): lax.all_to_all(message, axis, split_axis=0, concat_axis=0, tiled=True, ax...]
    pallas_call x2, Pallas kernels: 6.14 us -> 9 us  [lowered(): pl.pallas_call(functools.partial(down, parts), out_shape=jax.ShapeDtypeSt...]
  transfers between devices with their start and end apart: 8 -> 8, of which waited for: 5 -> 5; matrix products, arithmetic and copies ran while one was open for 2% -> 1% of each run, Pallas kernels for 10% -> 11%
where the time goes in v10:
time: 243 us; the launch traced here: 242 us
  blocking collectives  82.5 us (34%)
  waiting for transfers between devices  56.2 us (23%)
  starting transfers between devices  51.2 us (21%)
  Pallas kernels  34.6 us (14%)
  between operations  13.7 us (6%)
  local copies, waits for them, and re-layouts  3.57 us (1%)
    all_to_all x2, blocking collectives, exchange(): lax.all_to_all(message, axis, split_axis=0, concat_axis=0, tiled=True, ax...  82.5 us
    all_to_all x2, waiting for transfers between devices, exchange(): lax.all_to_all(message, axis, split_axis=0, concat_axis=0, tiled=True, ax...  41.5 us
    all_to_all x2, starting transfers between devices, exchange(): lax.all_to_all(message, axis, split_axis=0, concat_axis=0, tiled=True, ax...  20.4 us
    pallas_call x2, Pallas kernels, gated(): pl.pallas_call(functools.partial(gate_up, last), out_shape=out_type if la...  13.7 us
    ppermute x1, starting transfers between devices, local(): rows_other = lax.ppermute(rows_own, 'tensor', NEIGHBOUR)  13.6 us
    pallas_call x2, Pallas kernels, lowered(): pl.pallas_call(functools.partial(down, parts), out_shape=jax.ShapeDtypeSt...  9 us
    all_gather x1, waiting for transfers between devices, local(): down_weights = lax.all_gather(down_half, ('dp', 'expert'), axis=0)  8.43 us
    ppermute x1, starting transfers between devices, local(): gathered_other = lax.ppermute(gathered, 'dp', SWAP)  8.3 us
  transfers between devices with their start and end apart: 8, of which 5 were waited for; matrix products, arithmetic and copies ran while one was open for 1% of the time, Pallas kernels for 11%

profile of v10, /device:TPU:1, one launch (start us, length us, event | category | flops | bytes accessed | tf_op | source)
XLA Modules:
  0.0 241.9 jit_solution(2172049348958969464)
XLA Ops:
  6.5 0.0 copy-start
  6.5 0.0 copy-start.2
  6.5 0.0 copy-start.3
  6.5 0.0 copy-start.4
  6.5 0.0 all-gather.6.cloned.1.call-start
  6.6 3.6 %pack.1 = bf16[1536,256]{1,0:T(8,128)(2,1)} custom-call(s32[1]{0:T(128)} %bitcast.1.core_ref, bf16[96,4096]{1,0:T(8,128)(2,1)} %bitcast.43, bf16[96,4096]{1,0:T(8,128)(2,1)} %bitcast.44), custom_call_target="tpu_custom_call" | custom-call | tf_op jit(solution)/shard_map/pack/pallas_call | solution.py:276
  10.2 0.0 all-gather.6.cloned.1.call-update
  10.2 0.0 all-gather.4.cloned.1.call-start
  10.3 0.0 copy-done
  10.3 0.8 constant_dynamic-slice_fusion
  11.0 0.0 all-gather.4.cloned.1.call-update
  11.1 0.0 copy-done.2
  11.1 0.0 copy-done.3
  11.1 0.0 copy-done.4
  11.1 0.4 compose.1
  11.5 53.1 %all_to_all.20 = bf16[32,384,128]{2,1,0:T(8,128)(2,1)} all-to-all(bf16[32,384,128]{2,1,0:T(8,128)(2,1)S(1)} %compose.1), channel_id=1, replica_groups={{0,1,2,3,4,5,6,7,8,9,10,11,12,13,14,15,16,17,18,19,20,21,22,23,24,25,26..., dimensions={0} | all-to-all | bytes 6291456 | tf_op jit(solution)/shard_map/all_to_all | solution.py:236
  64.6 8.3 %collective-permute-start.1 = (bf16[32,384,128]{2,1,0:T(8,128)(2,1)}, bf16[32,384,128]{2,1,0:T(8,128)(2,1)}, u32[]{:S(2)}, u32[]{:S(2)}) collective-permute-start(bf16[32,384,128]{2,1,0:T(8,128)(2,1)} %all_to_all.20), channel_id=1, source_target_pairs={{0,256},{256,0},{1,257},{257,1},{2,258},{258,2},{3,259},{259,3},{4... | collective-permute-start | bytes 9437192 | tf_op jit(solution)/shard_map/ppermute | solution.py:330
  72.9 3.1 %attend.1.attended_ref = bf16[2,128,256]{2,1,0:T(8,128)(2,1)} custom-call(s32[1]{0:T(128)} %bitcast.2.place_ref, bf16[128,512]{1,0:T(8,128)(2,1)} %query_ref.1, bf16[2,16,384,128]{3,2,1,0:T(8,128)(2,1)} %bitcast.5.piece_ref), custom_call_target="tpu_custom_call" | custom-call | tf_op jit(solution)/shard_map/attend/pallas_call | solution.py:332
  76.0 2.8 %collective-permute-start = (bf16[2,128,256]{2,1,0:T(8,128)(2,1)}, bf16[2,128,256]{2,1,0:T(8,128)(2,1)S(1)}, u32[]{:S(2)}, u32[]{:S(2)}) collective-permute-start(bf16[2,128,256]{2,1,0:T(8,128)(2,1)} %attend.1.attended_ref), channel_id=1, source_target_pairs={{0,16},{16,0},{32,48},{48,32},{64,80},{80,64},{96,112},{112,96},{1... | collective-permute-start | bytes 393224 | tf_op jit(solution)/shard_map/ppermute | solution.py:352
  78.9 0.0 collective-permute-done.1
  78.9 0.0 copy-start.1
  78.9 0.9 copy-done.1
  79.9 2.0 project.2.refs_0_
  81.8 1.4 collective-permute-done.attended_ref
  83.3 2.8 %project.3 = bf16[8,128,256]{2,1,0:T(8,128)(2,1)} custom-call(s32[1]{0:T(128)} %bitcast.1.core_ref, s32[1]{0:T(128)} %bitcast.source_ref.scalar_ref, bf16[2,128,256]{2,1,0:T(8,128)(2,1)S(1)} %collective-permute-done.attended_ref, bf16[2,8,2,384,128]{4,3,2,1,0:T(8,128)(2,1)} %bitcast.6.own_ref, bf16[2,8,2,384,128]{4,3,2,1,0:T(8,128)(2,1)} %bitcast.7.other_ref, ...), custom_call_target="tpu_custom_call" | custom-call | flops 268435456 | bytes 2097152 | tf_op jit(solution)/shard_map/project/pallas_call | solution.py:362
  86.1 0.0 copy-start.6
  86.1 14.9 %all-to-all-start.1 = ((bf16[8,128,256]{2,1,0:T(8,128)(2,1)}), bf16[8,128,256]{2,1,0:T(8,128)(2,1)S(1)}, u32[]{:S(2)}, u32[]{:S(2)}) async-start(bf16[8,128,256]{2,1,0:T(8,128)(2,1)} %project.3), calls=%async_computation.1 | async-start | bytes 1048576 | tf_op jit(solution)/shard_map/all_to_all | solution.py:236
  101.0 0.8 constant_dynamic-slice_fusion.2
  101.8 23.2 %all-to-all-done.1 = bf16[8,128,256]{2,1,0:T(8,128)(2,1)S(1)} async-done(((bf16[8,128,256]{2,1,0:T(8,128)(2,1)}), bf16[8,128,256]{2,1,0:T(8,128)(2,1)S(1)}, u32[]{:S(2)}, u32[]{:S(2)}) %all-to-all-start.1) | async-done | bytes 524320 | tf_op jit(solution)/shard_map/all_to_all | solution.py:236
  125.0 0.1 convert_reduce_fusion
  125.1 29.4 %all_to_all.21.rows_ref = bf16[8,128,256]{2,1,0:T(8,128)(2,1)S(1)} all-to-all(bf16[8,128,256]{2,1,0:T(8,128)(2,1)S(1)} %broadcast_in_dim.4), channel_id=1, replica_groups={{0,32,64,96,128,160,192,224},{16,48,80,112,144,176,208,240},{1,33,65,97..., dimensions={0} | all-to-all | bytes 1048576 | tf_op jit(solution)/shard_map/all_to_all | solution.py:236
  154.6 0.0 all-gather.6.cloned.1.call-done
  154.6 13.6 %collective-permute-start.2 = (bf16[8,128,256]{2,1,0:T(8,128)(2,1)S(1)}, bf16[8,128,256]{2,1,0:T(8,128)(2,1)S(1)}, u32[]{:S(2)}, u32[]{:S(2)}) collective-permute-start(bf16[8,128,256]{2,1,0:T(8,128)(2,1)S(1)} %all_to_all.21.rows_ref), channel_id=1, source_target_pairs={{0,16},{16,0},{32,48},{48,32},{64,80},{80,64},{96,112},{112,96},{1... | collective-permute-start | bytes 1572872 | tf_op jit(solution)/shard_map/ppermute | solution.py:391
  168.2 0.0 copy-done.6
  168.2 0.0 copy-start.5
  168.2 6.6 %gate_up.2 = (f32[2,1536,128]{2,1,0:T(8,128)S(1)}, f32[128,1]{1,0:T(8,128)S(1)}) custom-call(s32[1]{0:T(128)} %bitcast.3.odd_ref.source_ref.scalar_ref, bf16[8,128,256]{2,1,0:T(8,128)(2,1)S(1)} %all_to_all.21.rows_ref, f32[8,2,1,256]{3,2,1,0:T(1,128)S(1)} %bitcast.28, bf16[32,8,2,96,256]{4,3,2,1,0:T(8,128)(2,1)} %bitcast.39, ...), custom_call_target="tpu_custom_call" | custom-call | flops 1610612736 | bytes 12582912 | tf_op jit(solution)/shard_map/gate_up/pallas_call | solution.py:415
  174.8 4.8 %collective-permute-done.2.rows_ref = bf16[8,128,256]{2,1,0:T(8,128)(2,1)S(1)} collective-permute-done((bf16[8,128,256]{2,1,0:T(8,128)(2,1)S(1)}, bf16[8,128,256]{2,1,0:T(8,128)(2,1)S(1)}, u32[]{:S(2)}, u32[]{:S(2)}) %collective-permute-start.2) | collective-permute-done | bytes 524320 | tf_op jit(solution)/shard_map/ppermute | solution.py:391
  179.7 0.0 copy-done.5
  179.7 0.0 copy-start.7
  179.7 7.1 %gate_up.3 = bf16[192,128]{1,0:T(8,128)(2,1)S(1)} custom-call(s32[1]{0:T(128)} %bitcast.source_ref.scalar_ref, bf16[8,128,256]{2,1,0:T(8,128)(2,1)S(1)} %collective-permute-done.2.rows_ref, f32[8,2,1,256]{3,2,1,0:T(1,128)S(1)} %bitcast.29, bf16[32,8,2,96,256]{4,3,2,1,0:T(8,128)(2,1)} %bitcast.41, bf16[32,8,2,96,256]{4,3,2,1,0:T(8,128)(2,1)} %bitcast.42, ...), custom_call_target="tpu_custom_call" | custom-call | flops 1610612736 | bytes 12582912 | tf_op jit(solution)/shard_map/gate_up/pallas_call | solution.py:415
  186.7 0.8 broadcast_in_dim.5
  187.5 5.5 %all-to-all-start.3 = ((bf16[8,192,128]{2,1,0:T(8,128)(2,1)}), bf16[8,192,128]{2,1,0:T(8,128)(2,1)S(1)}, u32[]{:S(2)}, u32[]{:S(2)}) async-start(bf16[8,192,128]{2,1,0:T(8,128)(2,1)} %broadcast_in_dim.5), calls=%async_computation.3 | async-start | bytes 786432 | tf_op jit(solution)/shard_map/all_to_all | solution.py:236
  193.1 0.1 copy.24.routes_ref
  193.2 0.0 copy-done.7
  193.2 0.1 copy.25.route_weight_ref
  193.3 18.3 %all-to-all-done.3.activation_ref = bf16[8,192,128]{2,1,0:T(8,128)(2,1)S(1)} async-done(((bf16[8,192,128]{2,1,0:T(8,128)(2,1)}), bf16[8,192,128]{2,1,0:T(8,128)(2,1)S(1)}, u32[]{:S(2)}, u32[]{:S(2)}) %all-to-all-start.3) | async-done | bytes 393248 | tf_op jit(solution)/shard_map/all_to_all | solution.py:236
  211.6 6.0 %collective-permute-start.3 = (bf16[8,192,128]{2,1,0:T(8,128)(2,1)S(1)}, bf16[8,192,128]{2,1,0:T(8,128)(2,1)S(1)}, u32[]{:S(2)}, u32[]{:S(2)}) collective-permute-start(bf16[8,192,128]{2,1,0:T(8,128)(2,1)S(1)} %all-to-all-done.3.activation_ref), channel_id=1, source_target_pairs={{0,16},{16,0},{32,48},{48,32},{64,80},{80,64},{96,112},{112,96},{1... | collective-permute-start | bytes 1179656 | tf_op jit(solution)/shard_map/ppermute | solution.py:437
  217.6 8.4 %all-gather.4.cloned.1.call-done = bf16[32,768,256]{2,1,0:T(8,128)(2,1)} async-done(((bf16[1,768,256]{2,1,0:T(8,128)(2,1)}), bf16[32,768,256]{2,1,0:T(8,128)(2,1)}) %all-gather.4.cloned.1.call-update) | async-done | bytes 12582928 | tf_op jit(solution)/shard_map/all_gather | solution.py:328
  226.1 4.2 %down.2.start_ref = f32[128,256]{1,0:T(8,128)S(1)} custom-call(s32[1]{0:T(128)} %bitcast.3.odd_ref.source_ref.scalar_ref, bf16[8,192,128]{2,1,0:T(8,128)(2,1)S(1)} %all-to-all-done.3.activation_ref, s32[128,2]{1,0:T(8,128)S(1)} %copy.24.routes_ref, f32[128,2]{1,0:T(8,128)S(1)} %copy.25.route_weight_ref, f32[128,256]{1,0:T(8,128)S(1)} %maximum_select_fusion.start_ref, ...), custom_call_target="tpu_custom_call" | custom-call | flops 805306368 | bytes 6291456 | tf_op jit(solution)/shard_map/down/pallas_call | solution.py:457
  230.3 0.0 collective-permute-done.3.activation_ref
  230.3 4.8 %down.3 = bf16[128,256]{1,0:T(8,128)(2,1)} custom-call(s32[1]{0:T(128)} %bitcast.source_ref.scalar_ref, bf16[8,192,128]{2,1,0:T(8,128)(2,1)S(1)} %collective-permute-done.3.activation_ref, s32[128,2]{1,0:T(8,128)S(1)} %copy.24.routes_ref, f32[128,2]{1,0:T(8,128)S(1)} %copy.25.route_weight_ref, f32[128,256]{1,0:T(8,128)S(1)} %down.2.start_ref, ...), custom_call_target="tpu_custom_call" | custom-call | flops 805306368 | bytes 6291456 | tf_op jit(solution)/shard_map/down/pallas_call | solution.py:457
  (6 shorter events, 0.1 us)
Async XLA Ops:
  6.5 3.7 %copy-start = (bf16[1,1536,256]{2,1,0:T(8,128)(2,1)S(1)}, bf16[1,1536,256]{2,1,0:T(8,128)(2,1)}, u32[]{:S(2)}) copy-start(bf16[1,1536,256]{2,1,0:T(8,128)(2,1)} %param.21) | copy-start | bytes 2359300
  6.5 4.6 %copy-start.2 = (bf16[512,256]{1,0:T(8,128)(2,1)S(1)}, bf16[512,256]{1,0:T(8,128)(2,1)}, u32[]{:S(2)}) copy-start(bf16[512,256]{1,0:T(8,128)(2,1)} %weight_ref.1) | copy-start | bytes 786436
  6.5 4.6 %copy-start.3 = (bf16[128,512]{1,0:T(8,128)(2,1)S(1)}, bf16[128,512]{1,0:T(8,128)(2,1)}, u32[]{:S(2)}) copy-start(bf16[128,512]{1,0:T(8,128)(2,1)} %key_ref.1) | copy-start | bytes 393220
  6.5 4.6 %copy-start.4 = (bf16[128,512]{1,0:T(8,128)(2,1)S(1)}, bf16[128,512]{1,0:T(8,128)(2,1)}, u32[]{:S(2)}) copy-start(bf16[128,512]{1,0:T(8,128)(2,1)} %value_ref.1) | copy-start | bytes 393220
  6.5 148.0 %all-gather.6.cloned.1.call-start = ((), (), s32[]{:S(2)}) async-start(), calls=%async_computation.5 | async-start | bytes 25952256 | tf_op jit(solution)/shard_map/all_gather | solution.py:327
  10.2 215.9 %all-gather.4.cloned.1.call-start = ((), (), s32[]{:S(2)}) async-start(), calls=%async_computation.4 | async-start | bytes 12976128 | tf_op jit(solution)/shard_map/all_gather | solution.py:328
  64.6 14.3 %collective-permute-start.1 = (bf16[32,384,128]{2,1,0:T(8,128)(2,1)}, bf16[32,384,128]{2,1,0:T(8,128)(2,1)}, u32[]{:S(2)}, u32[]{:S(2)}) collective-permute-start(bf16[32,384,128]{2,1,0:T(8,128)(2,1)} %all_to_all.20), channel_id=1, source_target_pairs={{0,256},{256,0},{1,257},{257,1},{2,258},{258,2},{3,259},{259,3},{4... | collective-permute-start | bytes 9437192 | tf_op jit(solution)/shard_map/ppermute | solution.py:330
  76.0 7.2 %collective-permute-start = (bf16[2,128,256]{2,1,0:T(8,128)(2,1)}, bf16[2,128,256]{2,1,0:T(8,128)(2,1)S(1)}, u32[]{:S(2)}, u32[]{:S(2)}) collective-permute-start(bf16[2,128,256]{2,1,0:T(8,128)(2,1)} %attend.1.attended_ref), channel_id=1, source_target_pairs={{0,16},{16,0},{32,48},{48,32},{64,80},{80,64},{96,112},{112,96},{1... | collective-permute-start | bytes 393224 | tf_op jit(solution)/shard_map/ppermute | solution.py:352
  78.9 0.9 copy-start.1
  86.1 82.1 %copy-start.6 = (f32[4096]{0:T(1024)S(1)}, f32[4096]{0:T(1024)}, u32[]{:S(2)}) copy-start(f32[4096]{0:T(1024)} %param.16) | copy-start | bytes 49156
  86.1 38.9 %all-to-all-start.1 = ((bf16[8,128,256]{2,1,0:T(8,128)(2,1)}), bf16[8,128,256]{2,1,0:T(8,128)(2,1)S(1)}, u32[]{:S(2)}, u32[]{:S(2)}) async-start(bf16[8,128,256]{2,1,0:T(8,128)(2,1)} %project.3), calls=%async_computation.1 | async-start | bytes 1048576 | tf_op jit(solution)/shard_map/all_to_all | solution.py:236
  154.6 25.1 %collective-permute-start.2 = (bf16[8,128,256]{2,1,0:T(8,128)(2,1)S(1)}, bf16[8,128,256]{2,1,0:T(8,128)(2,1)S(1)}, u32[]{:S(2)}, u32[]{:S(2)}) collective-permute-start(bf16[8,128,256]{2,1,0:T(8,128)(2,1)S(1)} %all_to_all.21.rows_ref), channel_id=1, source_target_pairs={{0,16},{16,0},{32,48},{48,32},{64,80},{80,64},{96,112},{112,96},{1... | collective-permute-start | bytes 1572872 | tf_op jit(solution)/shard_map/ppermute | solution.py:391
  168.2 11.5 %copy-start.5 = (s32[128,2]{0,1:T(2,128)S(1)}, s32[128,2]{0,1:T(2,128)}, u32[]{:S(2)}) copy-start(s32[128,2]{0,1:T(2,128)} %param.17) | copy-start | bytes 3076
  179.7 13.5 %copy-start.7 = (f32[128,2]{0,1:T(2,128)S(1)}, f32[128,2]{0,1:T(2,128)}, u32[]{:S(2)}) copy-start(f32[128,2]{0,1:T(2,128)} %param.18) | copy-start | bytes 3076
  187.5 24.1 %all-to-all-start.3 = ((bf16[8,192,128]{2,1,0:T(8,128)(2,1)}), bf16[8,192,128]{2,1,0:T(8,128)(2,1)S(1)}, u32[]{:S(2)}, u32[]{:S(2)}) async-start(bf16[8,192,128]{2,1,0:T(8,128)(2,1)} %broadcast_in_dim.5), calls=%async_computation.3 | async-start | bytes 786432 | tf_op jit(solution)/shard_map/all_to_all | solution.py:236
  211.6 18.6 %collective-permute-start.3 = (bf16[8,192,128]{2,1,0:T(8,128)(2,1)S(1)}, bf16[8,192,128]{2,1,0:T(8,128)(2,1)S(1)}, u32[]{:S(2)}, u32[]{:S(2)}) collective-permute-start(bf16[8,192,128]{2,1,0:T(8,128)(2,1)S(1)} %all-to-all-done.3.activation_ref), channel_id=1, source_target_pairs={{0,16},{16,0},{32,48},{48,32},{64,80},{80,64},{96,112},{112,96},{1... | collective-permute-start | bytes 1179656 | tf_op jit(solution)/shard_map/ppermute | solution.py:437
Sparse Core Ops, SparseCore 0:
  10.5 134.6 all-gather.5
  148.3 77.7 all-gather.3

commit v11 on v10

--- a/solution.py
+++ b/solution.py
@@ -184,7 +184,9 @@
                 out_ref[k * units : (k + 1) * units] = chosen[k].astype(out_ref.dtype)
 
 
-def down(parts, scalar_ref, activation_ref, routes_ref, route_weight_ref, start_ref, *refs):
+def down(
+    parts, odd_ref, own_ref, neighbour_ref, routes_ref, route_weight_ref, hidden_ref, *refs
+):
     half_refs = refs[:parts], refs[parts : 2 * parts]
     out_ref, turned, mixed = refs[2 * parts :]
     step = pl.program_id(0)
@@ -192,13 +194,16 @@
 
     @pl.when(step == 0)
     def _():
-        for half in range(2):
-            for k in range(TOP):
-                part = activation_ref[blocks * half : blocks * (half + 1), k * units : (k + 1) * units]
-                part = part.reshape(blocks * units, part.shape[2]).astype(jnp.float32)
-                turned[half, k] = jnp.transpose(part).astype(turned.dtype)
-        mixed[...] = start_ref[...]
-
+        for which, activation_ref in enumerate((own_ref, neighbour_ref)):
+            for half in range(2):
+                for k in range(TOP):
+                    place = pl.ds(blocks * half, blocks)
+                    part = activation_ref[place, k * units : (k + 1) * units]
+                    part = part.reshape(blocks * units, part.shape[2]).astype(jnp.float32)
+                    turned[which, half, k] = jnp.transpose(part).astype(turned.dtype)
+        mixed[...] = hidden_ref[...]
+
+    parities = odd_ref[0], 1 - odd_ref[0]
     for part in range(parts):
         for place in range(per_part):
             expert = (step * parts + part) * per_part + place
@@ -207,9 +212,10 @@
             masks = [here[k].astype(jnp.bfloat16) for k in range(TOP)]
             total = jnp.zeros(mixed.shape, jnp.float32)
             for half in range(2):
-                rows = sum(turned[half, k] * masks[k] for k in range(TOP))
-                weight = half_refs[half][part][place].reshape(blocks * units, columns)
-                total += jnp.dot(rows, weight, preferred_element_type=jnp.float32)
+                for which, parity in enumerate(parities):
+                    rows = sum(turned[which, half, k] * masks[k] for k in range(TOP))
+                    weight = half_refs[half][part][place, :, parity].reshape(blocks * units, columns)
+                    total += jnp.dot(rows, weight, preferred_element_type=jnp.float32)
             mixed[...] += total * share
 
     @pl.when(step == pl.num_programs(0) - 1)
@@ -272,14 +278,17 @@
 
     first_blocks = D // columns
 
-    span = 1024
+    span = 2048
     gate_or_up = pl.pallas_call(
         pack,
         out_shape=jax.ShapeDtypeStruct((first_blocks * local_units, columns), jnp.bfloat16),
         grid_spec=pltpu.PrefetchScalarGridSpec(
             num_scalar_prefetch=1,
             grid=(D // span,),
-            in_specs=[pl.BlockSpec((local_units, span), lambda i, core_ref: (0, i))] * 2,
+            in_specs=[
+                pl.BlockSpec((local_units, span), lambda i, core_ref: (0, i * (1 - core_ref[0]))),
+                pl.BlockSpec((local_units, span), lambda i, core_ref: (0, i * core_ref[0])),
+            ],
             out_specs=pl.BlockSpec((span // columns * local_units, columns), lambda i, core_ref: (i, 0)),
         ),
         compiler_params=WIDE,
@@ -436,50 +445,16 @@
     activation_own = spread(activation, "tensor", PAIRS, PARITY)
     activation_other = lax.ppermute(activation_own, "tensor", NEIGHBOUR)
     parts = 2
-    per_part = 4
+    per_part = 2
     down_steps = expert_count // (parts * per_part)
     quarter = PAIRS // 2
     down_weights = down_weights.reshape(2 * expert_count, quarter, 2, local_units, columns)
 
     def down_spec(half, part):
         return pl.BlockSpec(
-            (per_part, quarter, 1, local_units, columns),
-            lambda i, scalar_ref: (
-                (half * down_steps + i) * parts + part,
-                0,
-                scalar_ref[0],
-                0,
-                0,
-            ),
-        )
-
-    def lowered(parity, rows, start, dtype):
-        return pl.pallas_call(
-            functools.partial(down, parts),
-            out_shape=jax.ShapeDtypeStruct((tokens, columns), dtype),
-            grid_spec=pltpu.PrefetchScalarGridSpec(
-                num_scalar_prefetch=1,
-                grid=(down_steps,),
-                in_specs=[
-                    whole(PAIRS, TOP * local_units, tokens),
-                    whole(tokens, TOP),
-                    whole(tokens, TOP),
-                    whole(tokens, columns),
-                ]
-                + [down_spec(half, part) for half in range(2) for part in range(parts)],
-                out_specs=whole(tokens, columns),
-                scratch_shapes=[
-                    pltpu.VMEM((2, TOP, tokens, quarter * local_units), jnp.bfloat16),
-                    pltpu.VMEM((tokens, columns), jnp.float32),
-                ],
-            ),
-            compiler_params=LARGE,
-            cost_estimate=cost(
-                2 * tokens * expert_count * hidden_units * columns // 2,
-                2 * expert_count * hidden_units * columns // 2,
-            ),
-            name="down",
-        )(parity.reshape(1), rows, routes, route_weight, start, *[down_weights] * (2 * parts))
+            (per_part, quarter, 2, local_units, columns),
+            lambda i, odd_ref: ((half * down_steps + i) * parts + part, 0, 0, 0, 0),
+        )
 
     shares = [
         lax.dynamic_slice(
@@ -490,8 +465,35 @@
     hidden_here = jnp.where(
         odd == 0, jnp.concatenate(shares, axis=1), jnp.concatenate(shares[::-1], axis=1)
     )
-    mixed = lowered(odd, activation_own, hidden_here, jnp.float32)
-    return lowered(1 - odd, activation_other, mixed, jnp.bfloat16)
+    return pl.pallas_call(
+        functools.partial(down, parts),
+        out_shape=jax.ShapeDtypeStruct((tokens, columns), jnp.bfloat16),
+        grid_spec=pltpu.PrefetchScalarGridSpec(
+            num_scalar_prefetch=1,
+            grid=(down_steps,),
+            in_specs=[HERE] * 5
+            + [down_spec(half, part) for half in range(2) for part in range(parts)],
+            out_specs=whole(tokens, columns),
+            scratch_shapes=[
+                pltpu.VMEM((2, 2, TOP, tokens, quarter * local_units), jnp.bfloat16),
+                pltpu.VMEM((tokens, columns), jnp.float32),
+            ],
+        ),
+        compiler_params=LARGE,
+        cost_estimate=cost(
+            2 * tokens * expert_count * hidden_units * columns,
+            2 * expert_count * hidden_units * columns,
+        ),
+        name="down",
+    )(
+        odd.reshape(1),
+        activation_own,
+        activation_other,
+        routes,
+        route_weight,
+        hidden_here,
+        *[down_weights] * (2 * parts),
+    )
 
 
 def solution(mesh):

time: 243 us -> 241 us (level)
  blocking collectives: 82.5 us -> 106 us
  waiting for transfers between devices: 56.2 us -> 37.8 us
  starting transfers between devices: 51.2 us -> 46.9 us
  Pallas kernels: 34.6 us -> 31.6 us
    all_to_all x2 -> x3, blocking collectives: 82.5 us -> 106 us  [exchange(): lax.all_to_all(message, axis, split_axis=0, concat_axis=0, tiled=True, ax...]
    all_to_all x2 -> x1, waiting for transfers between devices: 41.5 us -> 23.2 us  [exchange(): lax.all_to_all(message, axis, split_axis=0, concat_axis=0, tiled=True, ax...]
    all_to_all x2 -> x1, starting transfers between devices: 20.4 us -> 15.1 us  [exchange(): lax.all_to_all(message, axis, split_axis=0, concat_axis=0, tiled=True, ax...]
    pallas_call x2 -> x1, Pallas kernels: 9 us -> 7.34 us  [local(): pl.pallas_call(functools.partial(down, parts), out_shape=jax.ShapeDtypeSt...]
  transfers between devices with their start and end apart: 8 -> 7, of which waited for: 5 -> 4; matrix products, arithmetic and copies ran while one was open for 1% -> 1% of each run, Pallas kernels for 11% -> 9%
where the time goes in v11:
time: 241 us; the launch traced here: 239 us
  blocking collectives  106 us (44%)
  starting transfers between devices  46.9 us (19%)
  waiting for transfers between devices  37.8 us (16%)
  Pallas kernels  31.6 us (13%)
  between operations  13.7 us (6%)
  local copies, waits for them, and re-layouts  2.81 us (1%)
    all_to_all x3, blocking collectives, exchange(): lax.all_to_all(message, axis, split_axis=0, concat_axis=0, tiled=True, ax...  106 us
    all_to_all x1, waiting for transfers between devices, exchange(): lax.all_to_all(message, axis, split_axis=0, concat_axis=0, tiled=True, ax...  23.2 us
    all_to_all x1, starting transfers between devices, exchange(): lax.all_to_all(message, axis, split_axis=0, concat_axis=0, tiled=True, ax...  15.1 us
    ppermute x1, starting transfers between devices, local(): rows_other = lax.ppermute(rows_own, 'tensor', NEIGHBOUR)  14.6 us
    pallas_call x2, Pallas kernels, gated(): pl.pallas_call(functools.partial(gate_up, last), out_shape=out_type if la...  13.7 us
    ppermute x1, starting transfers between devices, local(): gathered_other = lax.ppermute(gathered, 'dp', SWAP)  8.14 us
    all_gather x1, waiting for transfers between devices, local(): down_weights = lax.all_gather(down_half, ('dp', 'expert'), axis=0)  7.85 us
    pallas_call x1, Pallas kernels, local(): pl.pallas_call(functools.partial(down, parts), out_shape=jax.ShapeDtypeSt...  7.34 us
  transfers between devices with their start and end apart: 7, of which 4 were waited for; matrix products, arithmetic and copies ran while one was open for 1% of the time, Pallas kernels for 9%

profile of v11, /device:TPU:1, one launch (start us, length us, event | category | flops | bytes accessed | tf_op | source)
XLA Modules:
  0.0 238.8 jit_solution(16244905331596391614)
XLA Ops:
  6.5 0.0 copy-start
  6.5 0.0 copy-start.2
  6.5 0.0 copy-start.3
  6.5 0.0 copy-start.4
  6.5 0.0 all-gather.6.cloned.1.call-start
  6.6 2.2 pack.1
  8.8 0.0 all-gather.6.cloned.1.call-update
  8.8 0.0 all-gather.4.cloned.1.call-start
  8.9 0.0 copy-done
  8.9 0.8 constant_dynamic-slice_fusion
  9.6 0.0 all-gather.4.cloned.1.call-update
  9.7 0.0 copy-done.2
  9.7 0.0 copy-done.3
  9.7 0.0 copy-done.4
  9.7 0.4 compose.1
  10.1 52.4 %all_to_all.20 = bf16[32,384,128]{2,1,0:T(8,128)(2,1)} all-to-all(bf16[32,384,128]{2,1,0:T(8,128)(2,1)S(1)} %compose.1), channel_id=1, replica_groups={{0,1,2,3,4,5,6,7,8,9,10,11,12,13,14,15,16,17,18,19,20,21,22,23,24,25,26..., dimensions={0} | all-to-all | bytes 6291456 | tf_op jit(solution)/shard_map/all_to_all | solution.py:242
  62.5 8.1 %collective-permute-start.1 = (bf16[32,384,128]{2,1,0:T(8,128)(2,1)}, bf16[32,384,128]{2,1,0:T(8,128)(2,1)}, u32[]{:S(2)}, u32[]{:S(2)}) collective-permute-start(bf16[32,384,128]{2,1,0:T(8,128)(2,1)} %all_to_all.20), channel_id=1, source_target_pairs={{0,256},{256,0},{1,257},{257,1},{2,258},{258,2},{3,259},{259,3},{4... | collective-permute-start | bytes 9437192 | tf_op jit(solution)/shard_map/ppermute | solution.py:339
  70.6 3.1 %attend.1.attended_ref = bf16[2,128,256]{2,1,0:T(8,128)(2,1)} custom-call(s32[1]{0:T(128)} %bitcast.3.place_ref, bf16[128,512]{1,0:T(8,128)(2,1)} %query_ref.1, bf16[2,16,384,128]{3,2,1,0:T(8,128)(2,1)} %bitcast.5.piece_ref), custom_call_target="tpu_custom_call" | custom-call | tf_op jit(solution)/shard_map/attend/pallas_call | solution.py:341
  73.8 2.7 %collective-permute-start = (bf16[2,128,256]{2,1,0:T(8,128)(2,1)}, bf16[2,128,256]{2,1,0:T(8,128)(2,1)S(1)}, u32[]{:S(2)}, u32[]{:S(2)}) collective-permute-start(bf16[2,128,256]{2,1,0:T(8,128)(2,1)} %attend.1.attended_ref), channel_id=1, source_target_pairs={{0,16},{16,0},{32,48},{48,32},{64,80},{80,64},{96,112},{112,96},{1... | collective-permute-start | bytes 393224 | tf_op jit(solution)/shard_map/ppermute | solution.py:361
  76.4 0.0 collective-permute-done.1
  76.5 0.0 copy-start.1
  76.5 0.9 copy-done.1
  77.4 2.0 project.2.refs_0_
  79.4 1.6 collective-permute-done.attended_ref
  81.0 2.8 %project.3 = bf16[8,128,256]{2,1,0:T(8,128)(2,1)} custom-call(s32[1]{0:T(128)} %bitcast.2.core_ref, s32[1]{0:T(128)} %bitcast.1.source_ref.scalar_ref, bf16[2,128,256]{2,1,0:T(8,128)(2,1)S(1)} %collective-permute-done.attended_ref, bf16[2,8,2,384,128]{4,3,2,1,0:T(8,128)(2,1)} %bitcast.6.own_ref, bf16[2,8,2,384,128]{4,3,2,1,0:T(8,128)(2,1)} %bitcast.7.other_ref, ...), custom_call_target="tpu_custom_call" | custom-call | flops 268435456 | bytes 2097152 | tf_op jit(solution)/shard_map/project/pallas_call | solution.py:371
  83.8 0.0 copy-start.6
  83.8 15.1 %all-to-all-start.1 = ((bf16[8,128,256]{2,1,0:T(8,128)(2,1)}), bf16[8,128,256]{2,1,0:T(8,128)(2,1)S(1)}, u32[]{:S(2)}, u32[]{:S(2)}) async-start(bf16[8,128,256]{2,1,0:T(8,128)(2,1)} %project.3), calls=%async_computation.1 | async-start | bytes 1048576 | tf_op jit(solution)/shard_map/all_to_all | solution.py:242
  98.9 0.8 constant_dynamic-slice_fusion.2
  99.7 23.2 %all-to-all-done.1 = bf16[8,128,256]{2,1,0:T(8,128)(2,1)S(1)} async-done(((bf16[8,128,256]{2,1,0:T(8,128)(2,1)}), bf16[8,128,256]{2,1,0:T(8,128)(2,1)S(1)}, u32[]{:S(2)}, u32[]{:S(2)}) %all-to-all-start.1) | async-done | bytes 524320 | tf_op jit(solution)/shard_map/all_to_all | solution.py:242
  122.9 0.1 convert_reduce_fusion
  123.0 29.6 %all_to_all.21.rows_ref = bf16[8,128,256]{2,1,0:T(8,128)(2,1)S(1)} all-to-all(bf16[8,128,256]{2,1,0:T(8,128)(2,1)S(1)} %broadcast_in_dim.4), channel_id=1, replica_groups={{0,32,64,96,128,160,192,224},{16,48,80,112,144,176,208,240},{1,33,65,97..., dimensions={0} | all-to-all | bytes 1048576 | tf_op jit(solution)/shard_map/all_to_all | solution.py:242
  152.6 0.0 all-gather.6.cloned.1.call-done
  152.6 14.6 %collective-permute-start.2 = (bf16[8,128,256]{2,1,0:T(8,128)(2,1)S(1)}, bf16[8,128,256]{2,1,0:T(8,128)(2,1)S(1)}, u32[]{:S(2)}, u32[]{:S(2)}) collective-permute-start(bf16[8,128,256]{2,1,0:T(8,128)(2,1)S(1)} %all_to_all.21.rows_ref), channel_id=1, source_target_pairs={{0,16},{16,0},{32,48},{48,32},{64,80},{80,64},{96,112},{112,96},{1... | collective-permute-start | bytes 1572872 | tf_op jit(solution)/shard_map/ppermute | solution.py:400
  167.3 0.0 copy-done.6
  167.3 0.0 copy-start.5
  167.3 6.7 %gate_up.2 = (f32[2,1536,128]{2,1,0:T(8,128)S(1)}, f32[128,1]{1,0:T(8,128)S(1)}) custom-call(s32[1]{0:T(128)} %bitcast.odd_ref.source_ref.scalar_ref, bf16[8,128,256]{2,1,0:T(8,128)(2,1)S(1)} %all_to_all.21.rows_ref, f32[8,2,1,256]{3,2,1,0:T(1,128)S(1)} %bitcast.28, bf16[32,8,2,96,256]{4,3,2,1,0:T(8,128)(2,1)} %bitcast.31, bf16[32,8,2,96,256]{4,3,2,1,0:T(8,128)(2,1)} %bitcast.32), custom_call_target="tpu_custom_call" | custom-call | flops 1610612736 | bytes 12582912 | tf_op jit(solution)/shard_map/gate_up/pallas_call | solution.py:424
  174.0 5.1 %collective-permute-done.2.rows_ref = bf16[8,128,256]{2,1,0:T(8,128)(2,1)S(1)} collective-permute-done((bf16[8,128,256]{2,1,0:T(8,128)(2,1)S(1)}, bf16[8,128,256]{2,1,0:T(8,128)(2,1)S(1)}, u32[]{:S(2)}, u32[]{:S(2)}) %collective-permute-start.2) | collective-permute-done | bytes 524320 | tf_op jit(solution)/shard_map/ppermute | solution.py:400
  179.1 0.0 copy-done.5
  179.1 0.0 copy-start.7
  179.1 7.1 %gate_up.3 = bf16[192,128]{1,0:T(8,128)(2,1)S(1)} custom-call(s32[1]{0:T(128)} %bitcast.1.source_ref.scalar_ref, bf16[8,128,256]{2,1,0:T(8,128)(2,1)S(1)} %collective-permute-done.2.rows_ref, f32[8,2,1,256]{3,2,1,0:T(1,128)S(1)} %bitcast.29, bf16[32,8,2,96,256]{4,3,2,1,0:T(8,128)(2,1)} %bitcast.33, bf16[32,8,2,96,256]{4,3,2,1,0:T(8,128)(2,1)} %bitcast.34, ...), custom_call_target="tpu_custom_call" | custom-call | flops 1610612736 | bytes 12582912 | tf_op jit(solution)/shard_map/gate_up/pallas_call | solution.py:424
  186.2 0.1 broadcast_in_dim.5
  186.3 23.9 %all_to_all.22.own_ref = bf16[8,192,128]{2,1,0:T(8,128)(2,1)S(1)} all-to-all(bf16[8,192,128]{2,1,0:T(8,128)(2,1)S(1)} %broadcast_in_dim.5), channel_id=1, replica_groups={{0,32,64,96,128,160,192,224},{16,48,80,112,144,176,208,240},{1,33,65,97..., dimensions={0} | all-to-all | bytes 786432 | tf_op jit(solution)/shard_map/all_to_all | solution.py:242
  210.2 6.2 %collective-permute-start.3 = (bf16[8,192,128]{2,1,0:T(8,128)(2,1)S(1)}, bf16[8,192,128]{2,1,0:T(8,128)(2,1)S(1)}, u32[]{:S(2)}, u32[]{:S(2)}) collective-permute-start(bf16[8,192,128]{2,1,0:T(8,128)(2,1)S(1)} %all_to_all.22.own_ref), channel_id=1, source_target_pairs={{0,16},{16,0},{32,48},{48,32},{64,80},{80,64},{96,112},{112,96},{1... | collective-permute-start | bytes 1179656 | tf_op jit(solution)/shard_map/ppermute | solution.py:446
  216.5 0.1 copy.18.routes_ref
  216.6 0.0 copy-done.7
  216.6 0.1 copy.19.route_weight_ref
  216.8 7.8 %all-gather.4.cloned.1.call-done = bf16[32,768,256]{2,1,0:T(8,128)(2,1)} async-done(((bf16[1,768,256]{2,1,0:T(8,128)(2,1)}), bf16[32,768,256]{2,1,0:T(8,128)(2,1)}) %all-gather.4.cloned.1.call-update) | async-done | bytes 12582928 | tf_op jit(solution)/shard_map/all_gather | solution.py:337
  224.6 0.0 collective-permute-done.3.neighbour_ref
  224.6 7.3 %down.1 = bf16[128,256]{1,0:T(8,128)(2,1)} custom-call(s32[1]{0:T(128)} %bitcast.odd_ref.source_ref.scalar_ref, bf16[8,192,128]{2,1,0:T(8,128)(2,1)S(1)} %all_to_all.22.own_ref, bf16[8,192,128]{2,1,0:T(8,128)(2,1)S(1)} %collective-permute-done.3.neighbour_ref, s32[128,2]{1,0:T(8,128)S(1)} %copy.18.routes_ref, f32[128,2]{1,0:T(8,128)S(1)} %copy.19.route_weight_ref, ...), custom_call_target="tpu_custom_call" | custom-call | flops 1610612736 | bytes 12582912 | tf_op jit(solution)/shard_map/down/pallas_call | solution.py:468
  (6 shorter events, 0.1 us)
Async XLA Ops:
  6.5 2.3 copy-start
  6.5 3.1 %copy-start.2 = (bf16[512,256]{1,0:T(8,128)(2,1)S(1)}, bf16[512,256]{1,0:T(8,128)(2,1)}, u32[]{:S(2)}) copy-start(bf16[512,256]{1,0:T(8,128)(2,1)} %weight_ref.1) | copy-start | bytes 786436
  6.5 3.2 %copy-start.3 = (bf16[128,512]{1,0:T(8,128)(2,1)S(1)}, bf16[128,512]{1,0:T(8,128)(2,1)}, u32[]{:S(2)}) copy-start(bf16[128,512]{1,0:T(8,128)(2,1)} %key_ref.1) | copy-start | bytes 393220
  6.5 3.2 %copy-start.4 = (bf16[128,512]{1,0:T(8,128)(2,1)S(1)}, bf16[128,512]{1,0:T(8,128)(2,1)}, u32[]{:S(2)}) copy-start(bf16[128,512]{1,0:T(8,128)(2,1)} %value_ref.1) | copy-start | bytes 393220
  6.5 146.1 %all-gather.6.cloned.1.call-start = ((), (), s32[]{:S(2)}) async-start(), calls=%async_computation.5 | async-start | bytes 25952256 | tf_op jit(solution)/shard_map/all_gather | solution.py:336
  8.8 215.8 %all-gather.4.cloned.1.call-start = ((), (), s32[]{:S(2)}) async-start(), calls=%async_computation.4 | async-start | bytes 12976128 | tf_op jit(solution)/shard_map/all_gather | solution.py:337
  62.5 14.0 %collective-permute-start.1 = (bf16[32,384,128]{2,1,0:T(8,128)(2,1)}, bf16[32,384,128]{2,1,0:T(8,128)(2,1)}, u32[]{:S(2)}, u32[]{:S(2)}) collective-permute-start(bf16[32,384,128]{2,1,0:T(8,128)(2,1)} %all_to_all.20), channel_id=1, source_target_pairs={{0,256},{256,0},{1,257},{257,1},{2,258},{258,2},{3,259},{259,3},{4... | collective-permute-start | bytes 9437192 | tf_op jit(solution)/shard_map/ppermute | solution.py:339
  73.8 7.2 %collective-permute-start = (bf16[2,128,256]{2,1,0:T(8,128)(2,1)}, bf16[2,128,256]{2,1,0:T(8,128)(2,1)S(1)}, u32[]{:S(2)}, u32[]{:S(2)}) collective-permute-start(bf16[2,128,256]{2,1,0:T(8,128)(2,1)} %attend.1.attended_ref), channel_id=1, source_target_pairs={{0,16},{16,0},{32,48},{48,32},{64,80},{80,64},{96,112},{112,96},{1... | collective-permute-start | bytes 393224 | tf_op jit(solution)/shard_map/ppermute | solution.py:361
  76.5 0.9 copy-start.1
  83.8 83.5 %copy-start.6 = (f32[4096]{0:T(1024)S(1)}, f32[4096]{0:T(1024)}, u32[]{:S(2)}) copy-start(f32[4096]{0:T(1024)} %param.16) | copy-start | bytes 49156
  83.8 39.1 %all-to-all-start.1 = ((bf16[8,128,256]{2,1,0:T(8,128)(2,1)}), bf16[8,128,256]{2,1,0:T(8,128)(2,1)S(1)}, u32[]{:S(2)}, u32[]{:S(2)}) async-start(bf16[8,128,256]{2,1,0:T(8,128)(2,1)} %project.3), calls=%async_computation.1 | async-start | bytes 1048576 | tf_op jit(solution)/shard_map/all_to_all | solution.py:242
  152.6 26.5 %collective-permute-start.2 = (bf16[8,128,256]{2,1,0:T(8,128)(2,1)S(1)}, bf16[8,128,256]{2,1,0:T(8,128)(2,1)S(1)}, u32[]{:S(2)}, u32[]{:S(2)}) collective-permute-start(bf16[8,128,256]{2,1,0:T(8,128)(2,1)S(1)} %all_to_all.21.rows_ref), channel_id=1, source_target_pairs={{0,16},{16,0},{32,48},{48,32},{64,80},{80,64},{96,112},{112,96},{1... | collective-permute-start | bytes 1572872 | tf_op jit(solution)/shard_map/ppermute | solution.py:400
  167.3 11.8 %copy-start.5 = (s32[128,2]{0,1:T(2,128)S(1)}, s32[128,2]{0,1:T(2,128)}, u32[]{:S(2)}) copy-start(s32[128,2]{0,1:T(2,128)} %param.17) | copy-start | bytes 3076
  179.1 37.5 %copy-start.7 = (f32[128,2]{0,1:T(2,128)S(1)}, f32[128,2]{0,1:T(2,128)}, u32[]{:S(2)}) copy-start(f32[128,2]{0,1:T(2,128)} %param.18) | copy-start | bytes 3076
  210.2 14.4 %collective-permute-start.3 = (bf16[8,192,128]{2,1,0:T(8,128)(2,1)S(1)}, bf16[8,192,128]{2,1,0:T(8,128)(2,1)S(1)}, u32[]{:S(2)}, u32[]{:S(2)}) collective-permute-start(bf16[8,192,128]{2,1,0:T(8,128)(2,1)S(1)} %all_to_all.22.own_ref), channel_id=1, source_target_pairs={{0,16},{16,0},{32,48},{48,32},{64,80},{80,64},{96,112},{112,96},{1... | collective-permute-start | bytes 1179656 | tf_op jit(solution)/shard_map/ppermute | solution.py:446
Sparse Core Ops, SparseCore 0:
  10.5 133.2 all-gather.5
  146.9 77.7 all-gather.3

commit v12 on v10

--- a/solution.py
+++ b/solution.py
@@ -184,19 +184,27 @@
                 out_ref[k * units : (k + 1) * units] = chosen[k].astype(out_ref.dtype)
 
 
-def down(parts, scalar_ref, activation_ref, routes_ref, route_weight_ref, start_ref, *refs):
+def turn(activation_ref, out_ref):
+    units = activation_ref.shape[1] // TOP
+    blocks = activation_ref.shape[0] // 2
+    for half in range(2):
+        for k in range(TOP):
+            part = activation_ref[blocks * half : blocks * (half + 1), k * units : (k + 1) * units]
+            part = part.reshape(blocks * units, part.shape[2]).astype(jnp.float32)
+            out_ref[half, k] = jnp.transpose(part).astype(out_ref.dtype)
+
+
+def down(ready, parts, scalar_ref, activation_ref, routes_ref, route_weight_ref, start_ref, *refs):
     half_refs = refs[:parts], refs[parts : 2 * parts]
-    out_ref, turned, mixed = refs[2 * parts :]
+    out_ref, mixed = refs[2 * parts : 2 * parts + 2]
+    turned = activation_ref if ready else refs[-1]
     step = pl.program_id(0)
     per_part, blocks, _, units, columns = refs[0].shape
 
     @pl.when(step == 0)
     def _():
-        for half in range(2):
-            for k in range(TOP):
-                part = activation_ref[blocks * half : blocks * (half + 1), k * units : (k + 1) * units]
-                part = part.reshape(blocks * units, part.shape[2]).astype(jnp.float32)
-                turned[half, k] = jnp.transpose(part).astype(turned.dtype)
+        if not ready:
+            turn(activation_ref, turned)
         mixed[...] = start_ref[...]
 
     for part in range(parts):
@@ -272,14 +280,17 @@
 
     first_blocks = D // columns
 
-    span = 1024
+    span = 2048
     gate_or_up = pl.pallas_call(
         pack,
         out_shape=jax.ShapeDtypeStruct((first_blocks * local_units, columns), jnp.bfloat16),
         grid_spec=pltpu.PrefetchScalarGridSpec(
             num_scalar_prefetch=1,
             grid=(D // span,),
-            in_specs=[pl.BlockSpec((local_units, span), lambda i, core_ref: (0, i))] * 2,
+            in_specs=[
+                pl.BlockSpec((local_units, span), lambda i, core_ref: (0, i * (1 - core_ref[0]))),
+                pl.BlockSpec((local_units, span), lambda i, core_ref: (0, i * core_ref[0])),
+            ],
             out_specs=pl.BlockSpec((span // columns * local_units, columns), lambda i, core_ref: (i, 0)),
         ),
         compiler_params=WIDE,
@@ -440,46 +451,46 @@
     down_steps = expert_count // (parts * per_part)
     quarter = PAIRS // 2
     down_weights = down_weights.reshape(2 * expert_count, quarter, 2, local_units, columns)
+    turned_type = jax.ShapeDtypeStruct((2, TOP, tokens, quarter * local_units), jnp.bfloat16)
 
     def down_spec(half, part):
         return pl.BlockSpec(
             (per_part, quarter, 1, local_units, columns),
-            lambda i, scalar_ref: (
-                (half * down_steps + i) * parts + part,
-                0,
-                scalar_ref[0],
-                0,
-                0,
-            ),
-        )
-
-    def lowered(parity, rows, start, dtype):
+            lambda i, parity_ref: ((half * down_steps + i) * parts + part, 0, parity_ref[0], 0, 0),
+        )
+
+    def lowered(ready, parity, rows, start, dtype):
+        scratch = [pltpu.VMEM((tokens, columns), jnp.float32)]
+        if not ready:
+            scratch.append(pltpu.VMEM(turned_type.shape, turned_type.dtype))
         return pl.pallas_call(
-            functools.partial(down, parts),
+            functools.partial(down, ready, parts),
             out_shape=jax.ShapeDtypeStruct((tokens, columns), dtype),
             grid_spec=pltpu.PrefetchScalarGridSpec(
                 num_scalar_prefetch=1,
                 grid=(down_steps,),
-                in_specs=[
-                    whole(PAIRS, TOP * local_units, tokens),
-                    whole(tokens, TOP),
-                    whole(tokens, TOP),
-                    whole(tokens, columns),
-                ]
+                in_specs=[HERE] * 4
                 + [down_spec(half, part) for half in range(2) for part in range(parts)],
                 out_specs=whole(tokens, columns),
-                scratch_shapes=[
-                    pltpu.VMEM((2, TOP, tokens, quarter * local_units), jnp.bfloat16),
-                    pltpu.VMEM((tokens, columns), jnp.float32),
-                ],
+                scratch_shapes=scratch,
             ),
             compiler_params=LARGE,
             cost_estimate=cost(
-                2 * tokens * expert_count * hidden_units * columns // 2,
-                2 * expert_count * hidden_units * columns // 2,
+                tokens * expert_count * hidden_units * columns,
+                expert_count * hidden_units * columns,
             ),
             name="down",
         )(parity.reshape(1), rows, routes, route_weight, start, *[down_weights] * (2 * parts))
+
+    turned_own = pl.pallas_call(
+        turn,
+        out_shape=turned_type,
+        in_specs=[HERE],
+        out_specs=HERE,
+        compiler_params=LIMIT,
+        name="turn",
+    )(activation_own)
+    turned_own, down_weights = lax.optimization_barrier((turned_own, down_weights))
 
     shares = [
         lax.dynamic_slice(
@@ -490,8 +501,8 @@
     hidden_here = jnp.where(
         odd == 0, jnp.concatenate(shares, axis=1), jnp.concatenate(shares[::-1], axis=1)
     )
-    mixed = lowered(odd, activation_own, hidden_here, jnp.float32)
-    return lowered(1 - odd, activation_other, mixed, jnp.bfloat16)
+    mixed = lowered(True, odd, turned_own, hidden_here, jnp.float32)
+    return lowered(False, 1 - odd, activation_other, mixed, jnp.bfloat16)
 
 
 def solution(mesh):

time: 243 us -> 241 us (level)
    pallas_call x2 -> x3, Pallas kernels: 9 us -> 8.96 us  [the longest x2 8.79 us: lowered(): pl.pallas_call(functools.partial(down, ready, parts), out_shape=jax.Shape...]
where the time goes in v12:
time: 241 us; the launch traced here: 240 us
  blocking collectives  81.9 us (34%)
  waiting for transfers between devices  57.6 us (24%)
  starting transfers between devices  50.2 us (21%)
  Pallas kernels  33.2 us (14%)
  between operations  13.7 us (6%)
  local copies, waits for them, and re-layouts  3.56 us (1%)
    all_to_all x2, blocking collectives, exchange(): lax.all_to_all(message, axis, split_axis=0, concat_axis=0, tiled=True, ax...  81.9 us
    all_to_all x2, waiting for transfers between devices, exchange(): lax.all_to_all(message, axis, split_axis=0, concat_axis=0, tiled=True, ax...  42 us
    all_to_all x2, starting transfers between devices, exchange(): lax.all_to_all(message, axis, split_axis=0, concat_axis=0, tiled=True, ax...  19.1 us
    ppermute x1, starting transfers between devices, local(): rows_other = lax.ppermute(rows_own, 'tensor', NEIGHBOUR)  14.5 us
    pallas_call x2, Pallas kernels, gated(): pl.pallas_call(functools.partial(gate_up, last), out_shape=out_type if la...  13.7 us
    all_gather x1, waiting for transfers between devices, local(): down_weights = lax.all_gather(down_half, ('dp', 'expert'), axis=0)  8.96 us
    pallas_call x2, Pallas kernels, lowered(): pl.pallas_call(functools.partial(down, ready, parts), out_shape=jax.Shape...  8.79 us
    ppermute x1, starting transfers between devices, local(): gathered_other = lax.ppermute(gathered, 'dp', SWAP)  8.13 us
  transfers between devices with their start and end apart: 8, of which 5 were waited for; matrix products, arithmetic and copies ran while one was open for 1% of the time, Pallas kernels for 11%

profile of v12, /device:TPU:1, one launch (start us, length us, event | category | flops | bytes accessed | tf_op | source)
XLA Modules:
  0.0 240.3 jit_solution(2133373990764819333)
XLA Ops:
  6.5 0.0 copy-start
  6.5 0.0 copy-start.2
  6.5 0.0 copy-start.3
  6.5 0.0 copy-start.4
  6.5 0.0 all-gather.6.cloned.1.call-start
  6.6 2.2 pack.1
  8.8 0.0 all-gather.6.cloned.1.call-update
  8.8 0.0 all-gather.4.cloned.1.call-start
  8.8 0.0 copy-done
  8.8 0.8 constant_dynamic-slice_fusion
  9.6 0.0 all-gather.4.cloned.1.call-update
  9.7 0.0 copy-done.2
  9.7 0.0 copy-done.3
  9.7 0.0 copy-done.4
  9.7 0.4 compose.1
  10.1 52.3 %all_to_all.20 = bf16[32,384,128]{2,1,0:T(8,128)(2,1)} all-to-all(bf16[32,384,128]{2,1,0:T(8,128)(2,1)S(1)} %compose.1), channel_id=1, replica_groups={{0,1,2,3,4,5,6,7,8,9,10,11,12,13,14,15,16,17,18,19,20,21,22,23,24,25,26..., dimensions={0} | all-to-all | bytes 6291456 | tf_op jit(solution)/shard_map/all_to_all | solution.py:244
  62.5 8.1 %collective-permute-start.1 = (bf16[32,384,128]{2,1,0:T(8,128)(2,1)}, bf16[32,384,128]{2,1,0:T(8,128)(2,1)}, u32[]{:S(2)}, u32[]{:S(2)}) collective-permute-start(bf16[32,384,128]{2,1,0:T(8,128)(2,1)} %all_to_all.20), channel_id=1, source_target_pairs={{0,256},{256,0},{1,257},{257,1},{2,258},{258,2},{3,259},{259,3},{4... | collective-permute-start | bytes 9437192 | tf_op jit(solution)/shard_map/ppermute | solution.py:341
  70.6 3.1 %attend.1.attended_ref = bf16[2,128,256]{2,1,0:T(8,128)(2,1)} custom-call(s32[1]{0:T(128)} %bitcast.2.place_ref, bf16[128,512]{1,0:T(8,128)(2,1)} %query_ref.1, bf16[2,16,384,128]{3,2,1,0:T(8,128)(2,1)} %bitcast.5.piece_ref), custom_call_target="tpu_custom_call" | custom-call | tf_op jit(solution)/shard_map/attend/pallas_call | solution.py:343
  73.7 2.7 %collective-permute-start = (bf16[2,128,256]{2,1,0:T(8,128)(2,1)}, bf16[2,128,256]{2,1,0:T(8,128)(2,1)S(1)}, u32[]{:S(2)}, u32[]{:S(2)}) collective-permute-start(bf16[2,128,256]{2,1,0:T(8,128)(2,1)} %attend.1.attended_ref), channel_id=1, source_target_pairs={{0,16},{16,0},{32,48},{48,32},{64,80},{80,64},{96,112},{112,96},{1... | collective-permute-start | bytes 393224 | tf_op jit(solution)/shard_map/ppermute | solution.py:363
  76.4 0.0 collective-permute-done.1
  76.4 0.0 copy-start.1
  76.4 0.9 copy-done.1
  77.4 2.0 project.2.refs_0_
  79.4 1.6 collective-permute-done.attended_ref
  80.9 2.8 %project.3 = bf16[8,128,256]{2,1,0:T(8,128)(2,1)} custom-call(s32[1]{0:T(128)} %bitcast.1.core_ref, s32[1]{0:T(128)} %bitcast.source_ref.scalar_ref, bf16[2,128,256]{2,1,0:T(8,128)(2,1)S(1)} %collective-permute-done.attended_ref, bf16[2,8,2,384,128]{4,3,2,1,0:T(8,128)(2,1)} %bitcast.6.own_ref, bf16[2,8,2,384,128]{4,3,2,1,0:T(8,128)(2,1)} %bitcast.7.other_ref, ...), custom_call_target="tpu_custom_call" | custom-call | flops 268435456 | bytes 2097152 | tf_op jit(solution)/shard_map/project/pallas_call | solution.py:373
  83.7 0.0 copy-start.6
  83.7 15.2 %all-to-all-start.1 = ((bf16[8,128,256]{2,1,0:T(8,128)(2,1)}), bf16[8,128,256]{2,1,0:T(8,128)(2,1)S(1)}, u32[]{:S(2)}, u32[]{:S(2)}) async-start(bf16[8,128,256]{2,1,0:T(8,128)(2,1)} %project.3), calls=%async_computation.1 | async-start | bytes 1048576 | tf_op jit(solution)/shard_map/all_to_all | solution.py:244
  98.9 0.8 constant_dynamic-slice_fusion.2
  99.7 23.2 %all-to-all-done.1 = bf16[8,128,256]{2,1,0:T(8,128)(2,1)S(1)} async-done(((bf16[8,128,256]{2,1,0:T(8,128)(2,1)}), bf16[8,128,256]{2,1,0:T(8,128)(2,1)S(1)}, u32[]{:S(2)}, u32[]{:S(2)}) %all-to-all-start.1) | async-done | bytes 524320 | tf_op jit(solution)/shard_map/all_to_all | solution.py:244
  122.9 0.1 convert_reduce_fusion
  123.0 29.6 %all_to_all.21.rows_ref = bf16[8,128,256]{2,1,0:T(8,128)(2,1)S(1)} all-to-all(bf16[8,128,256]{2,1,0:T(8,128)(2,1)S(1)} %broadcast_in_dim.4), channel_id=1, replica_groups={{0,32,64,96,128,160,192,224},{16,48,80,112,144,176,208,240},{1,33,65,97..., dimensions={0} | all-to-all | bytes 1048576 | tf_op jit(solution)/shard_map/all_to_all | solution.py:244
  152.6 0.0 all-gather.6.cloned.1.call-done
  152.6 14.5 %collective-permute-start.2 = (bf16[8,128,256]{2,1,0:T(8,128)(2,1)S(1)}, bf16[8,128,256]{2,1,0:T(8,128)(2,1)S(1)}, u32[]{:S(2)}, u32[]{:S(2)}) collective-permute-start(bf16[8,128,256]{2,1,0:T(8,128)(2,1)S(1)} %all_to_all.21.rows_ref), channel_id=1, source_target_pairs={{0,16},{16,0},{32,48},{48,32},{64,80},{80,64},{96,112},{112,96},{1... | collective-permute-start | bytes 1572872 | tf_op jit(solution)/shard_map/ppermute | solution.py:402
  167.2 0.0 copy-done.6
  167.2 0.0 copy-start.5
  167.2 6.7 %gate_up.2 = (f32[2,1536,128]{2,1,0:T(8,128)S(1)}, f32[128,1]{1,0:T(8,128)S(1)}) custom-call(s32[1]{0:T(128)} %bitcast.3.odd_ref.source_ref.scalar_ref, bf16[8,128,256]{2,1,0:T(8,128)(2,1)S(1)} %all_to_all.21.rows_ref, f32[8,2,1,256]{3,2,1,0:T(1,128)S(1)} %bitcast.28, bf16[32,8,2,96,256]{4,3,2,1,0:T(8,128)(2,1)} %bitcast.39, ...), custom_call_target="tpu_custom_call" | custom-call | flops 1610612736 | bytes 12582912 | tf_op jit(solution)/shard_map/gate_up/pallas_call | solution.py:426
  173.9 5.0 %collective-permute-done.2.rows_ref = bf16[8,128,256]{2,1,0:T(8,128)(2,1)S(1)} collective-permute-done((bf16[8,128,256]{2,1,0:T(8,128)(2,1)S(1)}, bf16[8,128,256]{2,1,0:T(8,128)(2,1)S(1)}, u32[]{:S(2)}, u32[]{:S(2)}) %collective-permute-start.2) | collective-permute-done | bytes 524320 | tf_op jit(solution)/shard_map/ppermute | solution.py:402
  178.9 0.0 copy-done.5
  178.9 0.0 copy-start.7
  178.9 7.1 %gate_up.3 = bf16[192,128]{1,0:T(8,128)(2,1)S(1)} custom-call(s32[1]{0:T(128)} %bitcast.source_ref.scalar_ref, bf16[8,128,256]{2,1,0:T(8,128)(2,1)S(1)} %collective-permute-done.2.rows_ref, f32[8,2,1,256]{3,2,1,0:T(1,128)S(1)} %bitcast.29, bf16[32,8,2,96,256]{4,3,2,1,0:T(8,128)(2,1)} %bitcast.41, bf16[32,8,2,96,256]{4,3,2,1,0:T(8,128)(2,1)} %bitcast.42, ...), custom_call_target="tpu_custom_call" | custom-call | flops 1610612736 | bytes 12582912 | tf_op jit(solution)/shard_map/gate_up/pallas_call | solution.py:426
  185.9 0.8 broadcast_in_dim.5
  186.7 3.9 %all-to-all-start.3 = ((bf16[8,192,128]{2,1,0:T(8,128)(2,1)}), bf16[8,192,128]{2,1,0:T(8,128)(2,1)S(1)}, u32[]{:S(2)}, u32[]{:S(2)}) async-start(bf16[8,192,128]{2,1,0:T(8,128)(2,1)} %broadcast_in_dim.5), calls=%async_computation.3 | async-start | bytes 786432 | tf_op jit(solution)/shard_map/all_to_all | solution.py:244
  190.7 0.1 copy.24.routes_ref
  190.8 0.0 copy-done.7
  190.8 0.1 copy.25.route_weight_ref
  190.9 18.8 %all-to-all-done.3.activation_ref = bf16[8,192,128]{2,1,0:T(8,128)(2,1)S(1)} async-done(((bf16[8,192,128]{2,1,0:T(8,128)(2,1)}), bf16[8,192,128]{2,1,0:T(8,128)(2,1)S(1)}, u32[]{:S(2)}, u32[]{:S(2)}) %all-to-all-start.3) | async-done | bytes 393248 | tf_op jit(solution)/shard_map/all_to_all | solution.py:244
  209.7 5.7 %collective-permute-start.3 = (bf16[8,192,128]{2,1,0:T(8,128)(2,1)S(1)}, bf16[8,192,128]{2,1,0:T(8,128)(2,1)S(1)}, u32[]{:S(2)}, u32[]{:S(2)}) collective-permute-start(bf16[8,192,128]{2,1,0:T(8,128)(2,1)S(1)} %all-to-all-done.3.activation_ref), channel_id=1, source_target_pairs={{0,16},{16,0},{32,48},{48,32},{64,80},{80,64},{96,112},{112,96},{1... | collective-permute-start | bytes 1179656 | tf_op jit(solution)/shard_map/ppermute | solution.py:448
  215.5 0.2 turn.1.activation_ref
  215.7 9.0 %all-gather.4.cloned.1.call-done = bf16[32,768,256]{2,1,0:T(8,128)(2,1)} async-done(((bf16[1,768,256]{2,1,0:T(8,128)(2,1)}), bf16[32,768,256]{2,1,0:T(8,128)(2,1)}) %all-gather.4.cloned.1.call-update) | async-done | bytes 12582928 | tf_op jit(solution)/shard_map/all_gather | solution.py:339
  224.6 4.0 %down.2.start_ref = f32[128,256]{1,0:T(8,128)S(1)} custom-call(s32[1]{0:T(128)} %bitcast.3.odd_ref.source_ref.scalar_ref, bf16[2,2,128,384]{3,2,1,0:T(8,128)(2,1)S(1)} %turn.1.activation_ref, s32[128,2]{1,0:T(8,128)S(1)} %copy.24.routes_ref, f32[128,2]{1,0:T(8,128)S(1)} %copy.25.route_weight_ref, f32[128,256]{1,0:T(8,128)S(1)} %maximum_select_fusion.start_ref, ...), custom_call_target="tpu_custom_call" | custom-call | flops 805306368 | bytes 6291456 | tf_op jit(solution)/shard_map/down/pallas_call | solution.py:466
  228.6 0.0 collective-permute-done.3.activation_ref
  228.6 4.8 %down.3 = bf16[128,256]{1,0:T(8,128)(2,1)} custom-call(s32[1]{0:T(128)} %bitcast.source_ref.scalar_ref, bf16[8,192,128]{2,1,0:T(8,128)(2,1)S(1)} %collective-permute-done.3.activation_ref, s32[128,2]{1,0:T(8,128)S(1)} %copy.24.routes_ref, f32[128,2]{1,0:T(8,128)S(1)} %copy.25.route_weight_ref, f32[128,256]{1,0:T(8,128)S(1)} %down.2.start_ref, ...), custom_call_target="tpu_custom_call" | custom-call | flops 805306368 | bytes 6291456 | tf_op jit(solution)/shard_map/down/pallas_call | solution.py:466
  (6 shorter events, 0.1 us)
Async XLA Ops:
  6.5 2.3 copy-start
  6.5 3.1 %copy-start.2 = (bf16[512,256]{1,0:T(8,128)(2,1)S(1)}, bf16[512,256]{1,0:T(8,128)(2,1)}, u32[]{:S(2)}) copy-start(bf16[512,256]{1,0:T(8,128)(2,1)} %weight_ref.1) | copy-start | bytes 786436
  6.5 3.1 %copy-start.3 = (bf16[128,512]{1,0:T(8,128)(2,1)S(1)}, bf16[128,512]{1,0:T(8,128)(2,1)}, u32[]{:S(2)}) copy-start(bf16[128,512]{1,0:T(8,128)(2,1)} %key_ref.1) | copy-start | bytes 393220
  6.5 3.1 %copy-start.4 = (bf16[128,512]{1,0:T(8,128)(2,1)S(1)}, bf16[128,512]{1,0:T(8,128)(2,1)}, u32[]{:S(2)}) copy-start(bf16[128,512]{1,0:T(8,128)(2,1)} %value_ref.1) | copy-start | bytes 393220
  6.5 146.1 %all-gather.6.cloned.1.call-start = ((), (), s32[]{:S(2)}) async-start(), calls=%async_computation.5 | async-start | bytes 25952256 | tf_op jit(solution)/shard_map/all_gather | solution.py:338
  8.8 215.8 %all-gather.4.cloned.1.call-start = ((), (), s32[]{:S(2)}) async-start(), calls=%async_computation.4 | async-start | bytes 12976128 | tf_op jit(solution)/shard_map/all_gather | solution.py:339
  62.5 13.9 %collective-permute-start.1 = (bf16[32,384,128]{2,1,0:T(8,128)(2,1)}, bf16[32,384,128]{2,1,0:T(8,128)(2,1)}, u32[]{:S(2)}, u32[]{:S(2)}) collective-permute-start(bf16[32,384,128]{2,1,0:T(8,128)(2,1)} %all_to_all.20), channel_id=1, source_target_pairs={{0,256},{256,0},{1,257},{257,1},{2,258},{258,2},{3,259},{259,3},{4... | collective-permute-start | bytes 9437192 | tf_op jit(solution)/shard_map/ppermute | solution.py:341
  73.7 7.2 %collective-permute-start = (bf16[2,128,256]{2,1,0:T(8,128)(2,1)}, bf16[2,128,256]{2,1,0:T(8,128)(2,1)S(1)}, u32[]{:S(2)}, u32[]{:S(2)}) collective-permute-start(bf16[2,128,256]{2,1,0:T(8,128)(2,1)} %attend.1.attended_ref), channel_id=1, source_target_pairs={{0,16},{16,0},{32,48},{48,32},{64,80},{80,64},{96,112},{112,96},{1... | collective-permute-start | bytes 393224 | tf_op jit(solution)/shard_map/ppermute | solution.py:363
  76.4 0.9 copy-start.1
  83.7 83.4 %copy-start.6 = (f32[4096]{0:T(1024)S(1)}, f32[4096]{0:T(1024)}, u32[]{:S(2)}) copy-start(f32[4096]{0:T(1024)} %param.16) | copy-start | bytes 49156
  83.7 39.2 %all-to-all-start.1 = ((bf16[8,128,256]{2,1,0:T(8,128)(2,1)}), bf16[8,128,256]{2,1,0:T(8,128)(2,1)S(1)}, u32[]{:S(2)}, u32[]{:S(2)}) async-start(bf16[8,128,256]{2,1,0:T(8,128)(2,1)} %project.3), calls=%async_computation.1 | async-start | bytes 1048576 | tf_op jit(solution)/shard_map/all_to_all | solution.py:244
  152.6 26.3 %collective-permute-start.2 = (bf16[8,128,256]{2,1,0:T(8,128)(2,1)S(1)}, bf16[8,128,256]{2,1,0:T(8,128)(2,1)S(1)}, u32[]{:S(2)}, u32[]{:S(2)}) collective-permute-start(bf16[8,128,256]{2,1,0:T(8,128)(2,1)S(1)} %all_to_all.21.rows_ref), channel_id=1, source_target_pairs={{0,16},{16,0},{32,48},{48,32},{64,80},{80,64},{96,112},{112,96},{1... | collective-permute-start | bytes 1572872 | tf_op jit(solution)/shard_map/ppermute | solution.py:402
  167.2 11.7 %copy-start.5 = (s32[128,2]{0,1:T(2,128)S(1)}, s32[128,2]{0,1:T(2,128)}, u32[]{:S(2)}) copy-start(s32[128,2]{0,1:T(2,128)} %param.17) | copy-start | bytes 3076
  178.9 11.9 %copy-start.7 = (f32[128,2]{0,1:T(2,128)S(1)}, f32[128,2]{0,1:T(2,128)}, u32[]{:S(2)}) copy-start(f32[128,2]{0,1:T(2,128)} %param.18) | copy-start | bytes 3076
  186.7 23.0 %all-to-all-start.3 = ((bf16[8,192,128]{2,1,0:T(8,128)(2,1)}), bf16[8,192,128]{2,1,0:T(8,128)(2,1)S(1)}, u32[]{:S(2)}, u32[]{:S(2)}) async-start(bf16[8,192,128]{2,1,0:T(8,128)(2,1)} %broadcast_in_dim.5), calls=%async_computation.3 | async-start | bytes 786432 | tf_op jit(solution)/shard_map/all_to_all | solution.py:244
  209.7 18.9 %collective-permute-start.3 = (bf16[8,192,128]{2,1,0:T(8,128)(2,1)S(1)}, bf16[8,192,128]{2,1,0:T(8,128)(2,1)S(1)}, u32[]{:S(2)}, u32[]{:S(2)}) collective-permute-start(bf16[8,192,128]{2,1,0:T(8,128)(2,1)S(1)} %all-to-all-done.3.activation_ref), channel_id=1, source_target_pairs={{0,16},{16,0},{32,48},{48,32},{64,80},{80,64},{96,112},{112,96},{1... | collective-permute-start | bytes 1179656 | tf_op jit(solution)/shard_map/ppermute | solution.py:448
Sparse Core Ops, SparseCore 0:
  10.5 133.1 all-gather.5
  146.9 77.7 all-gather.3

commit v13 on v12

--- a/solution.py
+++ b/solution.py
@@ -130,7 +130,7 @@
     else:
         totals, square, scaled = refs
     step = pl.program_id(0)
-    experts, per_step, _, units, columns = gate_ref.shape
+    experts, _, per_step, _, units, columns = gate_ref.shape
     pieces, tokens, _ = rows_ref.shape
     together = 2 * units
 
@@ -151,7 +151,7 @@
                 product = None if start is None else start[which, place]
                 for piece in range(per_step):
                     part = lax.dot_general(
-                        weight_ref[expert : expert + 2, piece, 0].reshape(together, columns),
+                        weight_ref[expert : expert + 2, 0, piece, 0].reshape(together, columns),
                         scaled[step * per_step + piece],
                         CONTRACT_LAST,
                         preferred_element_type=jnp.float32,
@@ -199,7 +199,7 @@
     out_ref, mixed = refs[2 * parts : 2 * parts + 2]
     turned = activation_ref if ready else refs[-1]
     step = pl.program_id(0)
-    per_part, blocks, _, units, columns = refs[0].shape
+    per_part, _, blocks, _, units, columns = refs[0].shape
 
     @pl.when(step == 0)
     def _():
@@ -335,8 +335,8 @@
         [(2 * pair + side) * expert_count + place for side in range(2) for place in range(expert_count)]
         for pair in range(PAIRS)
     ]
-    weights = lax.all_gather(gate_or_up, ("dp", "expert"), axis=0)
-    down_weights = lax.all_gather(down_half, ("dp", "expert"), axis=0)
+    weights = lax.all_gather(gate_or_up, ("expert", "dp"), axis=0)
+    down_weights = lax.all_gather(down_half, ("expert", "dp"), axis=0)
     gathered = exchange(message, ("tensor", "expert"), both)
     gathered_other = lax.ppermute(gathered, "dp", SWAP)
 
@@ -400,7 +400,7 @@
     rows_own = spread(hidden_share.astype(jnp.bfloat16), "tensor", PAIRS, PARITY)
     rows_own, weights = lax.optimization_barrier((rows_own, weights))
     rows_other = lax.ppermute(rows_own, "tensor", NEIGHBOUR)
-    weights = weights.reshape(2 * expert_count, PAIRS, 2, local_units, columns)
+    weights = weights.reshape(expert_count, 2, PAIRS, 2, local_units, columns)
 
     per_step = 4
     gains = jnp.transpose(post_gain.reshape(PAIRS, 2, 2, half_columns), (0, 2, 1, 3)).reshape(
@@ -414,8 +414,8 @@
 
     def first_spec(which):
         return pl.BlockSpec(
-            (expert_count, per_step, 1, local_units, columns),
-            lambda i, parity_ref: (which, i, parity_ref[0], 0, 0),
+            (expert_count, 1, per_step, 1, local_units, columns),
+            lambda i, parity_ref: (0, which, i, parity_ref[0], 0, 0),
         )
 
     def gated(parity, rows, *before):
@@ -450,13 +450,13 @@
     per_part = 4
     down_steps = expert_count // (parts * per_part)
     quarter = PAIRS // 2
-    down_weights = down_weights.reshape(2 * expert_count, quarter, 2, local_units, columns)
+    down_weights = down_weights.reshape(expert_count, 2, quarter, 2, local_units, columns)
     turned_type = jax.ShapeDtypeStruct((2, TOP, tokens, quarter * local_units), jnp.bfloat16)
 
     def down_spec(half, part):
         return pl.BlockSpec(
-            (per_part, quarter, 1, local_units, columns),
-            lambda i, parity_ref: ((half * down_steps + i) * parts + part, 0, parity_ref[0], 0, 0),
+            (per_part, 1, quarter, 1, local_units, columns),
+            lambda i, parity_ref: (i * parts + part, half, 0, parity_ref[0], 0, 0),
         )
 
     def lowered(ready, parity, rows, start, dtype):

time: 241 us -> 241 us (level)
  no operation moved by 1% of the time
where the time goes in v13:
time: 241 us; the launch traced here: 240 us
  blocking collectives  81.9 us (34%)
  waiting for transfers between devices  57.6 us (24%)
  starting transfers between devices  50.2 us (21%)
  Pallas kernels  33.2 us (14%)
  between operations  13.7 us (6%)
  local copies, waits for them, and re-layouts  3.56 us (1%)
    all_to_all x2, blocking collectives, exchange(): lax.all_to_all(message, axis, split_axis=0, concat_axis=0, tiled=True, ax...  81.9 us
    all_to_all x2, waiting for transfers between devices, exchange(): lax.all_to_all(message, axis, split_axis=0, concat_axis=0, tiled=True, ax...  42 us
    all_to_all x2, starting transfers between devices, exchange(): lax.all_to_all(message, axis, split_axis=0, concat_axis=0, tiled=True, ax...  19.1 us
    ppermute x1, starting transfers between devices, local(): rows_other = lax.ppermute(rows_own, 'tensor', NEIGHBOUR)  14.5 us
    pallas_call x2, Pallas kernels, gated(): pl.pallas_call(functools.partial(gate_up, last), out_shape=out_type if la...  13.7 us
    all_gather x1, waiting for transfers between devices, local(): down_weights = lax.all_gather(down_half, ('expert', 'dp'), axis=0)  8.98 us
    pallas_call x2, Pallas kernels, lowered(): pl.pallas_call(functools.partial(down, ready, parts), out_shape=jax.Shape...  8.78 us
    ppermute x1, starting transfers between devices, local(): gathered_other = lax.ppermute(gathered, 'dp', SWAP)  8.13 us
  transfers between devices with their start and end apart: 8, of which 5 were waited for; matrix products, arithmetic and copies ran while one was open for 1% of the time, Pallas kernels for 11%

profile of v13, /device:TPU:1, one launch (start us, length us, event | category | flops | bytes accessed | tf_op | source)
XLA Modules:
  0.0 240.3 jit_solution(14177853086150286890)
XLA Ops:
  6.5 0.0 copy-start
  6.5 0.0 copy-start.2
  6.5 0.0 copy-start.3
  6.5 0.0 copy-start.4
  6.5 0.0 all-gather.6.cloned.1.call-start
  6.6 2.2 pack.1
  8.8 0.0 all-gather.6.cloned.1.call-update
  8.8 0.0 all-gather.4.cloned.1.call-start
  8.8 0.0 copy-done
  8.8 0.8 constant_dynamic-slice_fusion
  9.6 0.0 all-gather.4.cloned.1.call-update
  9.7 0.0 copy-done.2
  9.7 0.0 copy-done.3
  9.7 0.0 copy-done.4
  9.7 0.4 compose.1
  10.1 52.3 %all_to_all.20 = bf16[32,384,128]{2,1,0:T(8,128)(2,1)} all-to-all(bf16[32,384,128]{2,1,0:T(8,128)(2,1)S(1)} %compose.1), channel_id=1, replica_groups={{0,1,2,3,4,5,6,7,8,9,10,11,12,13,14,15,16,17,18,19,20,21,22,23,24,25,26..., dimensions={0} | all-to-all | bytes 6291456 | tf_op jit(solution)/shard_map/all_to_all | solution.py:244
  62.5 8.1 %collective-permute-start.1 = (bf16[32,384,128]{2,1,0:T(8,128)(2,1)}, bf16[32,384,128]{2,1,0:T(8,128)(2,1)}, u32[]{:S(2)}, u32[]{:S(2)}) collective-permute-start(bf16[32,384,128]{2,1,0:T(8,128)(2,1)} %all_to_all.20), channel_id=1, source_target_pairs={{0,256},{256,0},{1,257},{257,1},{2,258},{258,2},{3,259},{259,3},{4... | collective-permute-start | bytes 9437192 | tf_op jit(solution)/shard_map/ppermute | solution.py:341
  70.6 3.1 %attend.1.attended_ref = bf16[2,128,256]{2,1,0:T(8,128)(2,1)} custom-call(s32[1]{0:T(128)} %bitcast.2.place_ref, bf16[128,512]{1,0:T(8,128)(2,1)} %query_ref.1, bf16[2,16,384,128]{3,2,1,0:T(8,128)(2,1)} %bitcast.5.piece_ref), custom_call_target="tpu_custom_call" | custom-call | tf_op jit(solution)/shard_map/attend/pallas_call | solution.py:343
  73.7 2.7 %collective-permute-start = (bf16[2,128,256]{2,1,0:T(8,128)(2,1)}, bf16[2,128,256]{2,1,0:T(8,128)(2,1)S(1)}, u32[]{:S(2)}, u32[]{:S(2)}) collective-permute-start(bf16[2,128,256]{2,1,0:T(8,128)(2,1)} %attend.1.attended_ref), channel_id=1, source_target_pairs={{0,16},{16,0},{32,48},{48,32},{64,80},{80,64},{96,112},{112,96},{1... | collective-permute-start | bytes 393224 | tf_op jit(solution)/shard_map/ppermute | solution.py:363
  76.4 0.0 collective-permute-done.1
  76.4 0.0 copy-start.1
  76.4 0.9 copy-done.1
  77.3 2.0 project.2.refs_0_
  79.3 1.6 collective-permute-done.attended_ref
  80.9 2.8 %project.3 = bf16[8,128,256]{2,1,0:T(8,128)(2,1)} custom-call(s32[1]{0:T(128)} %bitcast.1.core_ref, s32[1]{0:T(128)} %bitcast.source_ref.scalar_ref, bf16[2,128,256]{2,1,0:T(8,128)(2,1)S(1)} %collective-permute-done.attended_ref, bf16[2,8,2,384,128]{4,3,2,1,0:T(8,128)(2,1)} %bitcast.6.own_ref, bf16[2,8,2,384,128]{4,3,2,1,0:T(8,128)(2,1)} %bitcast.7.other_ref, ...), custom_call_target="tpu_custom_call" | custom-call | flops 268435456 | bytes 2097152 | tf_op jit(solution)/shard_map/project/pallas_call | solution.py:373
  83.7 0.0 copy-start.6
  83.8 15.2 %all-to-all-start.1 = ((bf16[8,128,256]{2,1,0:T(8,128)(2,1)}), bf16[8,128,256]{2,1,0:T(8,128)(2,1)S(1)}, u32[]{:S(2)}, u32[]{:S(2)}) async-start(bf16[8,128,256]{2,1,0:T(8,128)(2,1)} %project.3), calls=%async_computation.1 | async-start | bytes 1048576 | tf_op jit(solution)/shard_map/all_to_all | solution.py:244
  98.9 0.8 constant_dynamic-slice_fusion.2
  99.7 23.2 %all-to-all-done.1 = bf16[8,128,256]{2,1,0:T(8,128)(2,1)S(1)} async-done(((bf16[8,128,256]{2,1,0:T(8,128)(2,1)}), bf16[8,128,256]{2,1,0:T(8,128)(2,1)S(1)}, u32[]{:S(2)}, u32[]{:S(2)}) %all-to-all-start.1) | async-done | bytes 524320 | tf_op jit(solution)/shard_map/all_to_all | solution.py:244
  122.9 0.1 convert_reduce_fusion
  123.0 29.6 %all_to_all.21.rows_ref = bf16[8,128,256]{2,1,0:T(8,128)(2,1)S(1)} all-to-all(bf16[8,128,256]{2,1,0:T(8,128)(2,1)S(1)} %broadcast_in_dim.4), channel_id=1, replica_groups={{0,32,64,96,128,160,192,224},{16,48,80,112,144,176,208,240},{1,33,65,97..., dimensions={0} | all-to-all | bytes 1048576 | tf_op jit(solution)/shard_map/all_to_all | solution.py:244
  152.6 0.0 all-gather.6.cloned.1.call-done
  152.6 14.5 %collective-permute-start.2 = (bf16[8,128,256]{2,1,0:T(8,128)(2,1)S(1)}, bf16[8,128,256]{2,1,0:T(8,128)(2,1)S(1)}, u32[]{:S(2)}, u32[]{:S(2)}) collective-permute-start(bf16[8,128,256]{2,1,0:T(8,128)(2,1)S(1)} %all_to_all.21.rows_ref), channel_id=1, source_target_pairs={{0,16},{16,0},{32,48},{48,32},{64,80},{80,64},{96,112},{112,96},{1... | collective-permute-start | bytes 1572872 | tf_op jit(solution)/shard_map/ppermute | solution.py:402
  167.2 0.0 copy-done.6
  167.2 0.0 copy-start.5
  167.2 6.7 %gate_up.2 = (f32[2,1536,128]{2,1,0:T(8,128)S(1)}, f32[128,1]{1,0:T(8,128)S(1)}) custom-call(s32[1]{0:T(128)} %bitcast.3.odd_ref.source_ref.scalar_ref, bf16[8,128,256]{2,1,0:T(8,128)(2,1)S(1)} %all_to_all.21.rows_ref, f32[8,2,1,256]{3,2,1,0:T(1,128)S(1)} %bitcast.28, bf16[16,2,8,2,96,256]{5,4,3,2,1,0:T(8,128)(2,1)} %bitcast.39, ...), custom_call_target="tpu_custom_call" | custom-call | flops 1610612736 | bytes 12582912 | tf_op jit(solution)/shard_map/gate_up/pallas_call | solution.py:426
  173.9 5.0 %collective-permute-done.2.rows_ref = bf16[8,128,256]{2,1,0:T(8,128)(2,1)S(1)} collective-permute-done((bf16[8,128,256]{2,1,0:T(8,128)(2,1)S(1)}, bf16[8,128,256]{2,1,0:T(8,128)(2,1)S(1)}, u32[]{:S(2)}, u32[]{:S(2)}) %collective-permute-start.2) | collective-permute-done | bytes 524320 | tf_op jit(solution)/shard_map/ppermute | solution.py:402
  178.9 0.0 copy-done.5
  178.9 0.0 copy-start.7
  178.9 7.1 %gate_up.3 = bf16[192,128]{1,0:T(8,128)(2,1)S(1)} custom-call(s32[1]{0:T(128)} %bitcast.source_ref.scalar_ref, bf16[8,128,256]{2,1,0:T(8,128)(2,1)S(1)} %collective-permute-done.2.rows_ref, f32[8,2,1,256]{3,2,1,0:T(1,128)S(1)} %bitcast.29, bf16[16,2,8,2,96,256]{5,4,3,2,1,0:T(8,128)(2,1)} %bitcast.41, bf16[16,2,8,2,96,256]{5,4,3,2,1,0:T(8,128)(2,1)} %bitcast.42, ...), custom_call_target="tpu_custom_call" | custom-call | flops 1610612736 | bytes 12582912 | tf_op jit(solution)/shard_map/gate_up/pallas_call | solution.py:426
  185.9 0.8 broadcast_in_dim.5
  186.7 3.9 %all-to-all-start.3 = ((bf16[8,192,128]{2,1,0:T(8,128)(2,1)}), bf16[8,192,128]{2,1,0:T(8,128)(2,1)S(1)}, u32[]{:S(2)}, u32[]{:S(2)}) async-start(bf16[8,192,128]{2,1,0:T(8,128)(2,1)} %broadcast_in_dim.5), calls=%async_computation.3 | async-start | bytes 786432 | tf_op jit(solution)/shard_map/all_to_all | solution.py:244
  190.7 0.1 copy.24.routes_ref
  190.8 0.0 copy-done.7
  190.8 0.1 copy.25.route_weight_ref
  190.9 18.8 %all-to-all-done.3.activation_ref = bf16[8,192,128]{2,1,0:T(8,128)(2,1)S(1)} async-done(((bf16[8,192,128]{2,1,0:T(8,128)(2,1)}), bf16[8,192,128]{2,1,0:T(8,128)(2,1)S(1)}, u32[]{:S(2)}, u32[]{:S(2)}) %all-to-all-start.3) | async-done | bytes 393248 | tf_op jit(solution)/shard_map/all_to_all | solution.py:244
  209.7 5.6 %collective-permute-start.3 = (bf16[8,192,128]{2,1,0:T(8,128)(2,1)S(1)}, bf16[8,192,128]{2,1,0:T(8,128)(2,1)S(1)}, u32[]{:S(2)}, u32[]{:S(2)}) collective-permute-start(bf16[8,192,128]{2,1,0:T(8,128)(2,1)S(1)} %all-to-all-done.3.activation_ref), channel_id=1, source_target_pairs={{0,16},{16,0},{32,48},{48,32},{64,80},{80,64},{96,112},{112,96},{1... | collective-permute-start | bytes 1179656 | tf_op jit(solution)/shard_map/ppermute | solution.py:448
  215.5 0.2 turn.1.activation_ref
  215.6 9.0 %all-gather.4.cloned.1.call-done = bf16[32,768,256]{2,1,0:T(8,128)(2,1)} async-done(((bf16[1,768,256]{2,1,0:T(8,128)(2,1)}), bf16[32,768,256]{2,1,0:T(8,128)(2,1)}) %all-gather.4.cloned.1.call-update) | async-done | bytes 12582928 | tf_op jit(solution)/shard_map/all_gather | solution.py:339
  224.6 4.0 %down.2.start_ref = f32[128,256]{1,0:T(8,128)S(1)} custom-call(s32[1]{0:T(128)} %bitcast.3.odd_ref.source_ref.scalar_ref, bf16[2,2,128,384]{3,2,1,0:T(8,128)(2,1)S(1)} %turn.1.activation_ref, s32[128,2]{1,0:T(8,128)S(1)} %copy.24.routes_ref, f32[128,2]{1,0:T(8,128)S(1)} %copy.25.route_weight_ref, f32[128,256]{1,0:T(8,128)S(1)} %maximum_select_fusion.start_ref, ...), custom_call_target="tpu_custom_call" | custom-call | flops 805306368 | bytes 6291456 | tf_op jit(solution)/shard_map/down/pallas_call | solution.py:466
  228.6 0.0 collective-permute-done.3.activation_ref
  228.6 4.8 %down.3 = bf16[128,256]{1,0:T(8,128)(2,1)} custom-call(s32[1]{0:T(128)} %bitcast.source_ref.scalar_ref, bf16[8,192,128]{2,1,0:T(8,128)(2,1)S(1)} %collective-permute-done.3.activation_ref, s32[128,2]{1,0:T(8,128)S(1)} %copy.24.routes_ref, f32[128,2]{1,0:T(8,128)S(1)} %copy.25.route_weight_ref, f32[128,256]{1,0:T(8,128)S(1)} %down.2.start_ref, ...), custom_call_target="tpu_custom_call" | custom-call | flops 805306368 | bytes 6291456 | tf_op jit(solution)/shard_map/down/pallas_call | solution.py:466
  (6 shorter events, 0.1 us)
Async XLA Ops:
  6.5 2.3 copy-start
  6.5 3.1 %copy-start.2 = (bf16[512,256]{1,0:T(8,128)(2,1)S(1)}, bf16[512,256]{1,0:T(8,128)(2,1)}, u32[]{:S(2)}) copy-start(bf16[512,256]{1,0:T(8,128)(2,1)} %weight_ref.1) | copy-start | bytes 786436
  6.5 3.1 %copy-start.3 = (bf16[128,512]{1,0:T(8,128)(2,1)S(1)}, bf16[128,512]{1,0:T(8,128)(2,1)}, u32[]{:S(2)}) copy-start(bf16[128,512]{1,0:T(8,128)(2,1)} %key_ref.1) | copy-start | bytes 393220
  6.5 3.1 %copy-start.4 = (bf16[128,512]{1,0:T(8,128)(2,1)S(1)}, bf16[128,512]{1,0:T(8,128)(2,1)}, u32[]{:S(2)}) copy-start(bf16[128,512]{1,0:T(8,128)(2,1)} %value_ref.1) | copy-start | bytes 393220
  6.5 146.1 %all-gather.6.cloned.1.call-start = ((), (), s32[]{:S(2)}) async-start(), calls=%async_computation.5 | async-start | bytes 25952256 | tf_op jit(solution)/shard_map/all_gather | solution.py:338
  8.8 215.8 %all-gather.4.cloned.1.call-start = ((), (), s32[]{:S(2)}) async-start(), calls=%async_computation.4 | async-start | bytes 12976128 | tf_op jit(solution)/shard_map/all_gather | solution.py:339
  62.5 13.9 %collective-permute-start.1 = (bf16[32,384,128]{2,1,0:T(8,128)(2,1)}, bf16[32,384,128]{2,1,0:T(8,128)(2,1)}, u32[]{:S(2)}, u32[]{:S(2)}) collective-permute-start(bf16[32,384,128]{2,1,0:T(8,128)(2,1)} %all_to_all.20), channel_id=1, source_target_pairs={{0,256},{256,0},{1,257},{257,1},{2,258},{258,2},{3,259},{259,3},{4... | collective-permute-start | bytes 9437192 | tf_op jit(solution)/shard_map/ppermute | solution.py:341
  73.7 7.2 %collective-permute-start = (bf16[2,128,256]{2,1,0:T(8,128)(2,1)}, bf16[2,128,256]{2,1,0:T(8,128)(2,1)S(1)}, u32[]{:S(2)}, u32[]{:S(2)}) collective-permute-start(bf16[2,128,256]{2,1,0:T(8,128)(2,1)} %attend.1.attended_ref), channel_id=1, source_target_pairs={{0,16},{16,0},{32,48},{48,32},{64,80},{80,64},{96,112},{112,96},{1... | collective-permute-start | bytes 393224 | tf_op jit(solution)/shard_map/ppermute | solution.py:363
  76.4 0.9 copy-start.1
  83.7 83.4 %copy-start.6 = (f32[4096]{0:T(1024)S(1)}, f32[4096]{0:T(1024)}, u32[]{:S(2)}) copy-start(f32[4096]{0:T(1024)} %param.16) | copy-start | bytes 49156
  83.8 39.1 %all-to-all-start.1 = ((bf16[8,128,256]{2,1,0:T(8,128)(2,1)}), bf16[8,128,256]{2,1,0:T(8,128)(2,1)S(1)}, u32[]{:S(2)}, u32[]{:S(2)}) async-start(bf16[8,128,256]{2,1,0:T(8,128)(2,1)} %project.3), calls=%async_computation.1 | async-start | bytes 1048576 | tf_op jit(solution)/shard_map/all_to_all | solution.py:244
  152.6 26.3 %collective-permute-start.2 = (bf16[8,128,256]{2,1,0:T(8,128)(2,1)S(1)}, bf16[8,128,256]{2,1,0:T(8,128)(2,1)S(1)}, u32[]{:S(2)}, u32[]{:S(2)}) collective-permute-start(bf16[8,128,256]{2,1,0:T(8,128)(2,1)S(1)} %all_to_all.21.rows_ref), channel_id=1, source_target_pairs={{0,16},{16,0},{32,48},{48,32},{64,80},{80,64},{96,112},{112,96},{1... | collective-permute-start | bytes 1572872 | tf_op jit(solution)/shard_map/ppermute | solution.py:402
  167.2 11.7 %copy-start.5 = (s32[128,2]{0,1:T(2,128)S(1)}, s32[128,2]{0,1:T(2,128)}, u32[]{:S(2)}) copy-start(s32[128,2]{0,1:T(2,128)} %param.17) | copy-start | bytes 3076
  178.9 11.9 %copy-start.7 = (f32[128,2]{0,1:T(2,128)S(1)}, f32[128,2]{0,1:T(2,128)}, u32[]{:S(2)}) copy-start(f32[128,2]{0,1:T(2,128)} %param.18) | copy-start | bytes 3076
  186.7 23.0 %all-to-all-start.3 = ((bf16[8,192,128]{2,1,0:T(8,128)(2,1)}), bf16[8,192,128]{2,1,0:T(8,128)(2,1)S(1)}, u32[]{:S(2)}, u32[]{:S(2)}) async-start(bf16[8,192,128]{2,1,0:T(8,128)(2,1)} %broadcast_in_dim.5), calls=%async_computation.3 | async-start | bytes 786432 | tf_op jit(solution)/shard_map/all_to_all | solution.py:244
  209.7 18.9 %collective-permute-start.3 = (bf16[8,192,128]{2,1,0:T(8,128)(2,1)S(1)}, bf16[8,192,128]{2,1,0:T(8,128)(2,1)S(1)}, u32[]{:S(2)}, u32[]{:S(2)}) collective-permute-start(bf16[8,192,128]{2,1,0:T(8,128)(2,1)S(1)} %all-to-all-done.3.activation_ref), channel_id=1, source_target_pairs={{0,16},{16,0},{32,48},{48,32},{64,80},{80,64},{96,112},{112,96},{1... | collective-permute-start | bytes 1179656 | tf_op jit(solution)/shard_map/ppermute | solution.py:448
Sparse Core Ops, SparseCore 0:
  10.5 133.1 all-gather.5
  146.9 77.7 all-gather.3
